TPU v7x, 32 devices: a whole 2x2x4 slice. The times are simulated.
32 devices in a mesh: nodes: 8 (over z, y), heads: 4 (over x, core).
Axes of the slice: x: 2, y: 2, z: 4, core: 2. Of those that a mesh axis runs over, the one named last changes fastest.
Arguments:
- node_state: bfloat16 [2, 4096, 512], P(None, 'nodes', 'heads'), may hold values from -6 to 6
- noise_embed: float32 [2, 256], replicated, may hold values from -5 to 5
- out_grad: bfloat16 [2, 4096, 512], P(None, 'nodes', 'heads'), may hold values from -6 to 6
- neighbours: int32 [2, 4096, 16], P(None, 'nodes'), may hold values from 0 to 4095, as said below
- patch_sizes: int32 [2, 8], P(None, 'nodes'), may hold values from 256 to 512, as said below
- w_project: float32 [512, 1536], P('nodes', 'heads'), may hold values from -0.25 to 0.25
- w_output: float32 [512, 512], P('heads', 'nodes'), may hold values from -0.75 to 0.75
- w_expand: float32 [512, 2048], P('nodes', 'heads'), may hold values from -0.25 to 0.25
- w_contract: float32 [2048, 512], P('heads', 'nodes'), may hold values from -0.125 to 0.125
- momentum_project: float32 [512, 1536], P('nodes', 'heads'), may hold values from -96 to 96
- momentum_output: float32 [512, 512], P('heads', 'nodes'), may hold values from -160 to 160
- momentum_expand: float32 [512, 2048], P('nodes', 'heads'), may hold values from -160 to 160
- momentum_contract: float32 [2048, 512], P('heads', 'nodes'), may hold values from -256 to 256
- w_modulate: float32 [4, 256, 512], P(None, None, 'heads'), may hold values from -0.1875 to 0.1875
- b_modulate: float32 [4, 512], P(None, 'heads'), may hold values from -0.6 to 0.6
- first_modulate: float32 [4, 256, 512], P(None, None, 'heads'), may hold values from -28 to 28
- second_modulate: float32 [4, 256, 512], P(None, None, 'heads'), may hold values from 1.536 to 6.144
- first_bias: float32 [4, 512], P(None, 'heads'), may hold values from -28 to 28
- second_bias: float32 [4, 512], P(None, 'heads'), may hold values from 1.536 to 6.144
Outputs:
- layer_output: bfloat16 [2, 4096, 512], P(None, 'nodes', 'heads')
- input_grad: float32 [2, 4096, 512], P(None, 'nodes', 'heads')
- new_momentum_project: float32 [512, 1536], P('nodes', 'heads')
- new_momentum_output: float32 [512, 512], P('heads', 'nodes')
- new_momentum_expand: float32 [512, 2048], P('nodes', 'heads')
- new_momentum_contract: float32 [2048, 512], P('heads', 'nodes')
- new_project: float32 [512, 1536], P('nodes', 'heads')
- new_output: float32 [512, 512], P('heads', 'nodes')
- new_expand: float32 [512, 2048], P('nodes', 'heads')
- new_contract: float32 [2048, 512], P('heads', 'nodes')
- new_first_modulate: float32 [4, 256, 512], P(None, None, 'heads')
- new_second_modulate: float32 [4, 256, 512], P(None, None, 'heads')
- new_modulate: float32 [4, 256, 512], P(None, None, 'heads')
- new_first_bias: float32 [4, 512], P(None, 'heads')
- new_second_bias: float32 [4, 512], P(None, 'heads')
- new_bias: float32 [4, 512], P(None, 'heads')
Inputs may be any that keep to these rules, and one draw needn't show every extreme that they name: `neighbours`: each entry is patch times 512 plus slot of a live node in the same patch or in one of the two patches beside it, patches taken cyclically. `patch_sizes`: in each micro-batch the last patch holds exactly 512 live nodes and another exactly half of 512; live nodes fill the lowest slots of a patch.
All inputs are finite; a program needn't handle non-finite values.
Results may differ from a plain program's by a relative error of at most 0.007.
The roundings to bfloat16 on the way count: a program that leaves them out, or rounds other values in their place, can miss the bound.
Values may be sent and summed in bfloat16 or wider, within the bound.
A program may use at most 128 MiB of HBM per device.

v0:
```python
import jax
import jax.numpy as jnp
from jax import lax
from jax.sharding import PartitionSpec as P

NS_STEPS = 5
STEP = 10


EPS_NORM = 1e-06
NEWTON_A = 3.4445
NEWTON_B = -4.775
NEWTON_C = 2.0315
MOMENTUM_DECAY = 0.5
LR_MUON = 1.0
LR_ADAM = 0.04
DECAY_WEIGHT = 0.01
BETA_FIRST = 0.9
BETA_SECOND = 0.999
EPS_ADAM = 1e-08
HIGH = lax.Precision.HIGHEST


def padded(array, sides, width):
    for axis, dim in sides:
        size, length = (lax.axis_size(axis), array.shape[dim])
        up = [(i, (i + 1) % size) for i in range(size)]
        down = [(j, i) for i, j in up]
        last = lax.slice_in_dim(array, length - width, length, axis=dim)
        first = lax.slice_in_dim(array, 0, width, axis=dim)
        before = lax.ppermute(last, axis, up)
        after = lax.ppermute(first, axis, down)
        array = jnp.concatenate([before, array, after], axis=dim)
    return array


def norm_sums(first_terms, second_terms):
    return lax.psum((first_terms, second_terms), "heads")


def norm_forward(values, full_width):
    sum_terms, sum_squares = norm_sums(jnp.sum(values, axis=-1), jnp.sum(values * values, axis=-1))
    row_mean = sum_terms / full_width
    inv_root = lax.rsqrt(sum_squares / full_width - row_mean * row_mean + EPS_NORM)
    return ((values - row_mean[:, None]) * inv_root[:, None], inv_root)


def norm_backward(grad_norm, normed, inv_root, full_width):
    sum_terms, sum_cross = norm_sums(
        jnp.sum(grad_norm, axis=-1), jnp.sum(grad_norm * normed, axis=-1)
    )
    return inv_root[:, None] * (
        grad_norm - sum_terms[:, None] / full_width - normed * sum_cross[:, None] / full_width
    )


def full_rows(piece):
    return lax.all_gather(piece, "heads", axis=1, tiled=True)


def head_sum(partial_rows):
    return lax.psum_scatter(partial_rows, "heads", scatter_dimension=1, tiled=True)


def orthogonal(matrix):
    is_tall = matrix.shape[0] > matrix.shape[1]
    iterate = matrix.T if is_tall else matrix
    iterate = iterate / (jnp.sqrt(jnp.sum(iterate * iterate)) + 1e-07)
    for repeat in range(NS_STEPS):
        square = jnp.dot(iterate, iterate.T, precision=HIGH)
        polynomial = NEWTON_B * square + NEWTON_C * jnp.dot(square, square, precision=HIGH)
        iterate = NEWTON_A * iterate + jnp.dot(polynomial, iterate, precision=HIGH)
    return iterate.T if is_tall else iterate


def assemble(stacked, rows_first, patch_count, head_count):
    block_rows, block_cols = (stacked.shape[1], stacked.shape[2])
    blocks = stacked.reshape(patch_count, head_count, block_rows, block_cols)
    if rows_first:
        return blocks.transpose(0, 2, 1, 3).reshape(
            patch_count * block_rows, head_count * block_cols
        )
    return blocks.transpose(1, 2, 0, 3).reshape(head_count * block_rows, patch_count * block_cols)


def own_block(whole_matrix, rows_first, block_rows, block_cols, patch_index, head_index):
    if rows_first:
        return lax.dynamic_slice(
            whole_matrix,
            (patch_index * block_rows, head_index * block_cols),
            (block_rows, block_cols),
        )
    return lax.dynamic_slice(
        whole_matrix, (head_index * block_rows, patch_index * block_cols), (block_rows, block_cols)
    )


def adam_step(weight, first_old, second_old, gradient):
    first_new = BETA_FIRST * first_old + (1.0 - BETA_FIRST) * gradient
    second_new = BETA_SECOND * second_old + (1.0 - BETA_SECOND) * gradient * gradient
    first_hat = first_new / (1.0 - BETA_FIRST**STEP)
    second_hat = second_new / (1.0 - BETA_SECOND**STEP)
    updated = weight * (1.0 - LR_ADAM * DECAY_WEIGHT) - LR_ADAM * first_hat / (
        jnp.sqrt(second_hat) + EPS_ADAM
    )
    return (first_new, second_new, updated)


def per_device(
    node_state,
    noise_embed,
    out_grad,
    neighbours,
    patch_sizes,
    w_project,
    w_output,
    w_expand,
    w_contract,
    momentum_project,
    momentum_output,
    momentum_expand,
    momentum_contract,
    w_modulate,
    b_modulate,
    first_modulate,
    second_modulate,
    first_bias,
    second_bias,
):
    micro_count, capacity, feature_share = node_state.shape
    head_count = lax.axis_size("heads")
    patch_count = lax.axis_size("nodes")
    full_width = feature_share * head_count
    head_dim = w_output.shape[0]
    total_rows = capacity * patch_count
    patch_index = lax.axis_index("nodes")
    head_index = lax.axis_index("heads")
    inv_head = head_dim ** (-0.5)
    f32 = jnp.float32
    bf16 = jnp.bfloat16
    low_project = w_project.astype(bf16)
    low_output = w_output.astype(bf16)
    low_expand = w_expand.astype(bf16)
    low_contract = w_contract.astype(bf16)

    def fetch():
        return (
            lax.all_gather(low_project, "nodes", axis=0, tiled=True),
            lax.all_gather(low_output, "nodes", axis=1, tiled=True),
            lax.all_gather(low_expand, "nodes", axis=0, tiled=True),
            lax.all_gather(low_contract, "nodes", axis=1, tiled=True),
        )

    hidden_units = w_expand.shape[1]
    grad_project = jnp.zeros((full_width, 3 * head_dim), f32)
    grad_output = jnp.zeros((head_dim, full_width), f32)
    grad_expand = jnp.zeros((full_width, hidden_units), f32)
    grad_contract = jnp.zeros((hidden_units, full_width), f32)
    mod_terms = []
    outputs = []
    input_grads = []
    slot_ids = lax.broadcasted_iota(jnp.int32, (capacity,), 0)
    for batch in range(micro_count):
        forward_set = fetch()
        gather_project, gather_output, gather_expand, gather_contract = forward_set
        live_rows = (slot_ids < patch_sizes[batch, 0]).astype(f32)[:, None]
        state_rows = node_state[batch].astype(f32)
        modulation = (
            jnp.einsum("c,jcd->jd", noise_embed[batch], w_modulate, precision=HIGH) + b_modulate
        )
        norm_one, root_one = norm_forward(state_rows, full_width)
        a_one = full_rows((norm_one * (1.0 + modulation[1]) + modulation[0]).astype(bf16))
        projected = jnp.dot(a_one, gather_project, preferred_element_type=f32).astype(bf16)
        queries = projected[:, :head_dim]
        key_value = projected[:, head_dim:]
        key_value_ext = padded(key_value, (("nodes", 0),), capacity)
        local_index = jnp.mod(neighbours[batch] - (patch_index - 1) * capacity, total_rows)
        gathered_rows = jnp.take(key_value_ext, local_index, axis=0)
        key_rows = gathered_rows[:, :, :head_dim]
        value_rows = gathered_rows[:, :, head_dim:]
        scores = jnp.einsum("rd,rkd->rk", queries, key_rows, preferred_element_type=f32) * inv_head
        row_max = jnp.max(scores, axis=-1, keepdims=True)
        exp_terms = jnp.exp(scores - row_max)
        sum_exp = jnp.sum(exp_terms, axis=-1, keepdims=True)
        log_total = row_max + jnp.log(sum_exp)
        prob_low = (exp_terms / sum_exp).astype(bf16)
        mixed = jnp.einsum("rk,rkd->rd", prob_low, value_rows, preferred_element_type=f32).astype(
            bf16
        )
        hidden_one = state_rows + head_sum(
            jnp.dot(mixed, gather_output, preferred_element_type=f32)
        )
        norm_two, root_two = norm_forward(hidden_one, full_width)
        a_two = full_rows((norm_two * (1.0 + modulation[3]) + modulation[2]).astype(bf16))
        up_rows = jnp.dot(a_two, gather_expand, preferred_element_type=f32)
        gate_rows = jax.nn.sigmoid(up_rows)
        act = (up_rows * gate_rows).astype(bf16)
        result = hidden_one + head_sum(jnp.dot(act, gather_contract, preferred_element_type=f32))
        outputs.append((result * live_rows).astype(bf16))
        back_project, back_output, back_expand, back_contract = fetch()
        cot_rows = out_grad[batch].astype(f32) * live_rows
        cot_full = full_rows(cot_rows.astype(bf16))
        grad_act = jnp.einsum("rd,fd->rf", cot_full, back_contract, preferred_element_type=f32)
        grad_contract = grad_contract + jnp.einsum(
            "rf,rd->fd", act, cot_full, preferred_element_type=f32
        )
        grad_up = (grad_act * gate_rows * (1.0 + up_rows * (1.0 - gate_rows))).astype(bf16)
        grad_expand = grad_expand + jnp.einsum(
            "rc,rf->cf", a_two, grad_up, preferred_element_type=f32
        )
        grad_two = head_sum(
            jnp.einsum("rf,cf->rc", grad_up, back_expand, preferred_element_type=f32)
        )
        grad_hidden = cot_rows + norm_backward(
            grad_two * (1.0 + modulation[3]), norm_two, root_two, full_width
        )
        grad_attn = full_rows(grad_hidden.astype(bf16))
        grad_mixed = jnp.einsum("rd,hd->rh", grad_attn, back_output, preferred_element_type=f32)
        grad_output = grad_output + jnp.einsum(
            "rh,rd->hd", mixed, grad_attn, preferred_element_type=f32
        )
        again_scores = (
            jnp.einsum("rd,rkd->rk", queries, key_rows, preferred_element_type=f32) * inv_head
        )
        prob = jnp.exp(again_scores - log_total)
        grad_prob = jnp.einsum("rd,rkd->rk", grad_mixed, value_rows.astype(f32), precision=HIGH)
        grad_score = prob * (grad_prob - jnp.sum(prob * grad_prob, axis=-1, keepdims=True))
        grad_query = (
            jnp.einsum("rk,rkd->rd", grad_score, key_rows.astype(f32), precision=HIGH) * inv_head
        )
        grad_keys = grad_score[:, :, None] * queries.astype(f32)[:, None, :] * inv_head
        grad_values = prob_low.astype(f32)[:, :, None] * grad_mixed[:, None, :]
        grad_ext = (
            jnp.zeros((3 * capacity, 2 * head_dim), f32)
            .at[local_index]
            .add(jnp.concatenate([grad_keys, grad_values], axis=-1))
        )
        outgoing = jnp.concatenate([grad_ext[:capacity], grad_ext[2 * capacity :]], axis=0)
        returned = padded(outgoing, (("nodes", 0),), capacity)
        grad_key_value = (
            grad_ext[capacity : 2 * capacity] + returned[:capacity] + returned[3 * capacity :]
        )
        grad_projected = jnp.concatenate([grad_query, grad_key_value], axis=-1).astype(bf16)
        grad_project = grad_project + jnp.einsum(
            "rc,rp->cp", a_one, grad_projected, preferred_element_type=f32
        )
        grad_one = head_sum(
            jnp.einsum("rp,cp->rc", grad_projected, back_project, preferred_element_type=f32)
        )
        input_grads.append(
            grad_hidden
            + norm_backward(grad_one * (1.0 + modulation[1]), norm_one, root_one, full_width)
        )
        mod_terms.append(
            jnp.stack(
                [
                    jnp.sum(grad_one, axis=0),
                    jnp.sum(grad_one * norm_one, axis=0),
                    jnp.sum(grad_two, axis=0),
                    jnp.sum(grad_two * norm_two, axis=0),
                ]
            )
        )
    mod_summed = lax.psum(jnp.stack(mod_terms), "nodes")
    grad_modulate = jnp.einsum("bc,bjd->jcd", noise_embed, mod_summed, precision=HIGH)
    grad_bias = jnp.sum(mod_summed, axis=0)
    summed = (
        lax.psum_scatter(grad_project, "nodes", scatter_dimension=0, tiled=True),
        lax.psum_scatter(grad_output, "nodes", scatter_dimension=1, tiled=True),
        lax.psum_scatter(grad_expand, "nodes", scatter_dimension=0, tiled=True),
        lax.psum_scatter(grad_contract, "nodes", scatter_dimension=1, tiled=True),
    )
    olds = (momentum_project, momentum_output, momentum_expand, momentum_contract)
    weights_old = (w_project, w_output, w_expand, w_contract)
    layouts = (True, False, True, False)
    moments = tuple(
        (MOMENTUM_DECAY * moment_old + grad_sum for moment_old, grad_sum in zip(olds, summed))
    )
    stacked = (
        lax.all_gather(moments[0][None], ("nodes", "heads"), axis=0, tiled=True),
        lax.all_gather(moments[1][None], ("nodes", "heads"), axis=0, tiled=True),
        lax.all_gather(moments[2][None], ("nodes", "heads"), axis=0, tiled=True),
        lax.all_gather(moments[3][None], ("nodes", "heads"), axis=0, tiled=True),
    )
    wholes = [
        assemble(piece, rows_first, patch_count, head_count)
        for piece, rows_first in zip(stacked, layouts)
    ]
    new_weights = []
    for number in range(4):
        whole_matrix = wholes[number]
        rows_first = layouts[number]
        factor = max(1.0, whole_matrix.shape[0] / whole_matrix.shape[1]) ** 0.5
        shard_rows, shard_cols = olds[number].shape
        ortho_shard = own_block(
            orthogonal(whole_matrix), rows_first, shard_rows, shard_cols, patch_index, head_index
        )
        new_weights.append(
            weights_old[number] * (1.0 - LR_MUON * DECAY_WEIGHT) - LR_MUON * factor * ortho_shard
        )
    first_mod, second_mod, new_mod = adam_step(
        w_modulate, first_modulate, second_modulate, grad_modulate
    )
    first_b, second_b, new_b = adam_step(b_modulate, first_bias, second_bias, grad_bias)
    return (
        jnp.stack(outputs),
        jnp.stack(input_grads),
        moments[0],
        moments[1],
        moments[2],
        moments[3],
        new_weights[0],
        new_weights[1],
        new_weights[2],
        new_weights[3],
        first_mod,
        second_mod,
        new_mod,
        first_b,
        second_b,
        new_b,
    )


def solution(mesh):
    in_specs = (
        P(None, "nodes", "heads"),
        P(),
        P(None, "nodes", "heads"),
        P(None, "nodes", None),
        P(None, "nodes"),
        P("nodes", "heads"),
        P("heads", "nodes"),
        P("nodes", "heads"),
        P("heads", "nodes"),
        P("nodes", "heads"),
        P("heads", "nodes"),
        P("nodes", "heads"),
        P("heads", "nodes"),
        P(None, None, "heads"),
        P(None, "heads"),
        P(None, None, "heads"),
        P(None, None, "heads"),
        P(None, "heads"),
        P(None, "heads"),
    )
    out_specs = (
        P(None, "nodes", "heads"),
        P(None, "nodes", "heads"),
        P("nodes", "heads"),
        P("heads", "nodes"),
        P("nodes", "heads"),
        P("heads", "nodes"),
        P("nodes", "heads"),
        P("heads", "nodes"),
        P("nodes", "heads"),
        P("heads", "nodes"),
        P(None, None, "heads"),
        P(None, None, "heads"),
        P(None, None, "heads"),
        P(None, "heads"),
        P(None, "heads"),
        P(None, "heads"),
    )
    return jax.shard_map(
        per_device, mesh=mesh, in_specs=in_specs, out_specs=out_specs, check_vma=False
    )
```

profile of v0, /device:TPU:0, one launch (start us, length us, event | category | flops | bytes accessed | tf_op | source)
XLA Modules:
  0.0 1337.8 jit_solution(941210835163310172)
XLA Ops:
  14.4 32.7 %all_gather.61 = bf16[512,384]{1,0:T(8,128)(2,1)S(1)} all-gather(bf16[64,384]{1,0:T(8,128)(2,1)S(1)} %convert_element_type.131), channel_id=1, replica_groups=mesh['nodes'=8,'heads'=4] {'nodes'}, dimensions={0}, use_global_device_ids=true | all-gather | bytes 442368 | tf_op jit(solution)/shard_map/all_gather | solution.py:148
  47.2 5.6 all-reduce.6
  53.9 7.4 all_gather.60
  68.0 33.7 %all_gather.62 = bf16[128,512]{0,1:T(8,128)(2,1)S(1)} all-gather(bf16[128,64]{0,1:T(8,128)(2,1)S(1)} %convert_element_type.135), channel_id=1, replica_groups=mesh['nodes'=8,'heads'=4] {'nodes'}, dimensions={1}, use_global_device_ids=true | all-gather | bytes 147456 | tf_op jit(solution)/shard_map/all_gather | solution.py:149
  102.0 32.9 %gather_fusion = bf16[8192,256]{1,0:T(8,128)(2,1)} fusion(bf16[1536,256]{1,0:T(8,128)(2,1)S(1)} %pad_maximum_fusion.2, s32[8192]{0:T(1024)S(1)} %broadcast_clamp_fusion.1), kind=kCustom, calls=%fused_computation.clone | custom fusion | bytes 8421376 | tf_op jit(solution)/shard_map/jit(_take)/gather | solution.py:178
  148.1 6.6 all_gather.68
  154.8 31.4 %all_gather.65 = bf16[512,512]{0,1:T(8,128)(2,1)S(1)} all-gather(bf16[512,64]{0,1:T(8,128)(2,1)S(1)} %convert_element_type.139), channel_id=1, replica_groups=mesh['nodes'=8,'heads'=4] {'nodes'}, dimensions={1}, use_global_device_ids=true | all-gather | bytes 589824 | tf_op jit(solution)/shard_map/all_gather | solution.py:151
  186.1 31.2 %all_gather.64 = bf16[512,512]{1,0:T(8,128)(2,1)S(1)} all-gather(bf16[64,512]{1,0:T(8,128)(2,1)S(1)} %convert_element_type.137), channel_id=1, replica_groups=mesh['nodes'=8,'heads'=4] {'nodes'}, dimensions={0}, use_global_device_ids=true | all-gather | bytes 589824 | tf_op jit(solution)/shard_map/all_gather | solution.py:150
  218.6 5.7 all-reduce.5
  224.5 6.9 all_gather.63
  239.6 21.3 %reduce-scatter.21.cloned.1.call-done = f32[512,128]{1,0:T(8,128)} async-done(((f32[512,512]{1,0:T(8,128)}), f32[512,128]{1,0:T(8,128)}) %reduce-scatter.21.cloned.1.call-update) | async-done | bytes 262160 | tf_op jit(solution)/shard_map/reduce_scatter | solution.py:62
  262.8 5.7 all-reduce.4
  268.5 19.8 %reduce-scatter.15.cloned.1.call-done = f32[512,128]{1,0:T(8,128)} async-done(((f32[512,512]{1,0:T(8,128)}), f32[512,128]{1,0:T(8,128)}) %reduce-scatter.15.cloned.1.call-update) | async-done | bytes 262160 | tf_op jit(solution)/shard_map/reduce_scatter | solution.py:62
  290.7 7.0 all_gather.69
  311.3 45.0 %scatter_custom_fusion = f32[1536,256]{1,0:T(8,128)S(1)} fusion(s32[8192]{0:T(1024)} %reshape.276, f32[8192,256]{1,0:T(8,128)} %bitcast.460, f32[]{:T(128)} %constant.47.clone.1), kind=kCustom, calls=%fused_computation.119 | custom fusion | flops 2097152 | bytes 1573376 | tf_op jit(solution)/shard_map/scatter-add | solution.py:236
  364.6 16.2 %collective-permute-done.4 = f32[512,256]{1,0:T(8,128)S(1)} collective-permute-done((f32[512,256]{1,0:T(8,128)S(1)}, f32[512,256]{1,0:T(8,128)S(1)}, u32[]{:S(2)}, u32[]{:S(2)}) %collective-permute-start.4) | collective-permute-done | bytes 524320 | tf_op jit(solution)/shard_map/ppermute | solution.py:31
  385.7 23.8 %reduce-scatter.23.cloned.1.call-done = f32[512,128]{1,0:T(8,128)} async-done(((f32[512,512]{1,0:T(8,128)}), f32[512,128]{1,0:T(8,128)}) %reduce-scatter.23.cloned.1.call-update) | async-done | bytes 262160 | tf_op jit(solution)/shard_map/reduce_scatter | solution.py:62
  411.5 5.7 all-reduce.3
  417.4 7.3 all_gather.66
  442.0 32.9 %gather_fusion.1 = bf16[8192,256]{1,0:T(8,128)(2,1)} fusion(bf16[1536,256]{1,0:T(8,128)(2,1)S(1)} %pad_maximum_fusion.3, s32[8192]{0:T(1024)S(1)} %broadcast_clamp_fusion), kind=kCustom, calls=%fused_computation.1.clone | custom fusion | bytes 8421376 | tf_op jit(solution)/shard_map/jit(_take)/gather | solution.py:178
  486.7 7.0 all_gather.70
  493.7 17.5 %reduce-scatter.17.cloned.1.call-done = f32[512,128]{1,0:T(8,128)} async-done(((f32[512,512]{1,0:T(8,128)}), f32[512,128]{1,0:T(8,128)}) %reduce-scatter.17.cloned.1.call-update) | async-done | bytes 262160 | tf_op jit(solution)/shard_map/reduce_scatter | solution.py:62
  512.4 5.8 all-reduce.2
  518.4 7.3 all_gather.67
  534.7 21.2 %reduce-scatter.25.cloned.1.call-done = f32[512,128]{1,0:T(8,128)} async-done(((f32[512,512]{1,0:T(8,128)}), f32[512,128]{1,0:T(8,128)}) %reduce-scatter.25.cloned.1.call-update) | async-done | bytes 262160 | tf_op jit(solution)/shard_map/reduce_scatter | solution.py:62
  557.8 5.7 all-reduce.1
  563.5 19.8 %reduce-scatter.19.cloned.1.call-done = f32[512,128]{1,0:T(8,128)} async-done(((f32[512,512]{1,0:T(8,128)}), f32[512,128]{1,0:T(8,128)}) %reduce-scatter.19.cloned.1.call-update) | async-done | bytes 262160 | tf_op jit(solution)/shard_map/reduce_scatter | solution.py:62
  585.5 6.9 all_gather.71
  618.1 45.0 %scatter_custom_fusion.1 = f32[1536,256]{1,0:T(8,128)S(1)} fusion(s32[8192]{0:T(1024)} %reshape.284, f32[8192,256]{1,0:T(8,128)} %bitcast.461, f32[]{:T(128)} %constant.47.clone.1), kind=kCustom, calls=%fused_computation.117 | custom fusion | flops 2097152 | bytes 1573376 | tf_op jit(solution)/shard_map/scatter-add | solution.py:236
  671.4 19.1 %collective-permute-done.6 = f32[512,256]{1,0:T(8,128)S(1)} collective-permute-done((f32[512,256]{1,0:T(8,128)S(1)}, f32[512,256]{1,0:T(8,128)S(1)}, u32[]{:S(2)}, u32[]{:S(2)}) %collective-permute-start.6) | collective-permute-done | bytes 524320 | tf_op jit(solution)/shard_map/ppermute | solution.py:31
  699.1 33.6 %reduce-scatter.33.cloned.1.call-done = f32[64,512]{1,0:T(8,128)} async-done(((f32[512,512]{1,0:T(8,128)}), f32[64,512]{1,0:T(8,128)}) %reduce-scatter.33.cloned.1.call-update) | async-done | bytes 131088 | tf_op jit(solution)/shard_map/reduce_scatter | solution.py:270
  734.3 64.2 %reduce-scatter.35.cloned.1.call-done = f32[512,64]{0,1:T(8,128)} async-done(((f32[512,512]{0,1:T(8,128)}), f32[512,64]{0,1:T(8,128)}) %reduce-scatter.35.cloned.1.call-update) | async-done | bytes 131088 | tf_op jit(solution)/shard_map/reduce_scatter | solution.py:271
  804.1 59.6 %reduce-scatter.29.cloned.1.call-done = f32[64,384]{1,0:T(8,128)} async-done(((f32[512,384]{1,0:T(8,128)}), f32[64,384]{1,0:T(8,128)}) %reduce-scatter.29.cloned.1.call-update) | async-done | bytes 98320 | tf_op jit(solution)/shard_map/reduce_scatter | solution.py:268
  865.3 53.2 %all-gather.11.cloned.1.call-done = f32[4096,64]{0,1:T(8,128)} async-done(((f32[128,64]{0,1:T(8,128)}), f32[4096,64]{0,1:T(8,128)}) %all-gather.11.cloned.1.call-update) | async-done | bytes 1048592 | tf_op jit(solution)/shard_map/all_gather | solution.py:281
  954.5 19.8 %psum.135 = f32[2,4,128]{2,0,1:T(2,128)S(1)} all-reduce(f32[2,4,128]{2,0,1:T(2,128)S(1)} %pad_maximum_fusion.12), channel_id=1, replica_groups=mesh['nodes'=8,'heads'=4] {'nodes'}, use_global_device_ids=true, to_apply=%region_64.66 | all-reduce | flops 1024 | bytes 8192 | tf_op jit(solution)/shard_map/psum | solution.py:264
  978.3 6.3 all-reduce
  989.8 22.2 %all-gather.13.cloned.1.call-done = f32[2048,512]{1,0:T(8,128)} async-done(((f32[64,512]{1,0:T(8,128)}), f32[2048,512]{1,0:T(8,128)}) %all-gather.13.cloned.1.call-update) | async-done | bytes 4194320 | tf_op jit(solution)/shard_map/all_gather | solution.py:282
  1025.8 50.2 %all-gather.15.cloned.1.call-done = f32[16384,64]{0,1:T(8,128)} async-done(((f32[512,64]{0,1:T(8,128)}), f32[16384,64]{0,1:T(8,128)}) %all-gather.15.cloned.1.call-update) | async-done | bytes 4194320 | tf_op jit(solution)/shard_map/all_gather | solution.py:283
  1085.0 6.4 div.204
  1096.5 6.9 fusion.180
  1103.4 7.1 fusion.174
  1112.4 7.2 multiply_add_fusion.6
  1119.6 6.9 fusion.175
  1128.4 7.4 multiply_add_fusion.5
  1135.7 6.9 fusion.176
  1144.7 6.9 multiply_add_fusion.4
  1151.7 7.1 fusion.177
  1160.7 6.9 multiply_add_fusion.3
  1167.6 7.3 fusion.178
  1176.9 7.0 fusion.179
  1186.5 6.9 bitcast_add_fusion
  1193.5 7.1 fusion.181
  1202.5 7.3 multiply_add_fusion.2
  1209.8 6.9 fusion.182
  1218.7 7.1 multiply_add_fusion.1
  1225.8 7.1 fusion.183
  1234.8 6.9 multiply_add_fusion
  1241.8 7.3 fusion.184
  1251.0 7.1 fusion.185
  1272.7 5.7 convolution_add_fusion.3
  1285.6 5.9 convolution_add_fusion.2
  1298.7 5.7 convolution_add_fusion.1
  1311.6 5.7 convolution_add_fusion
  1324.4 5.7 fusion.168
  (412 shorter events, 298.5 us)
Async XLA Ops:
  7.2 59.9 %copy-start.56 = (f32[128,64]{0,1:T(8,128)S(1)}, f32[128,64]{0,1:T(8,128)}, u32[]{:S(2)}) copy-start(f32[128,64]{0,1:T(8,128)} %param.27) | copy-start | bytes 98308
  7.2 59.9 %copy-start.51 = (s32[2,512,16]{1,2,0:T(8,128)S(1)}, s32[2,512,16]{1,2,0:T(8,128)}, u32[]{:S(2)}) copy-start(s32[2,512,16]{1,2,0:T(8,128)} %param.24) | copy-start | bytes 196612
  7.2 210.2 %reduce-scatter.13.cloned.1.call-start = ((), (), s32[]{:S(2)}) async-start(), calls=%async_computation.12 | async-start | bytes 1310720 | tf_op jit(solution)/shard_map/reduce_scatter | solution.py:62
  13.5 396.0 %copy-start.64 = (f32[128]{0:T(128)}, f32[128]{0:T(128)S(1)}, u32[]{:S(2)}) copy-start(f32[128]{0:T(128)S(1)} %get-tuple-element.150) | copy-start | bytes 1540
  62.6 39.3 %collective-permute-start.1 = (bf16[512,256]{1,0:T(8,128)(2,1)S(1)}, bf16[512,256]{1,0:T(8,128)(2,1)S(1)}, u32[]{:S(2)}, u32[]{:S(2)}) collective-permute-start(bf16[512,256]{1,0:T(8,128)(2,1)S(1)} %slice.137), channel_id=1, source_target_pairs={{4,0},{8,4},{12,8},{16,12},{20,16},{24,20},{28,24},{0,28},{5,1},{9... | collective-permute-start | bytes 786440 | tf_op jit(solution)/shard_map/ppermute | solution.py:32
  67.1 34.9 %collective-permute-start = (bf16[512,256]{1,0:T(8,128)(2,1)S(1)}, bf16[512,256]{1,0:T(8,128)(2,1)S(1)}, u32[]{:S(2)}, u32[]{:S(2)}) collective-permute-start(bf16[512,256]{1,0:T(8,128)(2,1)S(1)} %slice.137), channel_id=1, source_target_pairs={{0,4},{4,8},{8,12},{12,16},{16,20},{20,24},{24,28},{28,0},{1,5},{5... | collective-permute-start | bytes 786440 | tf_op jit(solution)/shard_map/ppermute | solution.py:31
  101.7 196.0 %copy-start.10 = (bf16[128,512]{0,1:T(8,128)(2,1)}, bf16[128,512]{0,1:T(8,128)(2,1)S(1)}, u32[]{:S(2)}) copy-start(bf16[128,512]{0,1:T(8,128)(2,1)S(1)} %all_gather.62) | copy-start | bytes 393220
  142.8 74.6 %copy-start.2 = (bf16[2,512,128]{2,1,0:T(8,128)(2,1)S(1)}, bf16[2,512,128]{2,1,0:T(8,128)(2,1)}, u32[]{:S(2)}) copy-start(bf16[2,512,128]{2,1,0:T(8,128)(2,1)} %param.21) | copy-start | bytes 786436
  146.6 114.3 %reduce-scatter.21.cloned.1.call-start = ((), (), s32[]{:S(2)}) async-start(), calls=%async_computation.16 | async-start | bytes 1310720 | tf_op jit(solution)/shard_map/reduce_scatter | solution.py:62
  154.8 77.9 %copy-start.14 = (bf16[512,512]{1,0:T(8,128)(2,1)}, bf16[512,512]{1,0:T(8,128)(2,1)S(1)}, u32[]{:S(2)}) copy-start(bf16[512,512]{1,0:T(8,128)(2,1)S(1)} %all_gather.68) | copy-start | bytes 1572868
  186.1 49.6 %copy-start.17 = (bf16[512,512]{0,1:T(8,128)(2,1)}, bf16[512,512]{0,1:T(8,128)(2,1)S(1)}, u32[]{:S(2)}) copy-start(bf16[512,512]{0,1:T(8,128)(2,1)S(1)} %all_gather.65) | copy-start | bytes 1572868
  234.1 54.3 %copy-start.32 = (bf16[2,512,128]{2,1,0:T(8,128)(2,1)S(1)}, bf16[2,512,128]{2,1,0:T(8,128)(2,1)}, u32[]{:S(2)}) copy-start(bf16[2,512,128]{2,1,0:T(8,128)(2,1)} %param.23) | copy-start | bytes 786436
  235.6 52.7 %reduce-scatter.15.cloned.1.call-start = ((), (), s32[]{:S(2)}) async-start(), calls=%async_computation.13 | async-start | bytes 1310720 | tf_op jit(solution)/shard_map/reduce_scatter | solution.py:62
  237.2 172.3 %reduce-scatter.23.cloned.1.call-start = ((), (), s32[]{:S(2)}) async-start(), calls=%async_computation.17 | async-start | bytes 1310720 | tf_op jit(solution)/shard_map/reduce_scatter | solution.py:62
  239.4 67.9 %copy-start.61 = (f32[512]{0:T(512)}, f32[512]{0:T(512)S(1)}, u32[]{:S(2)}) copy-start(f32[512]{0:T(512)S(1)} %fusion.129) | copy-start | bytes 6148
  307.3 53.8 %copy-start.50 = (f32[512,16,1]{1,2,0:T(1,128)S(1)}, f32[512,16,1]{1,2,0:T(1,128)}, u32[]{:S(2)}) copy-start(f32[512,16,1]{1,2,0:T(1,128)} %copy.95) | copy-start | bytes 98308
  356.3 29.0 %copy-start.55 = (s32[512,16]{0,1:T(8,128)S(1)}, s32[512,16]{0,1:T(8,128)}, u32[]{:S(2)}) copy-start(s32[512,16]{0,1:T(8,128)} %get-tuple-element.114) | copy-start | bytes 98308
  356.4 24.4 %collective-permute-start.4 = (f32[512,256]{1,0:T(8,128)S(1)}, f32[512,256]{1,0:T(8,128)S(1)}, u32[]{:S(2)}, u32[]{:S(2)}) collective-permute-start(f32[512,256]{1,0:T(8,128)S(1)} %get-tuple-element.122), channel_id=1, source_target_pairs={{0,4},{4,8},{8,12},{12,16},{16,20},{20,24},{24,28},{28,0},{1,5},{5... | collective-permute-start | bytes 1572872 | tf_op jit(solution)/shard_map/ppermute | solution.py:31
  357.9 27.8 %copy-start.71 = (f32[4,128]{1,0:T(4,128)S(1)}, f32[4,128]{1,0:T(4,128)}, u32[]{:S(2)}) copy-start(f32[4,128]{1,0:T(4,128)} %get-tuple-element.154) | copy-start | bytes 6148
  357.9 25.1 %collective-permute-start.5 = (f32[512,256]{1,0:T(8,128)S(1)}, f32[512,256]{1,0:T(8,128)S(1)}, u32[]{:S(2)}, u32[]{:S(2)}) collective-permute-start(f32[512,256]{1,0:T(8,128)S(1)} %get-tuple-element.123), channel_id=1, source_target_pairs={{4,0},{8,4},{12,8},{16,12},{20,16},{24,20},{28,24},{0,28},{5,1},{9... | collective-permute-start | bytes 1572872 | tf_op jit(solution)/shard_map/ppermute | solution.py:32
  364.6 65.4 %copy-start.60 = (pred[512,16]{0,1:T(8,128)(4,1)S(1)}, pred[512,16]{0,1:T(8,128)(4,1)}, u32[]{:S(2)}) copy-start(pred[512,16]{0,1:T(8,128)(4,1)} %get-tuple-element.113) | copy-start | bytes 24580
  385.3 125.9 %reduce-scatter.17.cloned.1.call-start = ((), (), s32[]{:S(2)}) async-start(), calls=%async_computation.14 | async-start | bytes 1310720 | tf_op jit(solution)/shard_map/reduce_scatter | solution.py:62
  385.7 50.0 %copy-start.66 = (f32[128]{0:T(128)}, f32[128]{0:T(128)S(1)}, u32[]{:S(2)}) copy-start(f32[128]{0:T(128)S(1)} %get-tuple-element.142) | copy-start | bytes 1540
  425.3 10.4 collective-permute-start.3
  429.6 11.5 collective-permute-start.2
  485.4 40.8 %copy-start.18 = (bf16[512,512]{0,1:T(8,128)(2,1)S(1)}, bf16[512,512]{0,1:T(8,128)(2,1)}, u32[]{:S(2)}) copy-start(bf16[512,512]{0,1:T(8,128)(2,1)} %copy-done.17) | copy-start | bytes 1572868
  486.7 69.2 %reduce-scatter.25.cloned.1.call-start = ((), (), s32[]{:S(2)}) async-start(), calls=%async_computation.18 | async-start | bytes 1310720 | tf_op jit(solution)/shard_map/reduce_scatter | solution.py:62
  530.5 52.8 %copy-start.33 = (bf16[2,512,128]{2,1,0:T(8,128)(2,1)S(1)}, bf16[2,512,128]{2,1,0:T(8,128)(2,1)}, u32[]{:S(2)}) copy-start(bf16[2,512,128]{2,1,0:T(8,128)(2,1)} %param.23) | copy-start | bytes 786436
  530.6 52.8 %copy-start.62 = (f32[512]{0:T(512)S(1)}, f32[512]{0:T(512)}, u32[]{:S(2)}) copy-start(f32[512]{0:T(512)} %copy-done.61) | copy-start | bytes 6148
  530.6 52.8 %reduce-scatter.19.cloned.1.call-start = ((), (), s32[]{:S(2)}) async-start(), calls=%async_computation.15 | async-start | bytes 1310720 | tf_op jit(solution)/shard_map/reduce_scatter | solution.py:62
  533.6 161.5 %reduce-scatter.31.cloned.1.call-start = ((), (), s32[]{:S(2)}) async-start(), calls=%async_computation.21 | async-start | bytes 294912 | tf_op jit(solution)/shard_map/reduce_scatter | solution.py:269
  594.6 138.1 %reduce-scatter.33.cloned.1.call-start = ((), (), s32[]{:S(2)}) async-start(), calls=%async_computation.22 | async-start | bytes 1179648 | tf_op jit(solution)/shard_map/reduce_scatter | solution.py:270
  598.9 199.6 %reduce-scatter.35.cloned.1.call-start = ((), (), s32[]{:S(2)}) async-start(), calls=%async_computation.23 | async-start | bytes 1179648 | tf_op jit(solution)/shard_map/reduce_scatter | solution.py:271
  605.7 258.0 %reduce-scatter.29.cloned.1.call-start = ((), (), s32[]{:S(2)}) async-start(), calls=%async_computation.20 | async-start | bytes 884736 | tf_op jit(solution)/shard_map/reduce_scatter | solution.py:268
  663.1 30.4 %copy-start.4 = (bf16[512,512]{1,0:T(8,128)(2,1)S(1)}, bf16[512,512]{1,0:T(8,128)(2,1)}, u32[]{:S(2)}) copy-start(bf16[512,512]{1,0:T(8,128)(2,1)} %copy-done.3) | copy-start | bytes 1572868
  663.1 30.4 %copy-start.13 = (bf16[512,256]{1,0:T(8,128)(2,1)S(1)}, bf16[512,256]{1,0:T(8,128)(2,1)}, u32[]{:S(2)}) copy-start(bf16[512,256]{1,0:T(8,128)(2,1)} %copy-done.12) | copy-start | bytes 786436
  663.1 30.4 %copy-start.23 = (bf16[512,128]{1,0:T(8,128)(2,1)S(1)}, bf16[512,128]{1,0:T(8,128)(2,1)}, u32[]{:S(2)}) copy-start(bf16[512,128]{1,0:T(8,128)(2,1)} %copy-done.22) | copy-start | bytes 393220
  663.2 27.3 %collective-permute-start.6 = (f32[512,256]{1,0:T(8,128)S(1)}, f32[512,256]{1,0:T(8,128)S(1)}, u32[]{:S(2)}, u32[]{:S(2)}) collective-permute-start(f32[512,256]{1,0:T(8,128)S(1)} %get-tuple-element.120), channel_id=1, source_target_pairs={{0,4},{4,8},{8,12},{12,16},{16,20},{20,24},{24,28},{28,0},{1,5},{5... | collective-permute-start | bytes 1572872 | tf_op jit(solution)/shard_map/ppermute | solution.py:31
  664.7 27.9 %collective-permute-start.7 = (f32[512,256]{1,0:T(8,128)S(1)}, f32[512,256]{1,0:T(8,128)S(1)}, u32[]{:S(2)}, u32[]{:S(2)}) collective-permute-start(f32[512,256]{1,0:T(8,128)S(1)} %get-tuple-element.121), channel_id=1, source_target_pairs={{4,0},{8,4},{12,8},{16,12},{20,16},{24,20},{28,24},{0,28},{5,1},{9... | collective-permute-start | bytes 1572872 | tf_op jit(solution)/shard_map/ppermute | solution.py:32
  692.8 107.5 %copy-start.7 = (f32[4,256,128]{2,1,0:T(8,128)S(1)}, f32[4,256,128]{2,1,0:T(8,128)}, u32[]{:S(2)}) copy-start(f32[4,256,128]{2,1,0:T(8,128)} %param.34) | copy-start | bytes 1572868
  693.5 39.2 %copy-start.52 = (f32[64,512]{1,0:T(8,128)S(1)}, f32[64,512]{1,0:T(8,128)}, u32[]{:S(2)}) copy-start(f32[64,512]{1,0:T(8,128)} %param.32) | copy-start | bytes 393220
  693.5 105.0 %copy-start.53 = (f32[512,64]{0,1:T(8,128)S(1)}, f32[512,64]{0,1:T(8,128)}, u32[]{:S(2)}) copy-start(f32[512,64]{0,1:T(8,128)} %param.33) | copy-start | bytes 393220
  693.5 107.8 %copy-start.38 = (f32[4,256,128]{2,1,0:T(8,128)S(1)}, f32[4,256,128]{2,1,0:T(8,128)}, u32[]{:S(2)}) copy-start(f32[4,256,128]{2,1,0:T(8,128)} %param.36) | copy-start | bytes 1572868
  693.5 108.8 %copy-start.39 = (f32[4,256,128]{2,1,0:T(8,128)S(1)}, f32[4,256,128]{2,1,0:T(8,128)}, u32[]{:S(2)}) copy-start(f32[4,256,128]{2,1,0:T(8,128)} %param.37) | copy-start | bytes 1572868
  694.9 108.5 %copy-start.72 = (f32[128]{0:T(128)S(1)}, f32[128]{0:T(128)}, u32[]{:S(2)}) copy-start(f32[128]{0:T(128)} %get-tuple-element.67) | copy-start | bytes 1540
  694.9 108.5 %copy-start.73 = (f32[128]{0:T(128)S(1)}, f32[128]{0:T(128)}, u32[]{:S(2)}) copy-start(f32[128]{0:T(128)} %get-tuple-element.79) | copy-start | bytes 1540
  694.9 108.5 %copy-start.74 = (f32[128]{0:T(128)S(1)}, f32[128]{0:T(128)}, u32[]{:S(2)}) copy-start(f32[128]{0:T(128)} %get-tuple-element.65) | copy-start | bytes 1540
  694.9 108.5 %copy-start.75 = (f32[128]{0:T(128)S(1)}, f32[128]{0:T(128)}, u32[]{:S(2)}) copy-start(f32[128]{0:T(128)} %get-tuple-element.77) | copy-start | bytes 1540
  694.9 108.5 %copy-start.43 = (bf16[1,512,128]{2,1,0:T(8,128)(2,1)S(1)}, bf16[1,512,128]{2,1,0:T(8,128)(2,1)}, u32[]{:S(2)}) copy-start(bf16[1,512,128]{2,1,0:T(8,128)(2,1)} %get-tuple-element.129) | copy-start | bytes 393220
  694.9 108.5 %copy-start.48 = (bf16[1,512,128]{2,1,0:T(8,128)(2,1)S(1)}, bf16[1,512,128]{2,1,0:T(8,128)(2,1)}, u32[]{:S(2)}) copy-start(bf16[1,512,128]{2,1,0:T(8,128)(2,1)} %get-tuple-element.128) | copy-start | bytes 393220
  694.9 168.8 %copy-start.59 = (f32[64,384]{1,0:T(8,128)S(1)}, f32[64,384]{1,0:T(8,128)}, u32[]{:S(2)}) copy-start(f32[64,384]{1,0:T(8,128)} %param.30) | copy-start | bytes 294916
  695.0 223.5 %all-gather.11.cloned.1.call-start = ((), (), s32[]{:S(2)}) async-start(), calls=%async_computation.25 | async-start | bytes 1081344 | tf_op jit(solution)/shard_map/all_gather | solution.py:281
  696.5 256.5 %reduce-scatter.27.cloned.1.call-start = ((), (), s32[]{:S(2)}) async-start(), calls=%async_computation.19 | async-start | bytes 1310720 | tf_op jit(solution)/shard_map/reduce_scatter | solution.py:62
  699.0 313.0 %all-gather.13.cloned.1.call-start = ((), (), s32[]{:S(2)}) async-start(), calls=%async_computation.26 | async-start | bytes 4325376 | tf_op jit(solution)/shard_map/all_gather | solution.py:282
  734.3 341.8 %all-gather.15.cloned.1.call-start = ((), (), s32[]{:S(2)}) async-start(), calls=%async_computation.27 | async-start | bytes 4325376 | tf_op jit(solution)/shard_map/all_gather | solution.py:283
  800.1 458.9 %all-gather.9.cloned.1.call-start = ((), (), s32[]{:S(2)}) async-start(), calls=%async_computation.24 | async-start | bytes 3244032 | tf_op jit(solution)/shard_map/all_gather | solution.py:280
  948.5 25.8 %copy-start.40 = (f32[4,256,128]{1,2,0:T(8,128)S(1)}, f32[4,256,128]{1,2,0:T(8,128)}, u32[]{:S(2)}) copy-start(f32[4,256,128]{1,2,0:T(8,128)} %copy.79) | copy-start | bytes 1572868
  950.4 27.9 %copy-start.68 = (f32[512]{0:T(512)S(1)}, f32[512]{0:T(512)}, u32[]{:S(2)}) copy-start(f32[512]{0:T(512)} %get-tuple-element.66) | copy-start | bytes 6148
  950.5 27.9 %copy-start.69 = (f32[512]{0:T(512)S(1)}, f32[512]{0:T(512)}, u32[]{:S(2)}) copy-start(f32[512]{0:T(512)} %get-tuple-element.76) | copy-start | bytes 6148
  952.3 35.4 %copy-start.24 = (f32[512,128]{1,0:T(8,128)S(1)}, f32[512,128]{1,0:T(8,128)}, u32[]{:S(2)}) copy-start(f32[512,128]{1,0:T(8,128)} %get-tuple-element.116) | copy-start | bytes 786436
  952.4 35.4 %copy-start.26 = (f32[512,128]{1,0:T(8,128)S(1)}, f32[512,128]{1,0:T(8,128)}, u32[]{:S(2)}) copy-start(f32[512,128]{1,0:T(8,128)} %reduce-scatter.23.cloned.1.call-done) | copy-start | bytes 786436
  952.4 35.4 %copy-start.29 = (f32[512,128]{1,0:T(8,128)S(1)}, f32[512,128]{1,0:T(8,128)}, u32[]{:S(2)}) copy-start(f32[512,128]{1,0:T(8,128)} %get-tuple-element.111) | copy-start | bytes 786436
  952.4 35.3 %copy-start.65 = (f32[128]{0:T(128)S(1)}, f32[128]{0:T(128)}, u32[]{:S(2)}) copy-start(f32[128]{0:T(128)} %copy-done.64) | copy-start | bytes 1540
  953.0 34.7 %copy-start.27 = (f32[512,128]{1,0:T(8,128)S(1)}, f32[512,128]{1,0:T(8,128)}, u32[]{:S(2)}) copy-start(f32[512,128]{1,0:T(8,128)} %reduce-scatter.27.cloned.1.call-done) | copy-start | bytes 786436
  (41 other events, 316.6 us)
Sparse Core Ops, SparseCore 0:
  146.8 24.4 reduce-scatter.12
  235.8 25.0 reduce-scatter.20
  263.4 24.9 reduce-scatter.14
  385.4 24.0 reduce-scatter.22
  486.8 24.4 reduce-scatter.16
  530.7 25.1 reduce-scatter.24
  558.4 24.8 reduce-scatter.18
  594.7 61.6 reduce-scatter.30
  660.2 72.4 reduce-scatter.32
  735.9 62.5 reduce-scatter.34
  802.1 61.5 reduce-scatter.28
  867.0 51.4 all-gather.10
  921.0 24.7 reduce-scatter.26
  949.5 62.4 all-gather.12
  1015.7 60.2 all-gather.14
  1079.7 57.3 all-gather.8
where the time goes:
time: 1350 us; the launch traced here: 1340 us
  waiting for transfers between devices  457 us (34%)
  matrix products  316 us (23%)
  blocking collectives  246 us (18%)
  other arithmetic  171 us (13%)
  local copies, waits for them, and re-layouts  110 us (8%)
  starting transfers between devices  19.7 us (1%)
  between operations  19.1 us (1%)
    reduce_scatter x8, waiting for transfers between devices, head_sum(): lax.psum_scatter(partial_rows, 'heads', scatter_dimension=1, tiled=True)  124 us
    dot_general x20, matrix products, orthogonal(): iterate = NEWTON_A * iterate + jnp.dot(polynomial, iterate, precision=HIGH)  109 us
    dot_general x20, matrix products, orthogonal(): square = jnp.dot(iterate, iterate.T, precision=HIGH)  106 us
    scatter-add x2, other arithmetic, per_device(): grad_ext = jnp.zeros((3 * capacity, 2 * head_dim), f32).at[local_index].a...  90 us
    gather x2, local copies, waits for them, and re-layouts, per_device(): gathered_rows = jnp.take(key_value_ext, local_index, axis=0)  65.9 us
    reduce_scatter x1, waiting for transfers between devices, per_device(): lax.psum_scatter(grad_contract, 'nodes', scatter_dimension=1, tiled=True)  64.2 us
    reduce_scatter x1, waiting for transfers between devices, per_device(): lax.psum_scatter(grad_project, 'nodes', scatter_dimension=0, tiled=True)  59.6 us
    all_gather x8, blocking collectives, full_rows(): return lax.all_gather(piece, 'heads', axis=1, tiled=True)  56.6 us
  transfers between devices with their start and end apart: 24, of which 18 were waited for; matrix products, arithmetic and copies ran while one was open for 26% of the time, Pallas kernels for 0%

commit v1 on v0

v1 whole, which is shorter than its diff:
```python
import functools

import jax
import jax.numpy as jnp
from jax import lax
from jax.experimental import pallas as pl
from jax.experimental.pallas import tpu as pltpu
from jax.sharding import PartitionSpec as P

NS_STEPS = 5
STEP = 10


EPS_NORM = 1e-06
NEWTON_A = 3.4445
NEWTON_B = -4.775
NEWTON_C = 2.0315
MOMENTUM_DECAY = 0.5
LR_MUON = 1.0
LR_ADAM = 0.04
DECAY_WEIGHT = 0.01
BETA_FIRST = 0.9
BETA_SECOND = 0.999
EPS_ADAM = 1e-08
HIGH = lax.Precision.HIGHEST
MESH = pl.DeviceIdType.MESH
F32 = jnp.float32
BF16 = jnp.bfloat16
NN = (((1,), (0,)), ((), ()))
NT = (((1,), (1,)), ((), ()))
TN = (((0,), (0,)), ((), ()))


def mul(left, right, dims=NN):
    return lax.dot_general(left, right, dims, preferred_element_type=F32)


class Links:
    def __init__(self, send_sems, recv_sems):
        self.send_sems, self.recv_sems = send_sems, recv_sems
        self.copies = []

    def send(self, source, target, device):
        slot = len(self.copies)
        copy = pltpu.make_async_remote_copy(
            src_ref=source,
            dst_ref=target,
            send_sem=self.send_sems.at[slot],
            recv_sem=self.recv_sems.at[slot],
            device_id=device,
            device_id_type=MESH,
        )
        copy.start()
        self.copies.append(copy)
        return copy

    def close(self):
        for copy in self.copies:
            copy.wait_send()


def meet(devices):
    barrier = pltpu.get_barrier_semaphore()
    for device in devices:
        pl.semaphore_signal(barrier, inc=1, device_id=device, device_id_type=MESH)
    pl.semaphore_wait(barrier, len(devices))


def norm_rows(values):
    width = values.shape[-1]
    row_mean = jnp.sum(values, axis=-1, keepdims=True) / width
    square_mean = jnp.sum(values * values, axis=-1, keepdims=True) / width
    inv_root = lax.rsqrt(square_mean - row_mean * row_mean + EPS_NORM)
    return ((values - row_mean) * inv_root, inv_root)


def wide(ref, *index):
    return jnp.concatenate([ref[(head, *index)] for head in range(ref.shape[0])], axis=-1)


def mod_row(mod_ref, batch, number):
    return wide(mod_ref, slice(batch * 4 + number, batch * 4 + number + 1), slice(None))


def attend_kernel(
    patch_count,
    own_gather,
    state_ref,
    cot_ref,
    index_ref,
    mod_ref,
    weight_ref,
    state_all,
    cot_all,
    mod_all,
    a_one,
    queries,
    key_value,
    prob_low,
    mixed_all,
    weight_all,
    output_all,
    halo,
    count,
    send_sems,
    recv_sems,
):
    node, head = lax.axis_index("nodes"), lax.axis_index("heads")
    after, before = lax.rem(node + 1, patch_count), lax.rem(node + patch_count - 1, patch_count)
    across, sibling = lax.rem(head + 2, 4), head + 1 - 2 * lax.rem(head, 2)
    to_across, to_sibling, to_diagonal = (node, across), (node, sibling), (node, 3 - head)
    to_after, to_before = (after, head), (before, head)
    partner = node + 1 - 2 * lax.rem(node, 2)
    peers = [(lax.rem(node + 2 * k, patch_count), head) for k in range(1, patch_count // 2)]
    met = [to_across, to_sibling, to_diagonal, to_after, to_before]
    meet(met + peers if own_gather else met)
    micro_count, capacity, share = state_ref.shape
    head_dim = queries.shape[-1]
    total = 3 * capacity
    links = Links(send_sems, recv_sems)

    state_across = links.send(state_ref, state_all.at[head], to_across)
    state_after = links.send(state_ref, halo.at[0, head], to_after)
    state_before = links.send(state_ref, halo.at[1, head], to_before)
    state_sibling = links.send(state_ref, state_all.at[head], to_sibling)
    mod_copies = [
        links.send(mod_ref, mod_all.at[head], to)
        for to in (to_across, to_sibling, to_diagonal)
    ]
    first_columns, other_columns = pl.ds(0, 3 * head_dim), pl.ds(3 * head_dim, weight_ref.shape[-1] - 3 * head_dim)

    def spread(columns):
        part = weight_ref.at[:, columns]
        into = weight_all.at[node, :, columns]
        return [links.send(part, into, to) for to in peers], [
            links.send(part, into, (partner, head))
        ]

    def pass_on(arriving, columns):
        passed = []
        for k, copy in enumerate(arriving):
            copy.wait_recv()
            owner = lax.rem(node + patch_count - 2 * (k + 1), patch_count)
            passed.append(
                links.send(
                    weight_all.at[owner, :, columns],
                    weight_all.at[owner, :, columns],
                    (partner, head),
                )
            )
        return passed

    if own_gather:
        first_peers, first_partner = spread(first_columns)
        weight_all[node] = weight_ref[...]
    state_all[head] = state_ref[...]
    cot_all[head] = cot_ref[...]
    mod_all[head] = mod_ref[...]

    group = index_ref.shape[-1] // 16
    blocks = total // share

    def count_group(batch, place):
        ids = index_ref[batch, pl.ds(place, 1), :]
        lanes = lax.broadcasted_iota(jnp.int32, ids.shape, 1)
        code = (ids >> 7) + 16 * (lanes >> 4)
        rows = lax.broadcasted_iota(jnp.int32, (blocks * group, ids.shape[1]), 0)
        pick = jnp.where(code == (rows // group) + 16 * (rows % group), 1.0, 0.0).astype(BF16)
        slots = lax.broadcasted_iota(jnp.int32, (share, ids.shape[1]), 0)
        spot = jnp.where((ids & 127) == slots, 1.0, 0.0).astype(BF16)
        found = mul(pick, spot, NT).astype(BF16)
        for block in range(blocks):
            count[batch, pl.ds(pl.multiple_of(place * group, group), group), block * share : (block + 1) * share] = found[
                block * group : (block + 1) * group
            ]

    for batch in range(micro_count):

        @pl.loop(0, capacity // group)
        def _(place):
            count_group(batch, place)

    state_across.wait_recv()
    pass_state = links.send(state_all.at[across], state_all.at[across], to_sibling)
    halo_across, halo_sibling = [], []
    for side, copy in ((0, state_after), (1, state_before)):
        copy.wait_recv()
        halo_across.append(links.send(halo.at[side, head], halo.at[side, head], to_across))
        halo_sibling.append(links.send(halo.at[side, head], halo.at[side, head], to_sibling))
    if own_gather:
        first_passed = pass_on(first_peers, first_columns)
        other_peers, other_partner = spread(other_columns)
    state_sibling.wait_recv()
    pass_state.wait_recv()
    for copy in mod_copies:
        copy.wait_recv()
    if own_gather:
        for copy in first_partner + first_passed:
            copy.wait_recv()
    inv_head = head_dim ** (-0.5)
    tile = capacity // 2

    def project(source, patch):
        for batch in range(micro_count):
            shift, scale = mod_row(mod_all, batch, 0), 1.0 + mod_row(mod_all, batch, 1)

            @pl.loop(0, capacity // tile)
            def _(step):
                rows = pl.ds(pl.multiple_of(step * tile, tile), tile)
                normed, _ = norm_rows(wide(source, batch, rows, slice(None)).astype(F32))
                a_rows = (normed * scale + shift).astype(BF16)
                a_one[patch, batch, rows, :] = a_rows
                first = 0 if patch == 1 else head_dim
                weight = weight_all[:, :, first : 3 * head_dim].reshape(4 * share, 3 * head_dim - first)
                out = mul(a_rows, weight).astype(BF16)
                if patch == 1:
                    queries[batch, rows, :] = out[:, :head_dim]
                key_value[batch, patch, rows, :] = out[:, out.shape[1] - 2 * head_dim :]

    project(state_all, 1)
    for side in range(2):
        halo_across[side].wait_recv()
        halo_sibling.append(links.send(halo.at[side, across], halo.at[side, across], to_sibling))
    cot_across = links.send(cot_ref, cot_all.at[head], to_across)
    cot_sibling = links.send(cot_ref, cot_all.at[head], to_sibling)
    for copy in halo_sibling:
        copy.wait_recv()
    project(halo.at[0], 0)
    project(halo.at[1], 2)
    if own_gather:
        other_passed = pass_on(other_peers, other_columns)

    attend_rows = 128
    mixed_copies = []
    for batch in range(micro_count):

        @pl.loop(0, capacity // attend_rows)
        def _(step):
            rows = pl.ds(pl.multiple_of(step * attend_rows, attend_rows), attend_rows)
            keys = key_value[batch, :, :, :head_dim].reshape(total, head_dim)
            values = key_value[batch, :, :, head_dim:].reshape(total, head_dim)
            scores = mul(queries[batch, rows, :], keys, NT) * inv_head
            times = count[batch, rows, :].astype(F32)
            scores = jnp.where(times > 0.0, scores, -1e30)
            exps = jnp.exp(scores - jnp.max(scores, axis=-1, keepdims=True)) * times
            prob = (exps * (1.0 / jnp.sum(exps, axis=-1, keepdims=True))).astype(BF16)
            prob_low[batch, rows, :] = prob
            mixed_all[head, batch, rows, :] = mul(prob, values).astype(BF16)

        part = mixed_all.at[head, batch]
        mixed_copies.append(
            (batch, links.send(part, part, to_across), links.send(part, part, to_sibling))
        )

    cot_across.wait_recv()
    last = [cot_sibling, links.send(cot_all.at[across], cot_all.at[across], to_sibling)]
    if own_gather:
        for copy in other_partner + other_passed:
            copy.wait_recv()
        output_columns = pl.ds(3 * head_dim, head_dim)
        output_all[head] = weight_all[:, :, 3 * head_dim : 4 * head_dim]
        output_part = weight_all.at[:, :, output_columns]
        output_across = links.send(output_part, output_all.at[head], to_across)
        last.append(links.send(output_part, output_all.at[head], to_sibling))
        output_across.wait_recv()
        last.append(links.send(output_all.at[across], output_all.at[across], to_sibling))
    for batch, copy, other in mixed_copies:
        copy.wait_recv()
        part = mixed_all.at[across, batch]
        last += [other, links.send(part, part, to_sibling)]
    for copy in last:
        copy.wait_recv()
    links.close()


def adam_step(weight, first_old, second_old, gradient):
    first_new = BETA_FIRST * first_old + (1.0 - BETA_FIRST) * gradient
    second_new = BETA_SECOND * second_old + (1.0 - BETA_SECOND) * gradient * gradient
    first_hat = first_new / (1.0 - BETA_FIRST**STEP)
    second_hat = second_new / (1.0 - BETA_SECOND**STEP)
    updated = weight * (1.0 - LR_ADAM * DECAY_WEIGHT) - LR_ADAM * first_hat / (
        jnp.sqrt(second_hat) + EPS_ADAM
    )
    return (first_new, second_new, updated)


def orthogonal(matrix):
    scale = 1.0 / (jnp.sqrt(jnp.sum(matrix * matrix)) + 1e-07)
    gram = jnp.dot(matrix, matrix.T, precision=HIGH) * (scale * scale)
    eye = jnp.eye(gram.shape[0], dtype=F32)
    chain = None
    for repeat in range(NS_STEPS):
        factor = NEWTON_A * eye + NEWTON_B * gram + NEWTON_C * jnp.dot(gram, gram, precision=HIGH)
        chain = factor if chain is None else jnp.dot(factor, chain, precision=HIGH)
        if repeat < NS_STEPS - 1:
            gram = jnp.dot(factor, jnp.dot(factor, gram, precision=HIGH), precision=HIGH)
    return jnp.dot(chain, matrix, precision=HIGH) * scale


def per_device(
    node_state,
    noise_embed,
    out_grad,
    neighbours,
    patch_sizes,
    w_project,
    w_output,
    w_expand,
    w_contract,
    momentum_project,
    momentum_output,
    momentum_expand,
    momentum_contract,
    w_modulate,
    b_modulate,
    first_modulate,
    second_modulate,
    first_bias,
    second_bias,
):
    micro_count, capacity, share = node_state.shape
    head_count = lax.axis_size("heads")
    patch_count = lax.axis_size("nodes")
    full_width = share * head_count
    head_dim = w_output.shape[0]
    total_rows = capacity * patch_count
    patch_index = lax.axis_index("nodes")
    head_index = lax.axis_index("heads")
    inv_head = head_dim ** (-0.5)
    hidden = w_expand.shape[1]
    shard_rows = w_project.shape[0]
    own_gather = patch_count == 8

    modulation = (
        jnp.einsum("bc,jcd->bjd", noise_embed, w_modulate, precision=HIGH) + b_modulate
    ).reshape(micro_count * 4, share)
    local_index = jnp.mod(neighbours - (patch_index - 1) * capacity, total_rows)
    index_rows = local_index.reshape(micro_count, capacity // 16, 256)
    weight_cat = jnp.concatenate([w_project, w_output.T, w_expand, w_contract.T], axis=1)
    low_cat = weight_cat.astype(BF16)
    weight_width = low_cat.shape[1]
    if not own_gather:
        low_cat = lax.all_gather(low_cat, "nodes", axis=0, tiled=True).reshape(8, full_width // 8, weight_width)
    vmem = pl.BlockSpec(memory_space=pltpu.VMEM)
    rows_all = jax.ShapeDtypeStruct((head_count, micro_count, capacity, share), BF16)
    out_shape = [
        rows_all,
        rows_all,
        jax.ShapeDtypeStruct((head_count, micro_count * 4, share), F32),
        jax.ShapeDtypeStruct((3, micro_count, capacity, full_width), BF16),
        jax.ShapeDtypeStruct((micro_count, capacity, head_dim), BF16),
        jax.ShapeDtypeStruct((micro_count, 3, capacity, 2 * head_dim), BF16),
        jax.ShapeDtypeStruct((micro_count, capacity, 3 * capacity), BF16),
        rows_all,
    ]
    if own_gather:
        out_shape += [
            jax.ShapeDtypeStruct((patch_count, shard_rows, weight_width), BF16),
            jax.ShapeDtypeStruct((head_count, patch_count, shard_rows, head_dim), BF16),
        ]

    def attend_body(*refs):
        refs = list(refs)
        if not own_gather:
            refs[13:13] = [refs[4], None]
        attend_kernel(patch_count, own_gather, *refs)

    gathered = pl.pallas_call(
        attend_body,
        out_shape=out_shape,
        in_specs=[vmem] * 5,
        out_specs=[vmem] * len(out_shape),
        scratch_shapes=[
            pltpu.VMEM((2, head_count, micro_count, capacity, share), BF16),
            pltpu.VMEM((micro_count, capacity, 3 * capacity), BF16),
            pltpu.SemaphoreType.DMA((64,)),
            pltpu.SemaphoreType.DMA((64,)),
        ],
        compiler_params=pltpu.CompilerParams(
            collective_id=0, has_side_effects=True, vmem_limit_bytes=56 << 20
        ),
        name="attend",
    )(node_state, out_grad, index_rows, modulation, low_cat)
    state_all, cot_all, mod_all, a_one, queries, key_value, prob_low, mixed_all = gathered[:8]
    if own_gather:
        weight_all, output_all = gathered[8:]
    else:
        weight_all = low_cat
        output_all = lax.all_gather(
            low_cat[:, :, 3 * head_dim : 4 * head_dim], "heads", axis=0, tiled=False
        )
    weight_full = weight_all.reshape(full_width, weight_width)
    w_proj_low, w_out_low, w_exp_low, w_con_low = jnp.split(
        weight_full, (3 * head_dim, 4 * head_dim, 4 * head_dim + hidden), axis=1
    )
    output_full = output_all.reshape(head_count, full_width, head_dim).transpose(1, 0, 2).reshape(full_width, full_width)

    def rows_of(blocks):
        return blocks.transpose(1, 2, 0, 3).reshape(micro_count * capacity, full_width)

    def own_columns(rows):
        return lax.dynamic_slice_in_dim(rows, head_index * share, share, axis=1)

    def per_batch(number):
        terms = mod_all.reshape(head_count, micro_count, 4, share)[:, :, number].transpose(1, 0, 2)
        return jnp.repeat(terms.reshape(micro_count, full_width), capacity, axis=0)

    slot_ids = lax.broadcasted_iota(jnp.int32, (micro_count, capacity), 1)
    live = (slot_ids < patch_sizes).astype(F32).reshape(micro_count * capacity, 1)
    state = rows_of(state_all).astype(F32)
    mixed = rows_of(mixed_all)
    hidden_one = state + mul(mixed, output_full, NT)
    norm_two, root_two = norm_rows(hidden_one)
    scale_two = 1.0 + per_batch(3)
    a_two = (norm_two * scale_two + per_batch(2)).astype(BF16)
    up = mul(a_two, w_exp_low)
    gate = jax.nn.sigmoid(up)
    act = (up * gate).astype(BF16)
    result = own_columns(hidden_one) + lax.psum_scatter(
        mul(act, w_con_low, NT), "heads", scatter_dimension=1, tiled=True
    )
    layer_output = (result * live).astype(BF16).reshape(micro_count, capacity, share)
    cot = rows_of(cot_all) * live.astype(BF16)
    grad_act = mul(cot, w_con_low)
    grad_contract = mul(cot, act, TN)
    grad_up = (grad_act * gate * (1.0 + up * (1.0 - gate))).astype(BF16)
    grad_expand = mul(a_two, grad_up, TN)
    grad_two = lax.psum(mul(grad_up, w_exp_low, NT), "heads")

    def norm_back(grad, normed, root):
        mean_grad = jnp.sum(grad, axis=-1, keepdims=True) / full_width
        mean_cross = jnp.sum(grad * normed, axis=-1, keepdims=True) / full_width
        return root * (grad - mean_grad - normed * mean_cross)

    grad_hidden = cot.astype(F32) + norm_back(grad_two * scale_two, norm_two, root_two)
    grad_attn = grad_hidden.astype(BF16)
    grad_mixed = mul(grad_attn, w_out_low).astype(BF16).reshape(micro_count, capacity, head_dim)
    own_mixed = lax.dynamic_index_in_dim(mixed_all, head_index, 0, keepdims=False)
    grad_output = mul(grad_attn, own_mixed.reshape(-1, head_dim), TN)
    keys = key_value[..., :head_dim].reshape(micro_count, 3 * capacity, head_dim)
    values = key_value[..., head_dim:].reshape(micro_count, 3 * capacity, head_dim)
    grad_prob = jnp.einsum("brd,bmd->brm", grad_mixed, values, preferred_element_type=F32)
    prob = prob_low.astype(F32)
    grad_score = prob * (grad_prob - jnp.sum(prob * grad_prob, axis=-1, keepdims=True))
    grad_score = (grad_score * inv_head).astype(BF16)
    grad_query = jnp.einsum("brm,bmd->brd", grad_score, keys, preferred_element_type=F32)
    grad_keys = jnp.einsum("brm,brd->bmd", grad_score, queries, preferred_element_type=F32)
    grad_values = jnp.einsum("brm,brd->bmd", prob_low, grad_mixed, preferred_element_type=F32)
    grad_ext = jnp.concatenate([grad_keys, grad_values], axis=-1).reshape(
        micro_count, 3, capacity, 2 * head_dim
    )
    up_perm = [(i, (i + 1) % patch_count) for i in range(patch_count)]
    down_perm = [(j, i) for i, j in up_perm]
    grad_kv = (
        grad_ext[:, 1]
        + lax.ppermute(grad_ext[:, 0].astype(BF16), "nodes", down_perm)
        + lax.ppermute(grad_ext[:, 2].astype(BF16), "nodes", up_perm)
    )
    grad_projected = (
        jnp.concatenate([grad_query, grad_kv], axis=-1).astype(BF16).reshape(-1, 3 * head_dim)
    )
    a_own = a_one[1].reshape(-1, full_width)
    grad_project = mul(a_own, grad_projected, TN)
    grad_one = lax.psum_scatter(
        mul(grad_projected, w_proj_low, NT), "heads", scatter_dimension=1, tiled=True
    )
    norm_one, root_one = norm_rows(state)
    norm_one = own_columns(norm_one)
    scale_one = own_columns(1.0 + per_batch(1))
    grad_in = grad_one * scale_one
    mean_grad, mean_cross = lax.psum(
        (jnp.sum(grad_in, axis=-1, keepdims=True), jnp.sum(grad_in * norm_one, axis=-1, keepdims=True)),
        "heads",
    )
    input_grad = own_columns(grad_hidden) + root_one * (
        grad_in - mean_grad / full_width - norm_one * mean_cross / full_width
    )
    grad_two_own, norm_two_own = own_columns(grad_two), own_columns(norm_two)

    def node_sum(rows):
        return jnp.sum(rows.reshape(micro_count, capacity, share), axis=1)

    mod_summed = lax.psum(
        jnp.stack(
            [
                node_sum(grad_one),
                node_sum(grad_one * norm_one),
                node_sum(grad_two_own),
                node_sum(grad_two_own * norm_two_own),
            ],
            axis=1,
        ),
        "nodes",
    )
    grad_modulate = jnp.einsum("bc,bjd->jcd", noise_embed, mod_summed, precision=HIGH)
    grad_bias = jnp.sum(mod_summed, axis=0)

    grad_cat = jnp.concatenate([grad_project, grad_output, grad_expand, grad_contract], axis=1)
    moment_cat = jnp.concatenate(
        [momentum_project, momentum_output.T, momentum_expand, momentum_contract.T], axis=1
    )
    moment_cat = MOMENTUM_DECAY * moment_cat + lax.psum_scatter(
        grad_cat, "nodes", scatter_dimension=0, tiled=True
    )
    whole = lax.all_gather(moment_cat.astype(BF16), ("nodes", "heads"), axis=0, tiled=False)
    whole = whole.reshape(patch_count, head_count, shard_rows, weight_width)
    whole = whole.transpose(0, 2, 1, 3).reshape(full_width, head_count, weight_width).astype(F32)
    cuts = (0, 3 * head_dim, 4 * head_dim, 4 * head_dim + hidden, weight_width)
    factors = (1.0, 1.0, 1.0, (head_count * hidden / full_width) ** 0.5)
    pieces = []
    for number in range(4):
        columns = cuts[number + 1] - cuts[number]
        matrix = whole[:, :, cuts[number] : cuts[number + 1]].reshape(full_width, head_count * columns)
        ortho = lax.dynamic_slice(
            orthogonal(matrix), (patch_index * shard_rows, head_index * columns), (shard_rows, columns)
        )
        pieces.append(factors[number] * ortho)
    new_cat = weight_cat * (1.0 - LR_MUON * DECAY_WEIGHT) - LR_MUON * jnp.concatenate(pieces, axis=1)

    def unpack(cat):
        project, output, expand, contract = (cat[:, cuts[i] : cuts[i + 1]] for i in range(4))
        return (project, output.T, expand, contract.T)

    first_mod, second_mod, new_mod = adam_step(
        w_modulate, first_modulate, second_modulate, grad_modulate
    )
    first_b, second_b, new_b = adam_step(b_modulate, first_bias, second_bias, grad_bias)
    return (
        layer_output,
        input_grad.reshape(micro_count, capacity, share),
        *unpack(moment_cat),
        *unpack(new_cat),
        first_mod,
        second_mod,
        new_mod,
        first_b,
        second_b,
        new_b,
    )


def solution(mesh):
    in_specs = (
        P(None, "nodes", "heads"),
        P(),
        P(None, "nodes", "heads"),
        P(None, "nodes", None),
        P(None, "nodes"),
        P("nodes", "heads"),
        P("heads", "nodes"),
        P("nodes", "heads"),
        P("heads", "nodes"),
        P("nodes", "heads"),
        P("heads", "nodes"),
        P("nodes", "heads"),
        P("heads", "nodes"),
        P(None, None, "heads"),
        P(None, "heads"),
        P(None, None, "heads"),
        P(None, None, "heads"),
        P(None, "heads"),
        P(None, "heads"),
    )
    out_specs = (
        P(None, "nodes", "heads"),
        P(None, "nodes", "heads"),
        P("nodes", "heads"),
        P("heads", "nodes"),
        P("nodes", "heads"),
        P("heads", "nodes"),
        P("nodes", "heads"),
        P("heads", "nodes"),
        P("nodes", "heads"),
        P("heads", "nodes"),
        P(None, None, "heads"),
        P(None, None, "heads"),
        P(None, None, "heads"),
        P(None, "heads"),
        P(None, "heads"),
        P(None, "heads"),
    )
    return jax.shard_map(
        per_device, mesh=mesh, in_specs=in_specs, out_specs=out_specs, check_vma=False
    )
```

time: 1350 us -> 632 us (0.47)
  waiting for transfers between devices: 457 us -> 184 us
  blocking collectives: 246 us -> 36.3 us
  other arithmetic: 171 us -> 39.2 us
  matrix products: 316 us -> 208 us
  Pallas kernels: 0 us -> 59 us
  local copies, waits for them, and re-layouts: 110 us -> 72.7 us
  starting transfers between devices: 19.7 us -> 4.71 us
    reduce_scatter x12 -> x2, waiting for transfers between devices: 281 us -> 49.2 us  [the longest x1 31.7 us: per_device(): lax.psum_scatter(mul(grad_projected, w_proj_low, NT), 'heads', scatter_di...]
    all_gather x12 -> x0, blocking collectives: 186 us -> none  [the longest x8 56.6 us: full_rows(): return lax.all_gather(piece, 'heads', axis=1, tiled=True)]
    dot_general x94 -> x92, matrix products: 314 us -> 205 us  [the longest x20 39.2 us: orthogonal(): jnp.dot(gram, gram, precision=HIGH)]
    all_gather x4 -> x1, waiting for transfers between devices: 126 us -> 16.8 us  [per_device(): lax.all_gather(moment_cat.astype(BF16), ('nodes', 'heads'), axis=0, tiled...]
    scatter-add x2 -> x0, other arithmetic: 90 us -> none  [per_device(): grad_ext = jnp.zeros((3 * capacity, 2 * head_dim), f32).at[local_index].a...]
    gather x2 -> x0, local copies, waits for them, and re-layouts: 65.9 us -> none  [per_device(): gathered_rows = jnp.take(key_value_ext, local_index, axis=0)]
    unnamed x16 -> x6, waiting for transfers between devices: 0.26 us -> 65.4 us
    pallas_call x0 -> x1, Pallas kernels: none -> 59 us  [per_device(): pl.pallas_call(attend_body, out_shape=out_shape, in_specs=[vmem] * 5, out...]
  transfers between devices with their start and end apart: 24 -> 7, of which waited for: 18 -> 6; matrix products, arithmetic and copies ran while one was open for 26% -> 10% of each run, Pallas kernels for 0% -> 0%
where the time goes in v1:
time: 632 us; the launch traced here: 622 us
  matrix products  208 us (33%)
  waiting for transfers between devices  184 us (29%)
  local copies, waits for them, and re-layouts  72.7 us (12%)
  Pallas kernels  59 us (9%)
  other arithmetic  39.2 us (6%)
  blocking collectives  36.3 us (6%)
  between operations  18.3 us (3%)
    unnamed x6, waiting for transfers between devices  65.4 us
    pallas_call x1, Pallas kernels, per_device(): pl.pallas_call(attend_body, out_shape=out_shape, in_specs=[vmem] * 5, out...  59 us
    psum x1, waiting for transfers between devices, per_device(): grad_two = lax.psum(mul(grad_up, w_exp_low, NT), 'heads')  40.1 us
    dot_general x20, matrix products, orthogonal(): jnp.dot(gram, gram, precision=HIGH)  39.2 us
    dot_general x16, matrix products, orthogonal(): chain = factor if chain is None else jnp.dot(factor, chain, precision=HIGH)  34.6 us
    dot_general x16, matrix products, orthogonal(): jnp.dot(factor, gram, precision=HIGH)  34.2 us
    reduce_scatter x1, waiting for transfers between devices, per_device(): lax.psum_scatter(mul(grad_projected, w_proj_low, NT), 'heads', scatter_di...  31.7 us
    dot_general x16, matrix products, orthogonal(): jnp.dot(factor, jnp.dot(factor, gram, precision=HIGH), precision=HIGH)  31.6 us
  transfers between devices with their start and end apart: 7, of which 6 were waited for; matrix products, arithmetic and copies ran while one was open for 10% of the time, Pallas kernels for 0%

profile of v1, /device:TPU:0, one launch (start us, length us, event | category | flops | bytes accessed | tf_op | source)
XLA Modules:
  0.0 621.9 jit_solution(18269008555015793852)
XLA Ops:
  13.7 59.0 %attend.1 = (bf16[4,2,512,128]{3,2,1,0:T(8,128)(2,1)}, bf16[4,2,512,128]{3,2,1,0:T(8,128)(2,1)}, f32[4,8,128]{2,1,0:T(8,128)}, bf16[3,2,512,512]{3,2,1,0:T(8,128...) custom-call(bf16[2,512,128]{2,1,0:T(8,128)(2,1)} %refs_0_.1, ...), custom_call_target="tpu_custom_call" | custom-call | tf_op jit(solution)/shard_map/attend/pallas_call | solution.py:368
  86.6 2.1 fusion.58
  90.1 2.3 slice.81
  96.3 2.0 fusion.45
  98.3 40.1 %all-reduce.3.cloned.1.call-done = f32[1024,512]{1,0:T(8,128)} async-done(((f32[1024,512]{1,0:T(8,128)}), f32[1024,512]{1,0:T(8,128)}) %all-reduce.3.cloned.1.call-update) | async-done | bytes 2097168 | tf_op jit(solution)/shard_map/psum | solution.py:428
  138.3 2.2 fusion.11
  140.8 2.5 multiply_add_fusion
  146.5 3.6 fusion.90
  150.1 9.5 %fusion.7 = f32[2,1536,128]{1,2,0:T(8,128)} fusion(bf16[2,512,128]{2,1,0:T(8,128)(2,1)S(1)} %copy-done.55, bf16[2,512,1536]{2,1,0:T(8,128)(2,1)} %get-tuple-element.32, f32[2,512,1536]{2,1,0:T(8,128)} %fusion.90), kind=kOutput, calls=%fused_computation.36 | convolution fusion | flops 413665792 | bytes 11272192 | tf_op jit(solution)/shard_map/brm,brd->bmd/dot_general | solution.py:447
  159.6 3.7 pad_maximum_fusion
  163.4 3.5 copy.94
  166.9 2.0 convert.17
  170.0 4.2 collective-permute-start
  174.2 8.2 %fusion.36 = bf16[2,512,128]{2,1,0:T(8,128)(2,1)S(1)} fusion(bf16[2,1536,128]{2,1,0:T(8,128)(2,1)S(1)} %bitcast.364, bf16[2,512,1536]{2,1,0:T(8,128)(2,1)} %get-tuple-element.32, f32[2,512,1536]{2,1,0:T(8,128)} %fusion.90), kind=kOutput, calls=%fused_computation.101 | convolution fusion | flops 413796864 | bytes 10485760 | tf_op jit(solution)/shard_map/brm,bmd->brd/dot_general | solution.py:446
  182.8 12.3 %collective-permute-done = bf16[2,512,256]{2,1,0:T(8,128)(2,1)} collective-permute-done((bf16[2,512,256]{2,1,0:T(8,128)(2,1)}, bf16[2,512,256]{2,1,0:T(8,128)(2,1)}, u32[]{:S(2)}, u32[]{:S(2)}) %collective-permute-start) | collective-permute-done | bytes 524320 | tf_op jit(solution)/shard_map/ppermute | solution.py:456
  198.4 2.0 pad_maximum_fusion.1
  200.4 3.5 copy.118
  204.0 3.8 fusion.56
  207.9 3.2 fusion.54
  213.7 65.3 %reduce-scatter.10.cloned.1.call-done = f32[64,1536]{1,0:T(8,128)} async-done(((f32[512,1536]{1,0:T(8,128)}), f32[64,1536]{1,0:T(8,128)}) %reduce-scatter.10.cloned.1.call-update) | async-done | bytes 393232
  280.3 2.2 fusion.86
  285.4 3.4 copy.141
  288.8 2.1 copy.106
  290.9 2.0 copy.107
  294.8 17.4 %reduce-scatter.6.cloned.1.call-done = f32[1024,128]{1,0:T(8,128)} async-done(((f32[1024,512]{1,0:T(8,128)}), f32[1024,128]{1,0:T(8,128)}) %reduce-scatter.6.cloned.1.call-update) | async-done | bytes 524304 | tf_op jit(solution)/shard_map/reduce_scatter | solution.py:419
  312.3 2.1 multiply_convert_fusion.2
  314.4 31.7 %reduce-scatter.8.cloned.1.call-done = f32[1024,128]{1,0:T(8,128)} async-done(((f32[1024,512]{1,0:T(8,128)}), f32[1024,128]{1,0:T(8,128)}) %reduce-scatter.8.cloned.1.call-update) | async-done | bytes 524304 | tf_op jit(solution)/shard_map/reduce_scatter | solution.py:464
  347.7 21.4 %psum.31 = f32[2,4,128]{2,0,1:T(2,128)S(1)} all-reduce(f32[2,4,128]{2,0,1:T(2,128)S(1)} %pad_maximum_fusion.6), channel_id=1, replica_groups=mesh['nodes'=8,'heads'=4] {'nodes'}, use_global_device_ids=true, to_apply=%region_23.24 | all-reduce | flops 1024 | bytes 8192 | tf_op jit(solution)/shard_map/psum | solution.py:483
  369.1 3.1 divide_subtract_fusion
  372.2 2.1 copy.115
  374.3 2.2 copy.114
  380.9 14.9 %all-reduce = (f32[1024]{0:T(1024)S(1)}, f32[1024,1]{0,1:T(1,128)S(1)}) all-reduce(f32[1024]{0:T(1024)S(1)} %get-tuple-element.87, f32[1024,1]{0,1:T(1,128)S(1)} %bitcast.386), channel_id=1, replica_groups=mesh['nodes'=8,'heads'=4] {'heads'}, use_global_device_ids=true, to_apply=%region_13.14 | all-reduce | flops 2048 | bytes 16384 | tf_op jit(solution)/shard_map/psum | solution.py:471
  396.5 2.6 multiply_add_fusion.2
  402.2 16.8 %all-gather.3.cloned.1.call-done = bf16[2048,1536]{1,0:T(8,128)(2,1)} async-done(((bf16[64,1536]{1,0:T(8,128)(2,1)}), bf16[2048,1536]{1,0:T(8,128)(2,1)}) %all-gather.3.cloned.1.call-update) | async-done | bytes 6291472 | tf_op jit(solution)/shard_map/all_gather | solution.py:505
  419.1 3.5 copy.101
  425.3 2.5 fusion.88
  427.8 2.2 bitcast_convert_fusion
  444.0 3.0 fusion.114
  447.0 2.8 fusion.108
  450.6 2.9 fusion.35
  461.1 3.3 fusion.101
  464.4 2.8 fusion.95
  467.9 3.5 fusion.17
  471.4 1.9 fusion.16
  479.0 2.9 fusion.140
  481.9 3.0 fusion.134
  485.7 3.5 fusion.23
  489.2 1.9 fusion.22
  496.8 2.8 fusion.127
  499.6 3.2 fusion.121
  502.9 2.1 copy.103
  504.9 2.6 copy.102
  507.5 4.2 copy.104
  511.7 4.1 copy.105
  515.8 3.4 fusion.109
  530.5 2.0 fusion.116
  543.9 2.1 fusion.98
  557.3 2.3 fusion.14
  570.9 2.0 fusion.139
  584.3 2.3 fusion.19
  597.1 2.0 fusion.143
  601.1 3.6 fusion.131
  604.7 3.6 fusion.144
  610.3 2.7 fusion.105
  (248 shorter events, 159.0 us)
Async XLA Ops:
  7.2 0.8 copy-start
  7.2 131.1 %all-reduce.3.cloned.1.call-start = ((), (), s32[]{:S(2)}) async-start(), calls=%async_computation.4 | async-start | bytes 4194304 | tf_op jit(solution)/shard_map/psum | solution.py:428
  76.1 1.4 copy-start.37
  77.5 2.8 copy-start.4
  77.5 2.0 copy-start.31
  78.4 5.8 copy-start.21
  81.2 1.3 copy-start.6
  81.2 2.2 copy-start.32
  82.5 55.8 %copy-start.3 = (f32[1024,512]{1,0:T(8,128)}, f32[1024,512]{1,0:T(8,128)S(1)}, u32[]{:S(2)}) copy-start(f32[1024,512]{1,0:T(8,128)S(1)} %get-tuple-element.109) | copy-start | bytes 6291460
  84.1 1.4 copy-start.27
  85.5 1.0 copy-start.34
  88.7 190.4 %reduce-scatter.10.cloned.1.call-start = ((), (), s32[]{:S(2)}) async-start(), calls=%async_computation.7 | async-start | bytes 3538944
  89.0 3.4 copy-start.33
  92.4 1.6 copy-start.35
  94.0 1.8 copy-start.22
  94.0 2.3 copy-start.28
  138.3 2.2 copy-start.7
  138.3 2.5 copy-start.23
  140.8 3.8 copy-start.24
  144.7 1.8 copy-start.25
  146.5 3.7 copy-start.55
  169.0 5.3 copy-start.40
  170.0 25.1 %collective-permute-start = (bf16[2,512,256]{2,1,0:T(8,128)(2,1)}, bf16[2,512,256]{2,1,0:T(8,128)(2,1)}, u32[]{:S(2)}, u32[]{:S(2)}) collective-permute-start(bf16[2,512,256]{2,1,0:T(8,128)(2,1)} %get-tuple-element.114), channel_id=1, source_target_pairs={{4,0},{8,4},{12,8},{16,12},{20,16},{24,20},{28,24},{0,28},{5,1},{9... | collective-permute-start | bytes 1572872 | tf_op jit(solution)/shard_map/ppermute | solution.py:456
  174.2 20.9 %collective-permute-start.1 = (bf16[2,512,256]{2,1,0:T(8,128)(2,1)}, bf16[2,512,256]{2,1,0:T(8,128)(2,1)}, u32[]{:S(2)}, u32[]{:S(2)}) collective-permute-start(bf16[2,512,256]{2,1,0:T(8,128)(2,1)} %get-tuple-element.115), channel_id=1, source_target_pairs={{0,4},{4,8},{8,12},{12,16},{16,20},{20,24},{24,28},{28,0},{1,5},{5... | collective-permute-start | bytes 1572872 | tf_op jit(solution)/shard_map/ppermute | solution.py:457
  182.5 14.4 %copy-start.36 = (bf16[1,2,512,512]{3,2,1,0:T(8,128)(2,1)S(1)}, bf16[1,2,512,512]{3,2,1,0:T(8,128)(2,1)}, u32[]{:S(2)}) copy-start(bf16[1,2,512,512]{3,2,1,0:T(8,128)(2,1)} %slice.81) | copy-start | bytes 3145732
  196.8 1.2 copy-start.38
  196.8 1.5 copy-start.39
  203.9 108.3 %reduce-scatter.6.cloned.1.call-start = ((), (), s32[]{:S(2)}) async-start(), calls=%async_computation.3 | async-start | bytes 2621440 | tf_op jit(solution)/shard_map/reduce_scatter | solution.py:419
  207.8 3.3 copy-start.51
  207.8 3.4 copy-start.50
  207.8 4.2 copy-start.47
  207.8 138.3 %reduce-scatter.8.cloned.1.call-start = ((), (), s32[]{:S(2)}) async-start(), calls=%async_computation.5 | async-start | bytes 2621440 | tf_op jit(solution)/shard_map/reduce_scatter | solution.py:464
  211.0 1.8 copy-start.48
  211.1 208.0 %all-gather.3.cloned.1.call-start = ((), (), s32[]{:S(2)}) async-start(), calls=%async_computation.6 | async-start | bytes 6488064 | tf_op jit(solution)/shard_map/all_gather | solution.py:505
  213.7 70.7 %copy-start.30 = (f32[4,256,128]{2,1,0:T(8,128)S(1)}, f32[4,256,128]{2,1,0:T(8,128)}, u32[]{:S(2)}) copy-start(f32[4,256,128]{2,1,0:T(8,128)} %param.32) | copy-start | bytes 1572868
  288.8 4.2 copy-start.20
  293.4 75.7 %copy-start.41 = (f32[4,256,128]{1,2,0:T(8,128)S(1)}, f32[4,256,128]{1,2,0:T(8,128)}, u32[]{:S(2)}) copy-start(f32[4,256,128]{1,2,0:T(8,128)} %copy.108) | copy-start | bytes 1572868
  293.4 75.7 %copy-start.42 = (f32[4,256,128]{1,2,0:T(8,128)S(1)}, f32[4,256,128]{1,2,0:T(8,128)}, u32[]{:S(2)}) copy-start(f32[4,256,128]{1,2,0:T(8,128)} %copy.106) | copy-start | bytes 1572868
  372.2 4.3 copy-start.43
  374.3 4.8 copy-start.12
  377.5 18.4 %copy-start.52 = (f32[4,128]{1,0:T(4,128)S(1)}, f32[4,128]{1,0:T(4,128)}, u32[]{:S(2)}) copy-start(f32[4,128]{1,0:T(4,128)} %param.33) | copy-start | bytes 6148
  377.5 18.4 %copy-start.53 = (f32[4,128]{1,0:T(4,128)S(1)}, f32[4,128]{1,0:T(4,128)}, u32[]{:S(2)}) copy-start(f32[4,128]{1,0:T(4,128)} %param.37) | copy-start | bytes 6148
  377.5 18.4 %copy-start.54 = (f32[4,128]{1,0:T(4,128)S(1)}, f32[4,128]{1,0:T(4,128)}, u32[]{:S(2)}) copy-start(f32[4,128]{1,0:T(4,128)} %param.36) | copy-start | bytes 6148
  377.8 1.4 copy-start.11
  379.2 20.0 %copy-start.26 = (f32[64,1536]{0,1:T(8,128)S(1)}, f32[64,1536]{0,1:T(8,128)}, u32[]{:S(2)}) copy-start(f32[64,1536]{0,1:T(8,128)} %get-tuple-element.107) | copy-start | bytes 1179652
  422.5 5.3 copy-start.2
  444.0 3.0 copy-start.5
  521.1 1.9 copy-start.16
  534.4 1.9 copy-start.18
  540.2 1.9 copy-start.14
  553.5 1.9 copy-start.17
  559.7 1.9 copy-start.13
  573.0 1.9 copy-start.19
  578.7 1.9 copy-start.15
  594.2 1.9 copy-start.29
  599.2 1.9 copy-start.9
  601.1 3.6 copy-start.8
  608.3 1.9 copy-start.10
  610.2 2.8 copy-start.44
  610.2 2.8 copy-start.45
  610.3 2.8 copy-start.46
  610.3 2.8 copy-start.49
  610.3 4.9 copy-start.1
Sparse Core Ops, SparseCore 0:
  88.8 49.4 all-reduce.2
  204.1 74.9 reduce-scatter.9
  281.7 30.4 reduce-scatter.5
  314.7 31.4 reduce-scatter.7
  349.2 69.7 all-gather.2

commit v2 on v1

--- a/solution.py
+++ b/solution.py
@@ -38,7 +38,7 @@
 class Links:
     def __init__(self, send_sems, recv_sems):
         self.send_sems, self.recv_sems = send_sems, recv_sems
-        self.copies = []
+        self.copies, self.finished = [], []
 
     def send(self, source, target, device):
         slot = len(self.copies)
@@ -54,9 +54,14 @@
         self.copies.append(copy)
         return copy
 
+    def finish(self, copy):
+        copy.wait_send()
+        self.finished.append(copy)
+
     def close(self):
         for copy in self.copies:
-            copy.wait_send()
+            if not any(copy is other for other in self.finished):
+                copy.wait_send()
 
 
 def meet(devices):
@@ -273,6 +278,613 @@
     links.close()
 
 
+def update_kernel(
+    patch_count,
+    own_gather,
+    sizes_ref,
+    state_all,
+    cot_all,
+    mod_all,
+    a_one,
+    queries,
+    key_value,
+    prob_low,
+    mixed_all,
+    weight_all,
+    output_all,
+    moment_ref,
+    weight_ref,
+    layer_output,
+    input_grad,
+    moment_new,
+    weight_new,
+    mod_sum,
+    hidden_one,
+    a_two,
+    act,
+    grad_up,
+    part_two,
+    part_core,
+    part_low,
+    part_across,
+    total_two,
+    out_low,
+    out_core,
+    out_keep,
+    out_across,
+    grad_hidden,
+    grad_attn,
+    grad_mixed,
+    score_low,
+    grad_own,
+    grad_away,
+    grad_back,
+    grad_projected,
+    mod_part,
+    mod_in,
+    grad_cat,
+    grad_low,
+    grad_core,
+    grad_line,
+    moment_low,
+    matrix,
+    gram_left,
+    gram_right,
+    factor_left,
+    chain,
+    turn_right,
+    ortho_out,
+    ortho_in,
+    send_sems,
+    recv_sems,
+    turn_send,
+    turn_recv,
+):
+    node, head = lax.axis_index("nodes"), lax.axis_index("heads")
+    after, before = lax.rem(node + 1, patch_count), lax.rem(node + patch_count - 1, patch_count)
+    across, sibling = lax.rem(head + 2, 4), head + 1 - 2 * lax.rem(head, 2)
+    to_across, to_sibling = (node, across), (node, sibling)
+    to_after, to_before = (after, head), (before, head)
+    side, core = lax.div(head, 2), lax.rem(head, 2)
+    plane, parity = lax.div(node, 2), lax.rem(node, 2)
+    to_partner = (node + 1 - 2 * parity, head)
+    met = [to_across, to_sibling]
+    if own_gather:
+        met += [(lax.rem(node + k, patch_count), head) for k in range(1, patch_count)]
+    else:
+        met += [to_after, to_before]
+    meet(met)
+    links = Links(send_sems, recv_sems)
+    micro_count, capacity, head_dim = queries.shape
+    full_width = a_one.shape[-1]
+    total = 3 * capacity
+    hidden = act.shape[-1]
+    inv_head = head_dim ** (-0.5)
+    cuts = (0, 3 * head_dim, 4 * head_dim, 4 * head_dim + hidden, 4 * head_dim + 2 * hidden)
+    expand_columns, contract_columns = slice(cuts[2], cuts[3]), slice(cuts[3], cuts[4])
+    tile = capacity // 2
+
+    def weight(columns):
+        return weight_all[:, :, columns].reshape(full_width, columns.stop - columns.start)
+
+    def live_rows(batch, start, count):
+        slots = lax.broadcasted_iota(jnp.int32, (count, 1), 0) + start
+        return (slots < sizes_ref[batch, 0]).astype(F32)
+
+    def rows_at(step, count):
+        start = step * count if isinstance(step, int) else pl.multiple_of(step * count, count)
+        return start, pl.ds(start, count)
+
+    def feed_forward(batch, step):
+        start, rows = rows_at(step, tile)
+        mixed = wide(mixed_all, batch, rows, slice(None))
+        mixer = jnp.concatenate(
+            [output_all[k].reshape(full_width, head_dim) for k in range(output_all.shape[0])], axis=-1
+        )
+        hid = wide(state_all, batch, rows, slice(None)).astype(F32) + mul(mixed, mixer, NT)
+        hidden_one[batch, rows, :] = hid
+        normed, _ = norm_rows(hid)
+        a_rows = (normed * (1.0 + mod_row(mod_all, batch, 3)) + mod_row(mod_all, batch, 2)).astype(BF16)
+        a_two[batch, rows, :] = a_rows
+        up = mul(a_rows, weight(expand_columns))
+        gate = jax.nn.sigmoid(up)
+        acted = (up * gate).astype(BF16)
+        act[batch, rows, :] = acted
+        live = live_rows(batch, start, tile)
+        cot = (wide(cot_all, batch, rows, slice(None)).astype(F32) * live).astype(BF16)
+        grad_act = mul(cot, weight(contract_columns))
+        grad_rows = (grad_act * gate * (1.0 + up * (1.0 - gate))).astype(BF16)
+        grad_up[batch, rows, :] = grad_rows
+        back = mul(grad_rows, weight(expand_columns), NT)
+        out = mul(acted, weight(contract_columns), NT)
+        for k in range(4):
+            block = slice(k * head_dim, (k + 1) * head_dim)
+            part_two[batch, k % 2, k // 2, rows, :] = back[:, block]
+            out_low[batch, k % 2, k // 2, rows, :] = out[:, block].astype(BF16)
+
+    def to_core(batch):
+        return links.send(part_two.at[batch, 1 - core], part_core.at[batch], to_sibling)
+
+    def to_side(batch, copy):
+        copy.wait_recv()
+        for k in range(2):
+            chip = part_two[batch, core, k] + part_core[batch, k]
+            part_core[batch, k] = chip
+            part_low[batch, k] = chip.astype(BF16)
+        return links.send(part_low.at[batch], part_across.at[batch], to_across)
+
+    def to_all(batch, copy):
+        copy.wait_recv()
+        for k in range(2):
+            total_two[batch, core, k] = part_core[batch, k] + part_across[batch, k].astype(F32)
+        return links.send(total_two.at[batch, core], total_two.at[batch, core], to_sibling)
+
+    def total_rows(batch, rows):
+        return jnp.concatenate(
+            [total_two[batch, k % 2, k // 2, rows, :] for k in range(4)], axis=-1
+        )
+
+    def back_norm(grad, normed, root):
+        mean_grad = jnp.sum(grad, axis=-1, keepdims=True) / full_width
+        mean_cross = jnp.sum(grad * normed, axis=-1, keepdims=True) / full_width
+        return root * (grad - mean_grad - normed * mean_cross)
+
+    def add_mod(batch, number, values):
+        sums = jnp.sum(values, axis=0, keepdims=True)
+        place = batch * 4 + number
+        for k in range(4):
+            mod_part[k, place : place + 1, :] += sums[:, k * head_dim : (k + 1) * head_dim]
+
+    for k in range(4):
+        mod_part[k] = jnp.zeros(mod_part.shape[1:], F32)
+
+    pl.loop(0, 2)(lambda step: feed_forward(0, step))
+    core_first = to_core(0)
+    feed_forward(1, 0)
+    side_first = to_side(0, core_first)
+    feed_forward(1, 1)
+    core_second = to_core(1)
+
+    def store_grad(step, columns, value):
+        half = full_width // 8
+        for k in range(2):
+            part = value[k * half : (k + 1) * half]
+            grad_cat[k, step, :, columns] = part
+            grad_low[k, step, :, columns] = part.astype(BF16)
+
+    def both(ref, columns):
+        return ref[:, :, columns].reshape(micro_count * capacity, -1)
+
+    def live_cot(batch, columns):
+        return (cot_all[columns, batch].astype(F32) * live_rows(batch, 0, capacity)).astype(BF16)
+
+    @pl.loop(0, 4)
+    def _(step):
+        columns = pl.ds(pl.multiple_of(step * head_dim, head_dim), head_dim)
+        store_grad(step, expand_columns, mul(both(a_two, columns), grad_up[...].reshape(-1, hidden), TN))
+        cot = jnp.concatenate([live_cot(b, step) for b in range(micro_count)], axis=0)
+        store_grad(step, contract_columns, mul(cot, act[...].reshape(-1, hidden), TN))
+
+    early, late = slice(cuts[2], cuts[4]), slice(0, cuts[2])
+
+    def grad_pair(columns):
+        return links.send(
+            grad_low.at[1 - parity, :, :, columns], grad_core.at[:, :, columns], to_partner
+        )
+
+    def grad_planes(copy, columns):
+        copy.wait_recv()
+        for k in range(4):
+            summed = grad_cat[parity, k, :, columns] + grad_core[k, :, columns].astype(F32)
+            grad_cat[parity, k, :, columns] = summed
+            grad_low[parity, k, :, columns] = summed.astype(BF16)
+        sent = []
+        for k in range(1, 4):
+            target = lax.rem(plane + k, 4)
+            sent.append(
+                links.send(
+                    grad_low.at[parity, target, :, columns],
+                    grad_line.at[k - 1, :, columns],
+                    (2 * target + parity, head),
+                )
+            )
+        return sent
+
+    def grad_finish(copies, columns):
+        for copy in copies:
+            copy.wait_recv()
+        summed = grad_cat[parity, plane, :, columns]
+        for k in range(3):
+            summed = summed + grad_line[k, :, columns].astype(F32)
+        moment_new[:, columns] = MOMENTUM_DECAY * moment_ref[:, columns] + summed
+
+    if own_gather:
+        early_pair = grad_pair(early)
+    side_second = to_side(1, core_second)
+    all_first = to_all(0, side_first)
+    out_copies = [
+        links.send(out_low.at[b, 1 - core], out_core.at[b], to_sibling) for b in range(micro_count)
+    ]
+
+    def norm_two_back(batch):
+        @pl.loop(0, capacity // tile)
+        def _(step):
+            start, rows = rows_at(step, tile)
+            normed, root = norm_rows(hidden_one[batch, rows, :])
+            grad = total_rows(batch, rows)
+            add_mod(batch, 2, grad)
+            add_mod(batch, 3, grad * normed)
+            cot = wide(cot_all, batch, rows, slice(None)).astype(F32) * live_rows(batch, start, tile)
+            grad = cot + back_norm(grad * (1.0 + mod_row(mod_all, batch, 3)), normed, root)
+            for k in range(4):
+                grad_hidden[k, batch, rows, :] = grad[:, k * head_dim : (k + 1) * head_dim]
+            low = grad.astype(BF16)
+            grad_attn[batch, rows, :] = low
+            grad_mixed[batch, rows, :] = mul(low, weight(slice(cuts[1], cuts[2]))).astype(BF16)
+
+    def attend_back(batch):
+        attend_rows = 128
+
+        @pl.loop(0, capacity // attend_rows)
+        def _(step):
+            _, rows = rows_at(step, attend_rows)
+            keys = key_value[batch, :, :, :head_dim].reshape(total, head_dim)
+            values = key_value[batch, :, :, head_dim:].reshape(total, head_dim)
+            prob = prob_low[batch, rows, :].astype(F32)
+            grad_prob = mul(grad_mixed[batch, rows, :], values, NT)
+            mean = jnp.sum(prob * grad_prob, axis=-1, keepdims=True)
+            score = (prob * (grad_prob - mean) * inv_head).astype(BF16)
+            score_low[rows, :] = score
+            grad_projected[batch, rows, :head_dim] = mul(score, keys).astype(BF16)
+
+        for patch in range(3):
+            slots = slice(patch * capacity, (patch + 1) * capacity)
+            grad_key = mul(score_low[:, slots], queries[batch], TN)
+            grad_value = mul(prob_low[batch, :, slots], grad_mixed[batch], TN)
+            if patch == 1:
+                grad_own[batch, :, :head_dim] = grad_key
+                grad_own[batch, :, head_dim:] = grad_value
+            else:
+                grad_away[batch, patch // 2, :, :head_dim] = grad_key.astype(BF16)
+                grad_away[batch, patch // 2, :, head_dim:] = grad_value.astype(BF16)
+
+    def send_back(batch):
+        return [
+            links.send(grad_away.at[batch, 0], grad_back.at[batch, 1], to_before),
+            links.send(grad_away.at[batch, 1], grad_back.at[batch, 0], to_after),
+        ]
+
+    all_first.wait_recv()
+    norm_two_back(0)
+    attend_back(0)
+    back_first = send_back(0)
+    all_second = to_all(1, side_second)
+    if own_gather:
+        early_line = grad_planes(early_pair, early)
+    out_across_copies = []
+    for batch in range(micro_count):
+        out_copies[batch].wait_recv()
+        for k in range(2):
+            chip = out_low[batch, core, k].astype(F32) + out_core[batch, k].astype(F32)
+            out_keep[batch, k] = chip
+            out_core[batch, k] = chip.astype(BF16)
+        out_across_copies.append(
+            links.send(out_core.at[batch, 1 - side], out_across.at[batch], to_across)
+        )
+    all_second.wait_recv()
+    norm_two_back(1)
+    attend_back(1)
+
+    @pl.loop(0, 4)
+    def _(step):
+        columns = pl.ds(pl.multiple_of(step * head_dim, head_dim), head_dim)
+        queries_part = mul(both(a_one.at[1], columns), both(grad_projected, slice(0, head_dim)), TN)
+        store_grad(step, slice(0, head_dim), queries_part)
+        rest = mul(both(a_one.at[1], columns), grad_own[...].reshape(-1, 2 * head_dim).astype(BF16), TN)
+        for patch in (0, 2):
+            away = grad_away[:, patch // 2].reshape(-1, 2 * head_dim)
+            rest = rest + mul(both(a_one.at[patch], columns), away, TN)
+        store_grad(step, slice(head_dim, cuts[1]), rest)
+        own_mixed = mixed_all[head].reshape(-1, head_dim)
+        store_grad(step, slice(cuts[1], cuts[2]), mul(both(grad_attn, columns), own_mixed, TN))
+
+    if own_gather:
+        late_pair = grad_pair(late)
+    back_second = send_back(1)
+    if own_gather:
+        grad_finish(early_line, early)
+        late_line = grad_planes(late_pair, late)
+    for batch in range(micro_count):
+        out_across_copies[batch].wait_recv()
+        own = hidden_one[batch, :, pl.ds(pl.multiple_of(head * head_dim, head_dim), head_dim)]
+        result = own + out_keep[batch, side] + out_across[batch].astype(F32)
+        layer_output[batch] = (result * live_rows(batch, 0, capacity)).astype(BF16)
+
+    def turn(source, target, device, send_slot, recv_slot):
+        return pltpu.make_async_remote_copy(
+            src_ref=source,
+            dst_ref=target,
+            send_sem=turn_send.at[send_slot],
+            recv_sem=turn_recv.at[recv_slot],
+            device_id=device,
+            device_id_type=MESH,
+        )
+
+    widths = (3 * head_dim, head_dim, hidden, hidden)
+
+    def to_owner(number):
+        columns = slice(cuts[number], cuts[number + 1])
+        return turn(
+            moment_low.at[:, columns],
+            matrix.at[head, parity, plane, :, : widths[number]],
+            (2 * number + parity, head),
+            number,
+            plane,
+        )
+
+    if own_gather:
+        grad_finish(late_line, late)
+        moment_low[...] = moment_new[...].astype(BF16)
+        for number in range(4):
+            columns = slice(cuts[number], cuts[number + 1])
+
+            @pl.when(plane != number)
+            def _():
+                to_owner(number).start()
+
+            @pl.when(plane == number)
+            def _():
+                matrix[head, parity, plane, :, : widths[number]] = moment_low[:, columns]
+
+        for number in range(4):
+
+            @pl.when(plane == number)
+            def _():
+                for other in range(4):
+                    if other != number:
+                        turn(
+                            moment_low.at[:, slice(cuts[number], cuts[number + 1])],
+                            matrix.at[head, parity, other, :, : widths[number]],
+                            (2 * number + parity, head),
+                            number,
+                            other,
+                        ).wait_recv()
+
+            @pl.when(plane != number)
+            def _():
+                to_owner(number).wait_send()
+
+        def gather_plane(width):
+            sends = []
+
+            def give(block, pair, device):
+                slot = 4 + len(sends)
+                part = matrix.at[block, pair, :, :, :width]
+                copy = turn(part, part, device, slot, slot)
+                copy.start()
+                sends.append(copy)
+                return copy
+
+            mirror = 1 - parity
+            first_across = give(head, parity, to_across)
+            first_partner = give(head, parity, to_partner)
+            waits = [give(head, parity, to_sibling)]
+            first_across.wait_recv()
+            waits.append(give(across, parity, to_partner))
+            waits.append(give(across, parity, to_sibling))
+            first_partner.wait_recv()
+            waits.append(give(head, mirror, to_sibling))
+            waits[1].wait_recv()
+            waits.append(give(across, mirror, to_sibling))
+            for copy in waits[:1] + waits[2:]:
+                copy.wait_recv()
+            for copy in sends:
+                copy.wait_send()
+            half = full_width // 2
+
+            @pl.loop(0, 2)
+            def _(step):
+                _, rows = rows_at(step, half)
+                gram = jnp.zeros((half, full_width), F32)
+                for k in range(4):
+                    left = matrix[k, step, :, :, :width].reshape(half, width)
+                    right = matrix[k, :, :, :, :width].reshape(full_width, width)
+                    gram = gram + mul(left, right, NT)
+                chain[rows, :] = gram
+
+        for low, high, width in ((0, 1, widths[0]), (1, 2, widths[1]), (2, 4, hidden)):
+
+            @pl.when((plane >= low) & (plane < high))
+            def _():
+                gather_plane(width)
+
+        half = full_width // 2
+        wide_shape = (half, full_width)
+
+        def split(value):
+            high = value.astype(BF16)
+            return high, (value - high.astype(F32)).astype(BF16)
+
+        def put_left(ref, rows, value):
+            high, low = split(value)
+            ref[rows, :full_width] = high
+            ref[rows, full_width : 2 * full_width] = high
+            ref[rows, 2 * full_width :] = low
+
+        def put_right(ref, rows, value):
+            high, low = split(value)
+            ref[0, rows, :] = high
+            ref[1, rows, :] = low
+            ref[2, rows, :] = high
+
+        def times(left, rows, right):
+            return mul(left[rows, :], right[...].reshape(3 * full_width, full_width))
+
+        def diagonal(start):
+            rows = lax.broadcasted_iota(jnp.int32, wide_shape, 0) + start
+            return rows == lax.broadcasted_iota(jnp.int32, wide_shape, 1)
+
+        trace = jnp.zeros((1, 1), F32)
+        for step in range(2):
+            rows = slice(step * half, (step + 1) * half)
+            kept = jnp.where(diagonal(step * half), chain[rows, :], 0.0)
+            trace = trace + jnp.sum(jnp.sum(kept, axis=1, keepdims=True), axis=0, keepdims=True)
+        scale = 1.0 / (jnp.sqrt(trace) + 1e-07)
+
+        @pl.loop(0, 2)
+        def _(step):
+            _, rows = rows_at(step, half)
+            gram = chain[rows, :] * (scale * scale)
+            chain[rows, :] = gram
+            put_left(gram_left, rows, gram)
+            put_right(gram_right, rows, gram)
+
+        def polynomial(repeat):
+            @pl.loop(0, 2)
+            def _(step):
+                start, rows = rows_at(step, half)
+                gram = chain[rows, :]
+                factor = NEWTON_B * gram + NEWTON_C * times(gram_left, rows, gram_right)
+                factor = factor + jnp.where(diagonal(start), NEWTON_A, 0.0)
+                put_left(factor_left, rows, factor)
+
+        done = 0
+        for repeat in range(NS_STEPS):
+            polynomial(repeat)
+            if repeat == 0:
+
+                @pl.loop(0, 2)
+                def _(step):
+                    _, rows = rows_at(step, half)
+                    high, low = factor_left[rows, :full_width], factor_left[rows, 2 * full_width :]
+                    turn_right[0, 0, rows, :] = high
+                    turn_right[0, 1, rows, :] = low
+                    turn_right[0, 2, rows, :] = high
+
+            else:
+
+                @pl.loop(0, 2)
+                def _(step):
+                    _, rows = rows_at(step, half)
+                    product = times(factor_left, rows, turn_right.at[done])
+                    put_right(turn_right.at[2 - done], rows, product)
+
+                done = 2 - done
+
+            if repeat < NS_STEPS - 1:
+
+                @pl.loop(0, 2)
+                def _(step):
+                    _, rows = rows_at(step, half)
+                    put_right(turn_right.at[1], rows, times(factor_left, rows, gram_right))
+
+                @pl.loop(0, 2)
+                def _(step):
+                    _, rows = rows_at(step, half)
+                    gram = times(factor_left, rows, turn_right.at[1])
+                    chain[rows, :] = gram
+                    put_left(gram_left, rows, gram)
+                    put_right(gram_right, rows, gram)
+
+        def spread_ortho(number):
+            width = widths[number]
+            left = jnp.concatenate(
+                [turn_right[done, k, pl.ds(pl.multiple_of(parity * half, half), half), :] for k in range(2)], axis=-1
+            )
+            right = matrix[head, :, :, :, :width].reshape(full_width, width)
+            right = jnp.concatenate([right, right], axis=0)
+            value = (mul(left, right) * scale).astype(BF16)
+            ortho_out[:, :, :width] = value.reshape(4, half // 4, width)
+            ortho_in[number, :, :width] = ortho_out[plane, :, :width]
+            for k in range(1, 4):
+                ortho_copy(number, k).start()
+
+        def ortho_copy(number, k):
+            target = (number + k) % 4
+            width = widths[number]
+            return turn(
+                ortho_out.at[target, :, :width],
+                ortho_in.at[number, :, :width],
+                (2 * target + parity, head),
+                12 + k,
+                12 + number,
+            )
+
+        for number in range(4):
+
+            @pl.when(plane == number)
+            def _():
+                spread_ortho(number)
+
+    for copy in (core_first, core_second, side_first, side_second, all_first, all_second):
+        links.finish(copy)
+    for batch, copies in enumerate((back_first, back_second)):
+        for copy in copies:
+            copy.wait_recv()
+        whole = grad_own[batch] + grad_back[batch, 0].astype(F32) + grad_back[batch, 1].astype(F32)
+        grad_projected[batch, :, head_dim:] = whole.astype(BF16)
+
+        @pl.loop(0, capacity // tile)
+        def _(step):
+            _, rows = rows_at(step, tile)
+            back = mul(grad_projected[batch, rows, :], weight(slice(0, cuts[1])), NT)
+            for k in range(4):
+                part_two[batch, k % 2, k // 2, rows, :] = back[:, k * head_dim : (k + 1) * head_dim]
+
+    one_core = [to_core(b) for b in range(micro_count)]
+    one_side = [to_side(b, one_core[b]) for b in range(micro_count)]
+    one_all = [to_all(b, one_side[b]) for b in range(micro_count)]
+    for batch in range(micro_count):
+        one_all[batch].wait_recv()
+
+        @pl.loop(0, capacity // tile)
+        def _(step):
+            _, rows = rows_at(step, tile)
+            normed, root = norm_rows(wide(state_all, batch, rows, slice(None)).astype(F32))
+            grad = total_rows(batch, rows)
+            add_mod(batch, 0, grad)
+            add_mod(batch, 1, grad * normed)
+            grad = back_norm(grad * (1.0 + mod_row(mod_all, batch, 1)), normed, root)
+            own = jnp.zeros((tile, head_dim), F32)
+            for k in range(4):
+                own = own + jnp.where(head == k, grad[:, k * head_dim : (k + 1) * head_dim], 0.0)
+            input_grad[batch, rows, :] = own + grad_hidden[head, batch, rows, :]
+
+    if own_gather:
+        mod_copies = [
+            links.send(mod_part.at[head], mod_in.at[k - 1], (lax.rem(node + k, patch_count), head))
+            for k in range(1, patch_count)
+        ]
+        for number in range(4):
+
+            @pl.when(plane != number)
+            def _():
+                ortho_copy(number, 1).wait_recv()
+
+            columns = slice(cuts[number], cuts[number + 1])
+            factor = (4.0 * hidden / full_width) ** 0.5 if number == 3 else 1.0
+            weight_new[:, columns] = weight_ref[:, columns] * (1.0 - LR_MUON * DECAY_WEIGHT) - (
+                LR_MUON * factor
+            ) * ortho_in[number, :, : widths[number]].astype(F32)
+
+            @pl.when(plane == number)
+            def _():
+                for k in range(1, 4):
+                    ortho_copy(number, k).wait_send()
+
+        summed = mod_part[head]
+        for copy in mod_copies:
+            copy.wait_recv()
+        for k in range(patch_count - 1):
+            summed = summed + mod_in[k]
+        mod_sum[...] = summed
+    else:
+        mod_sum[...] = mod_part[head]
+        for k in range(8):
+            moment_new[k] = grad_cat[k % 2, k // 2]
+    links.close()
+
+
 def adam_step(weight, first_old, second_old, gradient):
     first_new = BETA_FIRST * first_old + (1.0 - BETA_FIRST) * gradient
     second_new = BETA_SECOND * second_old + (1.0 - BETA_SECOND) * gradient * gradient
@@ -389,145 +1001,146 @@
         output_all = lax.all_gather(
             low_cat[:, :, 3 * head_dim : 4 * head_dim], "heads", axis=0, tiled=False
         )
-    weight_full = weight_all.reshape(full_width, weight_width)
-    w_proj_low, w_out_low, w_exp_low, w_con_low = jnp.split(
-        weight_full, (3 * head_dim, 4 * head_dim, 4 * head_dim + hidden), axis=1
-    )
-    output_full = output_all.reshape(head_count, full_width, head_dim).transpose(1, 0, 2).reshape(full_width, full_width)
-
-    def rows_of(blocks):
-        return blocks.transpose(1, 2, 0, 3).reshape(micro_count * capacity, full_width)
-
-    def own_columns(rows):
-        return lax.dynamic_slice_in_dim(rows, head_index * share, share, axis=1)
-
-    def per_batch(number):
-        terms = mod_all.reshape(head_count, micro_count, 4, share)[:, :, number].transpose(1, 0, 2)
-        return jnp.repeat(terms.reshape(micro_count, full_width), capacity, axis=0)
-
-    slot_ids = lax.broadcasted_iota(jnp.int32, (micro_count, capacity), 1)
-    live = (slot_ids < patch_sizes).astype(F32).reshape(micro_count * capacity, 1)
-    state = rows_of(state_all).astype(F32)
-    mixed = rows_of(mixed_all)
-    hidden_one = state + mul(mixed, output_full, NT)
-    norm_two, root_two = norm_rows(hidden_one)
-    scale_two = 1.0 + per_batch(3)
-    a_two = (norm_two * scale_two + per_batch(2)).astype(BF16)
-    up = mul(a_two, w_exp_low)
-    gate = jax.nn.sigmoid(up)
-    act = (up * gate).astype(BF16)
-    result = own_columns(hidden_one) + lax.psum_scatter(
-        mul(act, w_con_low, NT), "heads", scatter_dimension=1, tiled=True
-    )
-    layer_output = (result * live).astype(BF16).reshape(micro_count, capacity, share)
-    cot = rows_of(cot_all) * live.astype(BF16)
-    grad_act = mul(cot, w_con_low)
-    grad_contract = mul(cot, act, TN)
-    grad_up = (grad_act * gate * (1.0 + up * (1.0 - gate))).astype(BF16)
-    grad_expand = mul(a_two, grad_up, TN)
-    grad_two = lax.psum(mul(grad_up, w_exp_low, NT), "heads")
-
-    def norm_back(grad, normed, root):
-        mean_grad = jnp.sum(grad, axis=-1, keepdims=True) / full_width
-        mean_cross = jnp.sum(grad * normed, axis=-1, keepdims=True) / full_width
-        return root * (grad - mean_grad - normed * mean_cross)
-
-    grad_hidden = cot.astype(F32) + norm_back(grad_two * scale_two, norm_two, root_two)
-    grad_attn = grad_hidden.astype(BF16)
-    grad_mixed = mul(grad_attn, w_out_low).astype(BF16).reshape(micro_count, capacity, head_dim)
-    own_mixed = lax.dynamic_index_in_dim(mixed_all, head_index, 0, keepdims=False)
-    grad_output = mul(grad_attn, own_mixed.reshape(-1, head_dim), TN)
-    keys = key_value[..., :head_dim].reshape(micro_count, 3 * capacity, head_dim)
-    values = key_value[..., head_dim:].reshape(micro_count, 3 * capacity, head_dim)
-    grad_prob = jnp.einsum("brd,bmd->brm", grad_mixed, values, preferred_element_type=F32)
-    prob = prob_low.astype(F32)
-    grad_score = prob * (grad_prob - jnp.sum(prob * grad_prob, axis=-1, keepdims=True))
-    grad_score = (grad_score * inv_head).astype(BF16)
-    grad_query = jnp.einsum("brm,bmd->brd", grad_score, keys, preferred_element_type=F32)
-    grad_keys = jnp.einsum("brm,brd->bmd", grad_score, queries, preferred_element_type=F32)
-    grad_values = jnp.einsum("brm,brd->bmd", prob_low, grad_mixed, preferred_element_type=F32)
-    grad_ext = jnp.concatenate([grad_keys, grad_values], axis=-1).reshape(
-        micro_count, 3, capacity, 2 * head_dim
-    )
-    up_perm = [(i, (i + 1) % patch_count) for i in range(patch_count)]
-    down_perm = [(j, i) for i, j in up_perm]
-    grad_kv = (
-        grad_ext[:, 1]
-        + lax.ppermute(grad_ext[:, 0].astype(BF16), "nodes", down_perm)
-        + lax.ppermute(grad_ext[:, 2].astype(BF16), "nodes", up_perm)
-    )
-    grad_projected = (
-        jnp.concatenate([grad_query, grad_kv], axis=-1).astype(BF16).reshape(-1, 3 * head_dim)
-    )
-    a_own = a_one[1].reshape(-1, full_width)
-    grad_project = mul(a_own, grad_projected, TN)
-    grad_one = lax.psum_scatter(
-        mul(grad_projected, w_proj_low, NT), "heads", scatter_dimension=1, tiled=True
-    )
-    norm_one, root_one = norm_rows(state)
-    norm_one = own_columns(norm_one)
-    scale_one = own_columns(1.0 + per_batch(1))
-    grad_in = grad_one * scale_one
-    mean_grad, mean_cross = lax.psum(
-        (jnp.sum(grad_in, axis=-1, keepdims=True), jnp.sum(grad_in * norm_one, axis=-1, keepdims=True)),
-        "heads",
-    )
-    input_grad = own_columns(grad_hidden) + root_one * (
-        grad_in - mean_grad / full_width - norm_one * mean_cross / full_width
-    )
-    grad_two_own, norm_two_own = own_columns(grad_two), own_columns(norm_two)
-
-    def node_sum(rows):
-        return jnp.sum(rows.reshape(micro_count, capacity, share), axis=1)
-
-    mod_summed = lax.psum(
-        jnp.stack(
-            [
-                node_sum(grad_one),
-                node_sum(grad_one * norm_one),
-                node_sum(grad_two_own),
-                node_sum(grad_two_own * norm_two_own),
-            ],
-            axis=1,
-        ),
-        "nodes",
-    )
-    grad_modulate = jnp.einsum("bc,bjd->jcd", noise_embed, mod_summed, precision=HIGH)
-    grad_bias = jnp.sum(mod_summed, axis=0)
-
-    grad_cat = jnp.concatenate([grad_project, grad_output, grad_expand, grad_contract], axis=1)
     moment_cat = jnp.concatenate(
         [momentum_project, momentum_output.T, momentum_expand, momentum_contract.T], axis=1
     )
-    moment_cat = MOMENTUM_DECAY * moment_cat + lax.psum_scatter(
-        grad_cat, "nodes", scatter_dimension=0, tiled=True
-    )
-    whole = lax.all_gather(moment_cat.astype(BF16), ("nodes", "heads"), axis=0, tiled=False)
-    whole = whole.reshape(patch_count, head_count, shard_rows, weight_width)
-    whole = whole.transpose(0, 2, 1, 3).reshape(full_width, head_count, weight_width).astype(F32)
+
+    def scratch(dtype, *shape):
+        return pltpu.VMEM(shape, dtype)
+
+    blocks = (micro_count, 2, 2, capacity, head_dim)
+    half_blocks = (micro_count, 2, capacity, head_dim)
+    rows_wide = (micro_count, capacity, full_width)
+    rows_hidden = (micro_count, capacity, hidden)
+    key_value_rows = (capacity, 2 * head_dim)
+    eighth = full_width // 8
+    scratches = [
+        scratch(F32, *rows_wide),
+        scratch(BF16, *rows_wide),
+        scratch(BF16, *rows_hidden),
+        scratch(BF16, *rows_hidden),
+        scratch(F32, *blocks),
+        scratch(F32, *half_blocks),
+        scratch(BF16, *half_blocks),
+        scratch(BF16, *half_blocks),
+        scratch(F32, *blocks),
+        scratch(BF16, *blocks),
+        scratch(BF16, *half_blocks),
+        scratch(F32, *half_blocks),
+        scratch(BF16, micro_count, capacity, head_dim),
+        scratch(F32, head_count, micro_count, capacity, head_dim),
+        scratch(BF16, *rows_wide),
+        scratch(BF16, micro_count, capacity, head_dim),
+        scratch(BF16, capacity, 3 * capacity),
+        scratch(F32, micro_count, *key_value_rows),
+        scratch(BF16, micro_count, 2, *key_value_rows),
+        scratch(BF16, micro_count, 2, *key_value_rows),
+        scratch(BF16, micro_count, capacity, 3 * head_dim),
+        scratch(F32, head_count, 4 * micro_count, share),
+        scratch(F32, 8, 4 * micro_count, share),
+        scratch(F32, 2, 4, eighth, weight_width),
+        scratch(BF16, 2, 4, eighth, weight_width),
+        scratch(BF16, 4, eighth, weight_width),
+        scratch(BF16, 3, eighth, weight_width),
+    ]
+    if own_gather:
+        scratches += [
+            scratch(BF16, eighth, weight_width),
+            scratch(BF16, head_count, 2, 4, eighth, hidden),
+            scratch(BF16, full_width, 3 * full_width),
+            scratch(BF16, 3, full_width, full_width),
+            scratch(BF16, full_width, 3 * full_width),
+            scratch(F32, full_width, full_width),
+            scratch(BF16, 3, 3, full_width, full_width),
+            scratch(BF16, 4, eighth, hidden),
+            scratch(BF16, 4, eighth, hidden),
+        ]
+    semaphores = [pltpu.SemaphoreType.DMA((count,)) for count in (64, 64, 16, 16)]
+    operands = [
+        patch_sizes,
+        state_all,
+        cot_all,
+        mod_all,
+        a_one,
+        queries,
+        key_value,
+        prob_low,
+        mixed_all,
+        weight_all,
+        output_all.reshape(head_count, 8, eighth, head_dim),
+    ]
+    out_shape = [
+        jax.ShapeDtypeStruct((micro_count, capacity, share), BF16),
+        jax.ShapeDtypeStruct((micro_count, capacity, share), F32),
+    ]
+    summed_shape = jax.ShapeDtypeStruct((4 * micro_count, share), F32)
+    if own_gather:
+        operands += [moment_cat, weight_cat]
+        shard = jax.ShapeDtypeStruct(weight_cat.shape, F32)
+        out_shape += [shard, shard, summed_shape]
+    else:
+        out_shape += [jax.ShapeDtypeStruct((8, eighth, weight_width), F32), summed_shape]
+
+    def update_body(*refs):
+        refs = list(refs)
+        if not own_gather:
+            refs[11:11] = [None, None]
+            refs[16:16] = [None]
+            refs[-4:-4] = [None] * 9
+        update_kernel(patch_count, own_gather, *refs)
+
+    updated = pl.pallas_call(
+        update_body,
+        out_shape=out_shape,
+        in_specs=[pl.BlockSpec(memory_space=pltpu.SMEM)] + [vmem] * (len(operands) - 1),
+        out_specs=[vmem] * len(out_shape),
+        scratch_shapes=scratches + semaphores,
+        compiler_params=pltpu.CompilerParams(
+            collective_id=1, has_side_effects=True, vmem_limit_bytes=60 << 20
+        ),
+        name="update",
+    )(*operands)
     cuts = (0, 3 * head_dim, 4 * head_dim, 4 * head_dim + hidden, weight_width)
-    factors = (1.0, 1.0, 1.0, (head_count * hidden / full_width) ** 0.5)
-    pieces = []
-    for number in range(4):
-        columns = cuts[number + 1] - cuts[number]
-        matrix = whole[:, :, cuts[number] : cuts[number + 1]].reshape(full_width, head_count * columns)
-        ortho = lax.dynamic_slice(
-            orthogonal(matrix), (patch_index * shard_rows, head_index * columns), (shard_rows, columns)
+    if own_gather:
+        layer_output, input_grad, moment_cat, new_cat, mod_summed = updated
+    else:
+        layer_output, input_grad, grad_cat, mod_summed = updated
+        mod_summed = lax.psum(mod_summed, "nodes")
+        moment_cat = MOMENTUM_DECAY * moment_cat + lax.psum_scatter(
+            grad_cat.reshape(full_width, weight_width), "nodes", scatter_dimension=0, tiled=True
         )
-        pieces.append(factors[number] * ortho)
-    new_cat = weight_cat * (1.0 - LR_MUON * DECAY_WEIGHT) - LR_MUON * jnp.concatenate(pieces, axis=1)
+        whole = lax.all_gather(moment_cat.astype(BF16), ("nodes", "heads"), axis=0, tiled=False)
+        whole = whole.reshape(patch_count, head_count, shard_rows, weight_width)
+        whole = whole.transpose(0, 2, 1, 3).reshape(full_width, head_count, weight_width).astype(F32)
+        factors = (1.0, 1.0, 1.0, (head_count * hidden / full_width) ** 0.5)
+        pieces = []
+        for number in range(4):
+            columns = cuts[number + 1] - cuts[number]
+            matrix = whole[:, :, cuts[number] : cuts[number + 1]].reshape(full_width, head_count * columns)
+            ortho = lax.dynamic_slice(
+                orthogonal(matrix),
+                (patch_index * shard_rows, head_index * columns),
+                (shard_rows, columns),
+            )
+            pieces.append(factors[number] * ortho)
+        new_cat = weight_cat * (1.0 - LR_MUON * DECAY_WEIGHT) - LR_MUON * jnp.concatenate(pieces, axis=1)
 
     def unpack(cat):
         project, output, expand, contract = (cat[:, cuts[i] : cuts[i + 1]] for i in range(4))
         return (project, output.T, expand, contract.T)
 
+    mod_summed = mod_summed.reshape(micro_count, 4, share)
+    grad_modulate = sum(
+        noise_embed[b][None, :, None] * mod_summed[b][:, None, :] for b in range(micro_count)
+    )
+    grad_bias = jnp.sum(mod_summed, axis=0)
     first_mod, second_mod, new_mod = adam_step(
         w_modulate, first_modulate, second_modulate, grad_modulate
     )
     first_b, second_b, new_b = adam_step(b_modulate, first_bias, second_bias, grad_bias)
     return (
         layer_output,
-        input_grad.reshape(micro_count, capacity, share),
+        input_grad,
         *unpack(moment_cat),
         *unpack(new_cat),
         first_mod,

time: 632 us -> 205 us (0.32); the launches traced: 622 us -> 205 us
  matrix products: 208 us -> 1.4 us
  waiting for transfers between devices: 184 us -> 0 us
  Pallas kernels: 59 us -> 189 us
  local copies, waits for them, and re-layouts: 72.7 us -> 7.41 us
  blocking collectives: 36.3 us -> 0 us
  other arithmetic: 39.2 us -> 6.54 us
  between operations: 18.3 us -> 0.91 us
    dot_general x92 -> x0, matrix products: 206 us -> none  [the longest x20 39.2 us: orthogonal(): jnp.dot(gram, gram, precision=HIGH)]
    pallas_call x0 -> x1, Pallas kernels: none -> 130 us  [per_device(): pl.pallas_call(update_body, out_shape=out_shape, in_specs=[pl.BlockSpec(m...]
    unnamed x6 -> x0, waiting for transfers between devices: 65.4 us -> none
    reduce_scatter x2 -> x0, waiting for transfers between devices: 49.2 us -> none  [the longest x1 31.7 us: per_device(): lax.psum_scatter(mul(grad_projected, w_proj_low, NT), 'heads', scatter_di...]
    psum x1 -> x0, waiting for transfers between devices: 40.1 us -> none  [per_device(): grad_two = lax.psum(mul(grad_up, w_exp_low, NT), 'heads')]
    psum x2 -> x0, blocking collectives: 36.3 us -> none  [the longest x1 21.4 us: per_device(): lax.psum(jnp.stack([node_sum(grad_one), node_sum(grad_one * norm_one), no...]
    unnamed x132 -> x45, local copies, waits for them, and re-layouts: 31.5 us -> 2.24 us
    slice x9 -> x2, local copies, waits for them, and re-layouts: 22.1 us -> 0.78 us  [the longest x1 0.77 us: per_device(): mod_summed[b][:, None, :]]
  transfers between devices with their start and end apart: 7 -> 0, of which waited for: 6 -> 0; matrix products, arithmetic and copies ran while one was open for 10% -> 0% of each run, Pallas kernels for 0% -> 0%
where the time goes in v2:
time: 205 us
  Pallas kernels  189 us (92%)
  local copies, waits for them, and re-layouts  7.41 us (4%)
  other arithmetic  6.54 us (3%)
    pallas_call x1, Pallas kernels, per_device(): pl.pallas_call(update_body, out_shape=out_shape, in_specs=[pl.BlockSpec(m...  130 us
    pallas_call x1, Pallas kernels, per_device(): pl.pallas_call(attend_body, out_shape=out_shape, in_specs=[vmem] * 5, out...  59 us

profile of v2, /device:TPU:0, one launch (start us, length us, event | category | flops | bytes accessed | tf_op | source)
XLA Modules:
  0.0 204.9 jit_solution(14821970616190302681)
XLA Ops:
  0.6 0.0 copy-start.10
  0.7 0.0 copy-start.4
  0.7 0.0 copy-start.6
  0.7 0.0 copy-start.5
  0.7 0.0 copy-start.14
  0.7 0.0 copy-start.11
  0.7 0.0 copy-start.13
  0.7 0.0 copy-start.12
  0.7 0.0 copy-start.20
  0.7 1.9 fusion.4.refs_4_
  2.6 0.9 add_select_fusion
  3.5 0.2 copy.38
  3.7 0.9 reshape.50.refs_2_
  4.5 1.4 convolution_add_fusion
  5.9 0.6 copy.39
  6.5 59.0 %attend.1 = (bf16[4,2,512,128]{3,2,1,0:T(8,128)(2,1)}, bf16[4,2,512,128]{3,2,1,0:T(8,128)(2,1)}, f32[4,8,128]{2,1,0:T(8,128)}, bf16[3,2,512,512]{3,2,1,0:T(8,128...) custom-call(bf16[2,512,128]{2,1,0:T(8,128)(2,1)} %refs_0_.2, ...), custom_call_target="tpu_custom_call" | custom-call | tf_op jit(solution)/shard_map/attend/pallas_call | solution.py:980
  65.5 0.0 copy-done.10
  65.5 0.0 copy-done.4
  65.6 0.0 copy-done.6
  65.6 0.0 copy-done.5
  65.6 0.8 pad_maximum_fusion.refs_12_
  66.3 0.0 copy-done.14
  66.3 0.0 copy-done.11
  66.4 0.0 copy-done.13
  66.4 0.0 copy-done.12
  66.4 0.8 pad_maximum_fusion.1.refs_11_
  67.1 0.0 copy-done.20
  67.1 0.6 copy.40.refs_0_
  67.8 0.0 copy-start.17
  67.8 0.0 copy-start
  67.8 0.0 copy-start.2
  67.8 0.0 copy-start.3
  67.8 129.7 %update.1 = (bf16[2,512,128]{2,1,0:T(8,128)(2,1)}, f32[2,512,128]{2,1,0:T(8,128)}, f32[64,1536]{1,0:T(8,128)}, f32[64,1536]{1,0:T(8,128)}, f32[8,128]{1,0:T(8,128)}) custom-call(s32[2,1]{1,0:T(2,128)} %copy.40.refs_0_, bf16[4,2,512,128]{3,2,1,0:T(8,128)(2,1)} %get-tuple-element.31.refs_1_, bf16[4,2,512,128]{3,2,1,0:T(8,128)(2,1)} %get-tuple-element.32.refs_2_, ...), custom_call_target="tpu_custom_call" | custom-call | tf_op jit(solution)/shard_map/update/pallas_call | solution.py:1092
  197.5 0.0 copy-start.7
  197.5 0.0 copy-start.8
  197.5 0.0 copy-start.15
  197.5 0.0 copy-start.16
  197.5 0.0 copy-start.18
  197.5 0.0 copy-start.19
  197.6 0.0 copy-start.9
  197.6 0.0 copy-start.1
  197.6 0.8 fusion.7
  198.3 0.0 copy-done.17
  198.4 0.0 copy-done
  198.4 0.0 copy-done.2
  198.4 0.0 copy-done.3
  198.4 1.7 divide_subtract_fusion
  200.0 0.0 copy-done.7
  200.1 0.0 copy-done.8
  200.1 0.8 slice_bitcast_fusion
  200.8 0.6 slice_bitcast_fusion.2
  201.5 0.6 slice.38
  202.1 0.6 slice.42
  202.8 0.0 copy-done.15
  202.8 0.0 copy-done.16
  202.8 0.0 copy-done.18
  202.8 0.0 copy-done.19
  202.8 0.6 divide_subtract_fusion.1
  203.4 0.0 copy-done.9
  203.4 0.7 copy.43
  204.1 0.0 copy-done.1
  204.1 0.8 copy.44
  (2 shorter events, 0.0 us)
Async XLA Ops:
  0.6 64.9 %copy-start.10 = (f32[128,64]{0,1:T(8,128)S(1)}, f32[128,64]{0,1:T(8,128)}, u32[]{:S(2)}) copy-start(f32[128,64]{0,1:T(8,128)} %param.25) | copy-start | bytes 98308
  0.7 64.9 %copy-start.4 = (f32[512,64]{0,1:T(8,128)S(1)}, f32[512,64]{0,1:T(8,128)}, u32[]{:S(2)}) copy-start(f32[512,64]{0,1:T(8,128)} %param.27) | copy-start | bytes 393220
  0.7 64.9 %copy-start.6 = (f32[64,384]{1,0:T(8,128)S(1)}, f32[64,384]{1,0:T(8,128)}, u32[]{:S(2)}) copy-start(f32[64,384]{1,0:T(8,128)} %param.24) | copy-start | bytes 294916
  0.7 64.9 %copy-start.5 = (f32[64,512]{1,0:T(8,128)S(1)}, f32[64,512]{1,0:T(8,128)}, u32[]{:S(2)}) copy-start(f32[64,512]{1,0:T(8,128)} %param.26) | copy-start | bytes 393220
  0.7 65.7 %copy-start.14 = (f32[128,64]{0,1:T(8,128)S(1)}, f32[128,64]{0,1:T(8,128)}, u32[]{:S(2)}) copy-start(f32[128,64]{0,1:T(8,128)} %param.29) | copy-start | bytes 98308
  0.7 65.7 %copy-start.11 = (f32[512,64]{0,1:T(8,128)S(1)}, f32[512,64]{0,1:T(8,128)}, u32[]{:S(2)}) copy-start(f32[512,64]{0,1:T(8,128)} %param.31) | copy-start | bytes 393220
  0.7 65.6 %copy-start.13 = (f32[64,384]{1,0:T(8,128)S(1)}, f32[64,384]{1,0:T(8,128)}, u32[]{:S(2)}) copy-start(f32[64,384]{1,0:T(8,128)} %param.28) | copy-start | bytes 294916
  0.7 65.6 %copy-start.12 = (f32[64,512]{1,0:T(8,128)S(1)}, f32[64,512]{1,0:T(8,128)}, u32[]{:S(2)}) copy-start(f32[64,512]{1,0:T(8,128)} %param.30) | copy-start | bytes 393220
  0.7 66.4 %copy-start.20 = (s32[2,1]{0,1:T(1,128)S(1)}, s32[2,1]{0,1:T(1,128)}, u32[]{:S(2)}) copy-start(s32[2,1]{0,1:T(1,128)} %param.23) | copy-start | bytes 28
  67.8 130.6 %copy-start.17 = (f32[2,256]{1,0:T(2,128)S(1)}, f32[2,256]{1,0:T(2,128)}, u32[]{:S(2)}) copy-start(f32[2,256]{1,0:T(2,128)} %param.20) | copy-start | bytes 6148
  67.8 130.6 %copy-start = (f32[4,256,128]{2,1,0:T(8,128)S(1)}, f32[4,256,128]{2,1,0:T(8,128)}, u32[]{:S(2)}) copy-start(f32[4,256,128]{2,1,0:T(8,128)} %param.32) | copy-start | bytes 1572868
  67.8 130.6 %copy-start.2 = (f32[4,256,128]{2,1,0:T(8,128)S(1)}, f32[4,256,128]{2,1,0:T(8,128)}, u32[]{:S(2)}) copy-start(f32[4,256,128]{2,1,0:T(8,128)} %param.35) | copy-start | bytes 1572868
  67.8 130.6 %copy-start.3 = (f32[4,256,128]{2,1,0:T(8,128)S(1)}, f32[4,256,128]{2,1,0:T(8,128)}, u32[]{:S(2)}) copy-start(f32[4,256,128]{2,1,0:T(8,128)} %param.34) | copy-start | bytes 1572868
  197.5 2.6 %copy-start.7 = (f32[64,1536]{1,0:T(8,128)S(1)}, f32[64,1536]{1,0:T(8,128)}, u32[]{:S(2)}) copy-start(f32[64,1536]{1,0:T(8,128)} %get-tuple-element.44) | copy-start | bytes 1179652
  197.5 2.6 %copy-start.8 = (f32[64,1536]{1,0:T(8,128)S(1)}, f32[64,1536]{1,0:T(8,128)}, u32[]{:S(2)}) copy-start(f32[64,1536]{1,0:T(8,128)} %get-tuple-element.43) | copy-start | bytes 1179652
  197.5 5.3 %copy-start.15 = (f32[8,128]{1,0:T(8,128)S(1)}, f32[8,128]{1,0:T(8,128)}, u32[]{:S(2)}) copy-start(f32[8,128]{1,0:T(8,128)} %get-tuple-element.45) | copy-start | bytes 12292
  197.5 5.3 %copy-start.16 = (f32[4,128]{1,0:T(4,128)S(1)}, f32[4,128]{1,0:T(4,128)}, u32[]{:S(2)}) copy-start(f32[4,128]{1,0:T(4,128)} %param.33) | copy-start | bytes 6148
  197.5 5.3 %copy-start.18 = (f32[4,128]{1,0:T(4,128)S(1)}, f32[4,128]{1,0:T(4,128)}, u32[]{:S(2)}) copy-start(f32[4,128]{1,0:T(4,128)} %param.37) | copy-start | bytes 6148
  197.5 5.3 %copy-start.19 = (f32[4,128]{1,0:T(4,128)S(1)}, f32[4,128]{1,0:T(4,128)}, u32[]{:S(2)}) copy-start(f32[4,128]{1,0:T(4,128)} %param.36) | copy-start | bytes 6148
  197.6 5.9 %copy-start.9 = (bf16[2,512,128]{2,1,0:T(8,128)(2,1)S(1)}, bf16[2,512,128]{2,1,0:T(8,128)(2,1)}, u32[]{:S(2)}) copy-start(bf16[2,512,128]{2,1,0:T(8,128)(2,1)} %get-tuple-element.80) | copy-start | bytes 786436
  197.6 6.6 %copy-start.1 = (f32[2,512,128]{2,1,0:T(8,128)S(1)}, f32[2,512,128]{2,1,0:T(8,128)}, u32[]{:S(2)}) copy-start(f32[2,512,128]{2,1,0:T(8,128)} %get-tuple-element.81) | copy-start | bytes 1572868

commit v3 on v1

v3 whole, which is shorter than its diff:
```python
import functools

import jax
import jax.numpy as jnp
from jax import lax
from jax.experimental import pallas as pl
from jax.experimental.pallas import tpu as pltpu
from jax.sharding import PartitionSpec as P

NS_STEPS = 5
STEP = 10


EPS_NORM = 1e-06
NEWTON_A = 3.4445
NEWTON_B = -4.775
NEWTON_C = 2.0315
MOMENTUM_DECAY = 0.5
LR_MUON = 1.0
LR_ADAM = 0.04
DECAY_WEIGHT = 0.01
BETA_FIRST = 0.9
BETA_SECOND = 0.999
EPS_ADAM = 1e-08
HIGH = lax.Precision.HIGHEST
MESH = pl.DeviceIdType.MESH
F32 = jnp.float32
BF16 = jnp.bfloat16
NN = (((1,), (0,)), ((), ()))
NT = (((1,), (1,)), ((), ()))
TN = (((0,), (0,)), ((), ()))


def mul(left, right, dims=NN):
    return lax.dot_general(left, right, dims, preferred_element_type=F32)


class Links:
    def __init__(self, send_sems, recv_sems):
        self.send_sems, self.recv_sems = send_sems, recv_sems
        self.copies, self.finished = [], []

    def send(self, source, target, device):
        slot = len(self.copies)
        copy = pltpu.make_async_remote_copy(
            src_ref=source,
            dst_ref=target,
            send_sem=self.send_sems.at[slot],
            recv_sem=self.recv_sems.at[slot],
            device_id=device,
            device_id_type=MESH,
        )
        copy.start()
        self.copies.append(copy)
        return copy

    def finish(self, copy):
        copy.wait_send()
        self.finished.append(copy)

    def close(self):
        for copy in self.copies:
            if not any(copy is other for other in self.finished):
                copy.wait_send()


def greet(devices):
    barrier = pltpu.get_barrier_semaphore()
    for device in devices:
        pl.semaphore_signal(barrier, inc=1, device_id=device, device_id_type=MESH)


def await_greetings(devices):
    pl.semaphore_wait(pltpu.get_barrier_semaphore(), len(devices))


def norm_rows(values):
    width = values.shape[-1]
    row_mean = jnp.sum(values, axis=-1, keepdims=True) / width
    square_mean = jnp.sum(values * values, axis=-1, keepdims=True) / width
    inv_root = lax.rsqrt(square_mean - row_mean * row_mean + EPS_NORM)
    return ((values - row_mean) * inv_root, inv_root)


def wide(ref, *index):
    return jnp.concatenate([ref[(head, *index)] for head in range(ref.shape[0])], axis=-1)


def mod_row(mod_ref, batch, number):
    return wide(mod_ref, slice(batch * 4 + number, batch * 4 + number + 1), slice(None))


def layer_kernel(
    patch_count,
    own_gather,
    sizes_ref,
    state_ref,
    cot_ref,
    index_ref,
    noise_ref,
    modulate_ref,
    bias_ref,
    weight_refs,
    moment_refs,
    layer_output,
    input_grad,
    moment_new,
    ortho_in,
    mod_sum,
    weight_low,
    weight_all,
    output_all,
    state_all,
    cot_all,
    mod_all,
    halo,
    a_one,
    queries,
    key_value,
    prob_low,
    mixed_all,
    hidden_one,
    a_two,
    act,
    grad_up,
    part_two,
    part_core,
    part_low,
    part_across,
    total_two,
    out_low,
    out_core,
    out_keep,
    out_across,
    grad_hidden,
    grad_attn,
    grad_mixed,
    score_low,
    grad_own,
    grad_away,
    grad_back,
    grad_projected,
    mod_part,
    mod_in,
    grad_cat,
    grad_low,
    grad_core,
    grad_line,
    grad_near,
    moment_low,
    matrix,
    gram,
    chain,
    ortho_out,
    send_sems,
    recv_sems,
    turn_send,
    turn_recv,
):
    node, head = lax.axis_index("nodes"), lax.axis_index("heads")
    after, before = lax.rem(node + 1, patch_count), lax.rem(node + patch_count - 1, patch_count)
    across, sibling = lax.rem(head + 2, 4), head + 1 - 2 * lax.rem(head, 2)
    to_across, to_sibling, to_diagonal = (node, across), (node, sibling), (node, 3 - head)
    to_after, to_before = (after, head), (before, head)
    side, core = lax.div(head, 2), lax.rem(head, 2)
    plane, parity = lax.div(node, 2), lax.rem(node, 2)
    mirror = 1 - parity
    partner = node + 1 - 2 * parity
    to_partner = (partner, head)
    micro_count, capacity, share = state_ref.shape
    head_dim = queries.shape[-1]
    full_width = a_one.shape[-1]
    hidden = act.shape[-1]
    total = 3 * capacity
    inv_head = head_dim ** (-0.5)
    cuts = (0, 3 * head_dim, 4 * head_dim, 4 * head_dim + hidden, 4 * head_dim + 2 * hidden)
    widths = (3 * head_dim, head_dim, hidden, hidden)
    expand_columns, contract_columns = slice(cuts[2], cuts[3]), slice(cuts[3], cuts[4])
    tile = capacity // 2
    batches = range(micro_count)
    peers = [(lax.rem(node + 2 * k, patch_count), head) for k in range(1, patch_count // 2)]
    met = [to_across, to_sibling, to_diagonal]
    if own_gather:
        met += [(lax.rem(node + k, patch_count), head) for k in range(1, patch_count)]
        met += [(partner, across)]
    else:
        met += [to_after, to_before]
    greet(met)
    for number in range(modulate_ref.shape[0]):
        terms = lax.dot_general(
            noise_ref[...], modulate_ref[number], NN, precision=HIGH, preferred_element_type=F32
        )
        terms = terms + bias_ref[number : number + 1, :]
        for b in batches:
            place = b * modulate_ref.shape[0] + number
            mod_all[head, place : place + 1, :] = terms[b : b + 1]
    if own_gather:
        for number, ref in enumerate(weight_refs):
            weight_low[:, cuts[number] : cuts[number + 1]] = ref[...].astype(BF16)
    await_greetings(met)
    links = Links(send_sems, recv_sems)

    def weight(columns):
        return weight_all[:, :, columns].reshape(full_width, columns.stop - columns.start)

    def live_rows(batch, start, count):
        slots = lax.broadcasted_iota(jnp.int32, (count, 1), 0) + start
        return (slots < sizes_ref[batch, 0]).astype(F32)

    def rows_at(step, count):
        start = step * count if isinstance(step, int) else pl.multiple_of(step * count, count)
        return start, pl.ds(start, count)

    first_columns = pl.ds(0, cuts[2])
    other_columns = pl.ds(cuts[2], cuts[4] - cuts[2])

    def spread(columns):
        part = weight_low.at[:, columns]
        into = weight_all.at[node, :, columns]
        return [links.send(part, into, to) for to in peers], (part, into)

    def pass_on(arriving, columns):
        passed = []
        for k, copy in enumerate(arriving):
            copy.wait_recv()
            owner = lax.rem(node + patch_count - 2 * (k + 1), patch_count)
            part = weight_all.at[owner, :, columns]
            passed.append(links.send(part, part, to_partner))
        return passed

    mod_copies = [
        links.send(mod_all.at[head], mod_all.at[head], to) for to in (to_across, to_sibling, to_diagonal)
    ]
    if own_gather:
        first_peers, first_partner = spread(first_columns)
        first_partner = [links.send(*first_partner, to_partner)]
    state_across, state_after, state_before, state_sibling = [], [], [], []
    for b in batches:
        state_across.append(links.send(state_ref.at[b], state_all.at[head, b], to_across))
        state_after.append(links.send(state_ref.at[b], halo.at[0, head, b], to_after))
        state_before.append(links.send(state_ref.at[b], halo.at[1, head, b], to_before))
        state_sibling.append(links.send(state_ref.at[b], state_all.at[head, b], to_sibling))
    if own_gather:
        other_peers, other_partner = spread(other_columns)
    cot_across = [links.send(cot_ref.at[0], cot_all.at[head, 0], to_across)]
    if own_gather:
        weight_all[node] = weight_low[...]
    state_all[head] = state_ref[...]
    cot_all[head] = cot_ref[...]

    group = index_ref.shape[-1] // 16
    blocks = total // share

    def count_group(batch, place):
        ids = index_ref[batch, pl.ds(place, 1), :]
        lanes = lax.broadcasted_iota(jnp.int32, ids.shape, 1)
        code = (ids >> 7) + 16 * (lanes >> 4)
        rows = lax.broadcasted_iota(jnp.int32, (blocks * group, ids.shape[1]), 0)
        pick = jnp.where(code == (rows // group) + 16 * (rows % group), 1.0, 0.0).astype(BF16)
        slots = lax.broadcasted_iota(jnp.int32, (share, ids.shape[1]), 0)
        spot = jnp.where((ids & 127) == slots, 1.0, 0.0).astype(BF16)
        found = mul(pick, spot, NT).astype(BF16)
        into = pl.ds(pl.multiple_of(place * group, group), group)
        for block in range(blocks):
            prob_low[batch, into, block * share : (block + 1) * share] = found[
                block * group : (block + 1) * group
            ]

    def count(batch):
        pl.loop(0, capacity // group, unroll=4)(lambda place: count_group(batch, place))

    pass_state, halo_across, halo_sibling = [], [], []

    def second_hops(b):
        state_across[b].wait_recv()
        part = state_all.at[across, b]
        pass_state.append(links.send(part, part, to_sibling))
        to_chip, to_core = [], []
        for k, copy in ((0, state_after[b]), (1, state_before[b])):
            copy.wait_recv()
            part = halo.at[k, head, b]
            to_chip.append(links.send(part, part, to_across))
            to_core.append(links.send(part, part, to_sibling))
        halo_across.append(to_chip)
        halo_sibling.append(to_core)

    count(0)
    second_hops(0)
    if own_gather:
        first_passed = pass_on(first_peers, first_columns)
    count(1)
    second_hops(1)
    if own_gather:
        other_partner = [links.send(*other_partner, to_partner)]
    cot_across += [links.send(cot_ref.at[b], cot_all.at[head, b], to_across) for b in batches[1:]]
    cot_sibling = links.send(cot_ref, cot_all.at[head], to_sibling)

    def project(source, patch, batch):
        shift, scale = mod_row(mod_all, batch, 0), 1.0 + mod_row(mod_all, batch, 1)

        @pl.loop(0, capacity // tile)
        def _(step):
            _, rows = rows_at(step, tile)
            normed, _ = norm_rows(wide(source, batch, rows, slice(None)).astype(F32))
            a_rows = (normed * scale + shift).astype(BF16)
            a_one[patch * micro_count + batch, rows, :] = a_rows
            first = 0 if patch == 1 else head_dim
            out = mul(a_rows, weight(slice(first, cuts[1]))).astype(BF16)
            if patch == 1:
                queries[batch, rows, :] = out[:, :head_dim]
            key_value[batch, patch, rows, :] = out[:, out.shape[1] - 2 * head_dim :]

    def project_all(b):
        state_sibling[b].wait_recv()
        pass_state[b].wait_recv()
        project(state_all, 1, b)
        for k in range(2):
            halo_across[b][k].wait_recv()
            part = halo.at[k, across, b]
            halo_sibling[b].append(links.send(part, part, to_sibling))
        for copy in halo_sibling[b]:
            copy.wait_recv()
        project(halo.at[0], 0, b)
        project(halo.at[1], 2, b)

    def attend(batch):
        attend_rows = 128

        @pl.loop(0, capacity // attend_rows)
        def _(step):
            _, rows = rows_at(step, attend_rows)
            keys = key_value[batch, :, :, :head_dim].reshape(total, head_dim)
            values = key_value[batch, :, :, head_dim:].reshape(total, head_dim)
            scores = mul(queries[batch, rows, :], keys, NT) * inv_head
            times = prob_low[batch, rows, :].astype(F32)
            scores = jnp.where(times > 0.0, scores, -1e30)
            exps = jnp.exp(scores - jnp.max(scores, axis=-1, keepdims=True)) * times
            prob = (exps * (1.0 / jnp.sum(exps, axis=-1, keepdims=True))).astype(BF16)
            prob_low[batch, rows, :] = prob
            mixed_all[head, batch, rows, :] = mul(prob, values).astype(BF16)

        part = mixed_all.at[head, batch]
        return links.send(part, part, to_across), links.send(part, part, to_sibling)

    def pass_mixed(batch, copies):
        copies[0].wait_recv()
        part = mixed_all.at[across, batch]
        return [copies[1], links.send(part, part, to_sibling)]

    def wait_all(copies):
        for copy in copies:
            copy.wait_recv()

    wait_all(mod_copies)
    ready = [cot_sibling]
    if own_gather:
        wait_all(first_partner + first_passed)
        output_all[head] = weight_all[:, :, cuts[1] : cuts[2]]
        output_part = weight_all.at[:, :, pl.ds(cuts[1], head_dim)]
        output_across = links.send(output_part, output_all.at[head], to_across)
        ready.append(links.send(output_part, output_all.at[head], to_sibling))
    project_all(0)
    mixed_first = attend(0)
    if own_gather:
        other_passed = pass_on(other_peers, other_columns)
    project_all(1)
    mixed_first = pass_mixed(0, mixed_first)
    wait_all(cot_across)
    ready.append(links.send(cot_all.at[across], cot_all.at[across], to_sibling))
    if own_gather:
        output_across.wait_recv()
        ready.append(links.send(output_all.at[across], output_all.at[across], to_sibling))
    mixed_second = attend(1)
    if own_gather:
        ready += other_partner + other_passed
    wait_all(ready + mixed_first)

    def feed_forward(batch, step):
        start, rows = rows_at(step, tile)
        mixed = wide(mixed_all, batch, rows, slice(None))
        mixer = jnp.concatenate(
            [output_all[k].reshape(full_width, head_dim) for k in range(output_all.shape[0])], axis=-1
        )
        hid = wide(state_all, batch, rows, slice(None)).astype(F32) + mul(mixed, mixer, NT)
        hidden_one[batch, rows, :] = hid
        normed, _ = norm_rows(hid)
        a_rows = (normed * (1.0 + mod_row(mod_all, batch, 3)) + mod_row(mod_all, batch, 2)).astype(BF16)
        a_two[batch, rows, :] = a_rows
        up = mul(a_rows, weight(expand_columns))
        gate = jax.nn.sigmoid(up)
        acted = (up * gate).astype(BF16)
        act[batch, rows, :] = acted
        live = live_rows(batch, start, tile)
        cot = (wide(cot_all, batch, rows, slice(None)).astype(F32) * live).astype(BF16)
        grad_act = mul(cot, weight(contract_columns))
        grad_rows = (grad_act * gate * (1.0 + up * (1.0 - gate))).astype(BF16)
        grad_up[batch, rows, :] = grad_rows
        back = mul(grad_rows, weight(expand_columns), NT)
        out = mul(acted, weight(contract_columns), NT)
        for k in range(4):
            block = slice(k * head_dim, (k + 1) * head_dim)
            part_two[batch, k % 2, k // 2, rows, :] = back[:, block]
            out_low[batch, k % 2, k // 2, rows, :] = out[:, block].astype(BF16)

    def to_core(batch):
        return links.send(part_two.at[batch, 1 - core], part_core.at[batch], to_sibling)

    def to_side(batch, copy):
        copy.wait_recv()
        for k in range(2):
            chip = part_two[batch, core, k] + part_core[batch, k]
            part_core[batch, k] = chip
            part_low[batch, k] = chip.astype(BF16)
        return links.send(part_low.at[batch], part_across.at[batch], to_across)

    def to_all(batch, copy):
        copy.wait_recv()
        for k in range(2):
            total_two[batch, core, k] = part_core[batch, k] + part_across[batch, k].astype(F32)
        return links.send(total_two.at[batch, core], total_two.at[batch, core], to_sibling)

    def total_rows(batch, rows):
        return jnp.concatenate(
            [total_two[batch, k % 2, k // 2, rows, :] for k in range(4)], axis=-1
        )

    def back_norm(grad, normed, root):
        mean_grad = jnp.sum(grad, axis=-1, keepdims=True) / full_width
        mean_cross = jnp.sum(grad * normed, axis=-1, keepdims=True) / full_width
        return root * (grad - mean_grad - normed * mean_cross)

    def add_mod(batch, number, values):
        sums = jnp.sum(values, axis=0, keepdims=True)
        place = batch * 4 + number
        for k in range(4):
            mod_part[k, place : place + 1, :] += sums[:, k * head_dim : (k + 1) * head_dim]

    def own_block(values):
        own = jnp.zeros((values.shape[0], head_dim), F32)
        for k in range(4):
            own = own + jnp.where(head == k, values[:, k * head_dim : (k + 1) * head_dim], 0.0)
        return own

    for k in range(4):
        mod_part[k] = jnp.zeros(mod_part.shape[1:], F32)

    pl.loop(0, 2)(lambda step: feed_forward(0, step))
    core_first = to_core(0)
    mixed_second = pass_mixed(1, mixed_second)
    side_first = to_side(0, core_first)
    wait_all(mixed_second)
    pl.loop(0, 2)(lambda step: feed_forward(1, step))
    core_second = to_core(1)

    def store_grad(step, columns, value):
        half = full_width // 8
        for k in range(2):
            part = value[k * half : (k + 1) * half]
            grad_cat[k, step, :, columns] = part
            grad_low[k, step, :, columns] = part.astype(BF16)

    def both(ref, columns):
        return ref[:, :, columns].reshape(micro_count * capacity, -1)

    def one_pair(patch, columns):
        pair = a_one[patch * micro_count : (patch + 1) * micro_count, :, columns]
        return pair.reshape(micro_count * capacity, -1)

    def live_cot(batch, columns):
        return (cot_all[columns, batch].astype(F32) * live_rows(batch, 0, capacity)).astype(BF16)

    late = slice(0, cuts[2])

    def grad_pair(columns):
        return links.send(
            grad_low.at[1 - parity, :, :, columns], grad_core.at[:, :, columns], to_partner
        )

    def grad_planes(copy, columns):
        copy.wait_recv()
        for k in range(4):
            summed = grad_cat[parity, k, :, columns] + grad_core[k, :, columns].astype(F32)
            grad_cat[parity, k, :, columns] = summed
            grad_low[parity, k, :, columns] = summed.astype(BF16)
        sent = []
        for k in range(1, 4):
            target = lax.rem(plane + k, 4)
            sent.append(
                links.send(
                    grad_low.at[parity, target, :, columns],
                    grad_line.at[k - 1, :, columns],
                    (2 * target + parity, head),
                )
            )
        return sent

    def grad_finish(copies, columns):
        wait_all(copies)
        summed = grad_cat[parity, plane, :, columns]
        for k in range(3):
            summed = summed + grad_line[k, :, columns].astype(F32)
        store_moment(summed, columns)

    def grad_direct(columns):
        sent = []
        for k in range(1, patch_count):
            target = lax.rem(node + k, patch_count)
            sent.append(
                links.send(
                    grad_low.at[lax.rem(target, 2), lax.div(target, 2), :, columns],
                    grad_near.at[k - 1],
                    (target, head),
                )
            )
        return sent

    def grad_direct_finish(copies, columns):
        summed = grad_cat[parity, plane, :, columns]
        for k, copy in enumerate(copies):
            copy.wait_recv()
            summed = summed + grad_near[k].astype(F32)
        store_moment(summed, columns)

    def store_moment(summed, columns):
        for number, ref in enumerate(moment_refs):
            if columns.start <= cuts[number] < columns.stop:
                own = slice(cuts[number], cuts[number + 1])
                part = summed[:, cuts[number] - columns.start : cuts[number + 1] - columns.start]
                moment = MOMENTUM_DECAY * ref[...] + part
                moment_new[:, own] = moment
                moment_low[:, own] = moment.astype(BF16)

    @pl.loop(0, 4)
    def _(step):
        columns = pl.ds(pl.multiple_of(step * head_dim, head_dim), head_dim)
        store_grad(step, expand_columns, mul(both(a_two, columns), grad_up[...].reshape(-1, hidden), TN))

    if own_gather:
        expand_pair = grad_pair(expand_columns)

    @pl.loop(0, 4)
    def _(step):
        cot = jnp.concatenate([live_cot(b, step) for b in batches], axis=0)
        store_grad(step, contract_columns, mul(cot, act[...].reshape(-1, hidden), TN))

    if own_gather:
        contract_pair = grad_pair(contract_columns)
    side_second = to_side(1, core_second)
    all_first = to_all(0, side_first)
    out_copies = [links.send(out_low.at[b, 1 - core], out_core.at[b], to_sibling) for b in batches]

    def norm_two_back(batch):
        @pl.loop(0, capacity // tile)
        def _(step):
            start, rows = rows_at(step, tile)
            normed, root = norm_rows(hidden_one[batch, rows, :])
            grad = total_rows(batch, rows)
            add_mod(batch, 2, grad)
            add_mod(batch, 3, grad * normed)
            cot = wide(cot_all, batch, rows, slice(None)).astype(F32) * live_rows(batch, start, tile)
            grad = cot + back_norm(grad * (1.0 + mod_row(mod_all, batch, 3)), normed, root)
            grad_hidden[batch, rows, :] = own_block(grad)
            low = grad.astype(BF16)
            grad_attn[batch, rows, :] = low
            grad_mixed[batch, rows, :] = mul(low, weight(slice(cuts[1], cuts[2]))).astype(BF16)

    def attend_back(batch):
        attend_rows = 128

        @pl.loop(0, capacity // attend_rows)
        def _(step):
            _, rows = rows_at(step, attend_rows)
            keys = key_value[batch, :, :, :head_dim].reshape(total, head_dim)
            values = key_value[batch, :, :, head_dim:].reshape(total, head_dim)
            prob = prob_low[batch, rows, :].astype(F32)
            grad_prob = mul(grad_mixed[batch, rows, :], values, NT)
            mean = jnp.sum(prob * grad_prob, axis=-1, keepdims=True)
            score = (prob * (grad_prob - mean) * inv_head).astype(BF16)
            score_low[rows, :] = score
            grad_projected[batch, rows, :head_dim] = mul(score, keys).astype(BF16)

        for patch in range(3):
            slots = slice(patch * capacity, (patch + 1) * capacity)
            grad_key = mul(score_low[:, slots], queries[batch], TN)
            grad_value = mul(prob_low[batch, :, slots], grad_mixed[batch], TN)
            if patch == 1:
                grad_own[batch, :, :head_dim] = grad_key
                grad_own[batch, :, head_dim:] = grad_value
            else:
                grad_away[batch, patch // 2, :, :head_dim] = grad_key.astype(BF16)
                grad_away[batch, patch // 2, :, head_dim:] = grad_value.astype(BF16)

    def send_back(batch):
        return [
            links.send(grad_away.at[batch, 0], grad_back.at[batch, 1], to_before),
            links.send(grad_away.at[batch, 1], grad_back.at[batch, 0], to_after),
        ]

    owners = (1, 2, 0, 3)

    def turn(source, target, device, send_slot, recv_slot):
        return pltpu.make_async_remote_copy(
            src_ref=source,
            dst_ref=target,
            send_sem=turn_send.at[send_slot],
            recv_sem=turn_recv.at[recv_slot],
            device_id=device,
            device_id_type=MESH,
        )

    def to_owner(number, sender):
        return turn(
            moment_low.at[:, slice(cuts[number], cuts[number + 1])],
            matrix.at[head, parity, sender, :, : widths[number]],
            (2 * owners[number] + parity, head),
            number,
            sender,
        )

    def give(width, number):
        block, pair, device = (
            (head, parity, to_across),
            (head, parity, to_partner),
            (head, parity, (partner, across)),
            (head, parity, to_sibling),
            (across, parity, to_sibling),
            (head, mirror, to_sibling),
            (across, mirror, to_sibling),
        )[number]
        part = matrix.at[block, pair, :, :, :width]
        return turn(part, part, device, 4 + number, 4 + number)

    def own_to_owner(numbers):
        for number in numbers:

            @pl.when(plane != owners[number])
            def _():
                to_owner(number, plane).start()

            @pl.when(plane == owners[number])
            def _():
                matrix[head, parity, plane, :, : widths[number]] = moment_low[
                    :, cuts[number] : cuts[number + 1]
                ]

    def own_arrive(numbers):
        for number in numbers:

            @pl.when(plane == owners[number])
            def _():
                for other in range(4):
                    if other != owners[number]:
                        to_owner(number, other).wait_recv()
                for k in range(4):
                    give(widths[number], k).start()

            @pl.when(plane != owners[number])
            def _():
                to_owner(number, plane).wait_send()

    all_first.wait_recv()
    if own_gather:
        expand_line = grad_planes(expand_pair, expand_columns)
    norm_two_back(0)
    attend_back(0)
    back_first = send_back(0)
    all_second = to_all(1, side_second)
    if own_gather:
        contract_line = grad_planes(contract_pair, contract_columns)
    out_across_copies = []
    for batch in batches:
        out_copies[batch].wait_recv()
        for k in range(2):
            chip = out_low[batch, core, k].astype(F32) + out_core[batch, k].astype(F32)
            out_keep[batch, k] = chip
            out_core[batch, k] = chip.astype(BF16)
        out_across_copies.append(
            links.send(out_core.at[batch, 1 - side], out_across.at[batch], to_across)
        )
    all_second.wait_recv()
    norm_two_back(1)
    attend_back(1)

    @pl.loop(0, 4)
    def _(step):
        columns = pl.ds(pl.multiple_of(step * head_dim, head_dim), head_dim)
        queries_part = mul(one_pair(1, columns), both(grad_projected, slice(0, head_dim)), TN)
        store_grad(step, slice(0, head_dim), queries_part)
        rest = mul(one_pair(1, columns), grad_own[...].reshape(-1, 2 * head_dim).astype(BF16), TN)
        for patch in (0, 2):
            away = grad_away[:, patch // 2].reshape(-1, 2 * head_dim)
            rest = rest + mul(one_pair(patch, columns), away, TN)
        store_grad(step, slice(head_dim, cuts[1]), rest)
        own_mixed = mixed_all[head].reshape(-1, head_dim)
        store_grad(step, slice(cuts[1], cuts[2]), mul(both(grad_attn, columns), own_mixed, TN))

    if own_gather:
        late_direct = grad_direct(late)
    back_second = send_back(1)
    if own_gather:
        grad_finish(expand_line, expand_columns)
        grad_finish(contract_line, contract_columns)
        own_to_owner((2, 3))
    for batch in batches:
        out_across_copies[batch].wait_recv()
        own = hidden_one[batch, :, pl.ds(pl.multiple_of(head * head_dim, head_dim), head_dim)]
        result = own + out_keep[batch, side] + out_across[batch].astype(F32)
        layer_output[batch] = (result * live_rows(batch, 0, capacity)).astype(BF16)

    for copy in (core_first, core_second, side_first, side_second, all_first, all_second):
        links.finish(copy)

    def rows_back(batch, copies):
        wait_all(copies)
        whole = grad_own[batch] + grad_back[batch, 0].astype(F32) + grad_back[batch, 1].astype(F32)
        grad_projected[batch, :, head_dim:] = whole.astype(BF16)

        @pl.loop(0, capacity // tile)
        def _(step):
            _, rows = rows_at(step, tile)
            back = mul(grad_projected[batch, rows, :], weight(slice(0, cuts[1])), NT)
            for k in range(4):
                part_two[batch, k % 2, k // 2, rows, :] = back[:, k * head_dim : (k + 1) * head_dim]

        return to_core(batch)

    def rows_end(batch, copy):
        copy.wait_recv()

        @pl.loop(0, capacity // tile)
        def _(step):
            _, rows = rows_at(step, tile)
            normed, root = norm_rows(wide(state_all, batch, rows, slice(None)).astype(F32))
            grad = total_rows(batch, rows)
            add_mod(batch, 0, grad)
            add_mod(batch, 1, grad * normed)
            grad = back_norm(grad * (1.0 + mod_row(mod_all, batch, 1)), normed, root)
            input_grad[batch, rows, :] = own_block(grad) + grad_hidden[batch, rows, :]

    one_core = [rows_back(0, back_first)]

    if not own_gather:
        one_core.append(rows_back(1, back_second))
        one_side = [to_side(b, one_core[b]) for b in batches]
        one_all = [to_all(b, one_side[b]) for b in batches]
        for b in batches:
            rows_end(b, one_all[b])
        mod_sum[...] = mod_part[head]
        for k in range(8):
            moment_new[k] = grad_cat[k % 2, k // 2]
        links.close()
        return

    grad_direct_finish(late_direct, late)
    own_to_owner((0, 1))
    own_arrive((2, 3))
    one_core.append(rows_back(1, back_second))
    own_arrive((0, 1))
    one_side = [to_side(b, one_core[b]) for b in batches]
    half = full_width // 2

    def gather_plane(width):
        for k in range(3):
            give(width, k).wait_recv()
            give(width, 4 + k).start()
        for k in range(3, 7):
            give(width, k).wait_recv()
        for k in range(7):
            give(width, k).wait_send()

        @pl.loop(0, 2)
        def _(step):
            _, rows = rows_at(step, half)
            summed = jnp.zeros((half, full_width), F32)
            for k in range(4):
                left = matrix[k, step, :, :, :width].reshape(half, width)
                right = matrix[k, :, :, :, :width].reshape(full_width, width)
                summed = summed + mul(left, right, NT)
            gram[rows, :] = summed

    for first, second, width in ((1, 1, widths[0]), (2, 2, widths[1]), (0, 3, hidden)):

        @pl.when((plane == first) | (plane == second))
        def _():
            gather_plane(width)

    gram_pair, factor_pair, turn_pair = (a_one.at[pl.ds(k, 2)] for k in (0, 2, 4))

    def put_pair(ref, value, rows=slice(None)):
        high = value.astype(BF16)
        ref[0, rows, :] = high
        ref[1, rows, :] = (value - high.astype(F32)).astype(BF16)

    def times(left, right, rows=slice(None)):
        left_high, left_low = left[0, rows, :], left[1, rows, :]
        right_high, right_low = right[0], right[1]
        return mul(
            jnp.concatenate([left_high, left_high, left_low], axis=1),
            jnp.concatenate([right_high, right_low, right_high], axis=0),
        )

    def diagonal(count, start=0):
        rows = lax.broadcasted_iota(jnp.int32, (count, full_width), 0) + start
        return rows == lax.broadcasted_iota(jnp.int32, (count, full_width), 1)

    trace = jnp.zeros((1, 1), F32)
    for step in range(2):
        kept = jnp.where(diagonal(half, step * half), gram[step * half : (step + 1) * half, :], 0.0)
        trace = trace + jnp.sum(jnp.sum(kept, axis=1, keepdims=True), axis=0, keepdims=True)
    scale = 1.0 / (jnp.sqrt(trace) + 1e-07)
    gram[...] = gram[...] * (scale * scale)
    put_pair(gram_pair, gram[...])
    own = pl.ds(pl.multiple_of(parity * half, half), half)

    one_all = []
    for repeat in range(NS_STEPS - 1):
        factor = NEWTON_B * gram[...] + NEWTON_C * times(gram_pair, gram_pair)
        factor = factor + jnp.where(diagonal(full_width), NEWTON_A, 0.0)
        put_pair(factor_pair, factor)
        if repeat == 0:
            put_pair(chain.at[0], factor)
        else:
            put_pair(chain.at[repeat % 2], times(factor_pair, chain.at[(repeat + 1) % 2]))
        put_pair(turn_pair, times(factor_pair, gram_pair))
        gram[...] = times(factor_pair, turn_pair)
        put_pair(gram_pair, gram[...])
        if repeat in (1, 2):
            one_all.append(to_all(repeat - 1, one_side[repeat - 1]))
    factor = NEWTON_B * gram[own, :] + NEWTON_C * times(gram_pair, gram_pair, own)
    factor = factor + jnp.where(diagonal(half, parity * half), NEWTON_A, 0.0)
    put_pair(factor_pair, factor, own)
    final = times(factor_pair, chain.at[(NS_STEPS - 2) % 2], own)

    put_pair(chain.at[0], final, slice(0, half))

    def ortho_copy(number, k):
        target = (owners[number] + k) % 4
        width = widths[number]
        return turn(
            ortho_out.at[target, :, :width],
            ortho_in.at[number, :, :width],
            (2 * target + parity, head),
            11 + k,
            11 + number,
        )

    for number in range(4):

        @pl.when(plane == owners[number])
        def _():
            width = widths[number]
            left = jnp.concatenate([chain[0, k, :half, :] for k in range(2)], axis=-1)
            right = matrix[head, :, :, :, :width].reshape(full_width, width)
            value = mul(left, jnp.concatenate([right, right], axis=0)) * scale
            ortho_out[:, :, :width] = value.astype(BF16).reshape(4, half // 4, width)
            for k in range(1, 4):
                ortho_copy(number, k).start()
            ortho_in[number, :, :width] = ortho_out[plane, :, :width]

    for b in batches:
        rows_end(b, one_all[b])
    mod_copies = [
        links.send(mod_part.at[head], mod_in.at[k - 1], (lax.rem(node + k, patch_count), head))
        for k in range(1, patch_count)
    ]
    for number in range(4):

        @pl.when(plane != owners[number])
        def _():
            ortho_copy(number, 1).wait_recv()

        @pl.when(plane == owners[number])
        def _():
            for k in range(1, 4):
                ortho_copy(number, k).wait_send()

    summed = mod_part[head]
    wait_all(mod_copies)
    for k in range(patch_count - 1):
        summed = summed + mod_in[k]
    mod_sum[...] = summed
    links.close()


def finish_kernel(
    cuts,
    factors,
    layer_ref,
    input_ref,
    moment_ref,
    ortho_ref,
    mod_ref,
    noise_ref,
    weight_refs,
    adam_refs,
    layer_out,
    input_out,
    moment_outs,
    weight_outs,
    adam_outs,
    sems,
):
    copies = [
        pltpu.make_async_copy(source, target, sems.at[k])
        for k, (source, target) in enumerate(((layer_ref, layer_out), (input_ref, input_out)))
    ]
    for copy in copies:
        copy.start()
    for number in range(4):
        columns = slice(cuts[number], cuts[number + 1])
        moment_outs[number][...] = moment_ref[:, columns]
        ortho = ortho_ref[number, :, : cuts[number + 1] - cuts[number]].astype(F32)
        weight_outs[number][...] = (
            weight_refs[number][...] * (1.0 - LR_MUON * DECAY_WEIGHT) - (LR_MUON * factors[number]) * ortho
        )
    weight, first, second, bias, first_bias, second_bias = adam_refs
    micro_count = noise_ref.shape[0]
    for number in range(4):
        rows = [mod_ref[b * 4 + number : b * 4 + number + 1, :] for b in range(micro_count)]
        grad = lax.dot_general(
            noise_ref[...], jnp.concatenate(rows, axis=0), TN, precision=HIGH, preferred_element_type=F32
        )
        place = slice(number, number + 1)
        stepped = adam_step(weight[number], first[number], second[number], grad)
        for ref, value in zip(adam_outs[:3], stepped):
            ref[number] = value
        stepped = adam_step(bias[place, :], first_bias[place, :], second_bias[place, :], sum(rows))
        for ref, value in zip(adam_outs[3:], stepped):
            ref[place, :] = value
    for copy in copies:
        copy.wait()


def adam_step(weight, first_old, second_old, gradient):
    first_new = BETA_FIRST * first_old + (1.0 - BETA_FIRST) * gradient
    second_new = BETA_SECOND * second_old + (1.0 - BETA_SECOND) * gradient * gradient
    first_hat = first_new / (1.0 - BETA_FIRST**STEP)
    second_hat = second_new / (1.0 - BETA_SECOND**STEP)
    updated = weight * (1.0 - LR_ADAM * DECAY_WEIGHT) - LR_ADAM * first_hat / (
        jnp.sqrt(second_hat) + EPS_ADAM
    )
    return (first_new, second_new, updated)


def orthogonal(matrix):
    scale = 1.0 / (jnp.sqrt(jnp.sum(matrix * matrix)) + 1e-07)
    gram = jnp.dot(matrix, matrix.T, precision=HIGH) * (scale * scale)
    eye = jnp.eye(gram.shape[0], dtype=F32)
    chain = None
    for repeat in range(NS_STEPS):
        factor = NEWTON_A * eye + NEWTON_B * gram + NEWTON_C * jnp.dot(gram, gram, precision=HIGH)
        chain = factor if chain is None else jnp.dot(factor, chain, precision=HIGH)
        if repeat < NS_STEPS - 1:
            gram = jnp.dot(factor, jnp.dot(factor, gram, precision=HIGH), precision=HIGH)
    return jnp.dot(chain, matrix, precision=HIGH) * scale


def per_device(
    node_state,
    noise_embed,
    out_grad,
    neighbours,
    patch_sizes,
    w_project,
    w_output,
    w_expand,
    w_contract,
    momentum_project,
    momentum_output,
    momentum_expand,
    momentum_contract,
    w_modulate,
    b_modulate,
    first_modulate,
    second_modulate,
    first_bias,
    second_bias,
):
    micro_count, capacity, share = node_state.shape
    head_count = lax.axis_size("heads")
    patch_count = lax.axis_size("nodes")
    full_width = share * head_count
    head_dim = w_output.shape[0]
    total_rows = capacity * patch_count
    patch_index = lax.axis_index("nodes")
    head_index = lax.axis_index("heads")
    inv_head = head_dim ** (-0.5)
    hidden = w_expand.shape[1]
    shard_rows = w_project.shape[0]
    own_gather = patch_count == 8

    local_index = jnp.mod(neighbours - (patch_index - 1) * capacity, total_rows)
    index_rows = local_index.reshape(micro_count, capacity // 16, 256)
    weights = [w_project, w_output.T, w_expand, w_contract.T]
    moments = [momentum_project, momentum_output.T, momentum_expand, momentum_contract.T]
    cuts = (0, 3 * head_dim, 4 * head_dim, 4 * head_dim + hidden, 4 * head_dim + 2 * hidden)
    factors = (1.0, 1.0, 1.0, (head_count * hidden / full_width) ** 0.5)
    weight_width = cuts[4]
    vmem = pl.BlockSpec(memory_space=pltpu.VMEM)
    def scratch(dtype, *shape):
        return pltpu.VMEM(shape, dtype)

    rows_all = (head_count, micro_count, capacity, share)
    blocks = (micro_count, 2, 2, capacity, head_dim)
    half_blocks = (micro_count, 2, capacity, head_dim)
    rows_wide = (micro_count, capacity, full_width)
    rows_hidden = (micro_count, capacity, hidden)
    rows_own = (micro_count, capacity, head_dim)
    key_value_rows = (capacity, 2 * head_dim)
    eighth = full_width // 8
    scratches = [
        scratch(BF16, eighth, weight_width),
        scratch(BF16, 8, eighth, weight_width),
        scratch(BF16, head_count, 8, eighth, head_dim),
    ]
    scratches = scratches if own_gather else []
    scratches += [
        scratch(BF16, *rows_all),
        scratch(BF16, *rows_all),
        scratch(F32, head_count, 4 * micro_count, share),
        scratch(BF16, 2, *rows_all),
        scratch(BF16, 3 * micro_count, capacity, full_width),
        scratch(BF16, *rows_own),
        scratch(BF16, micro_count, 3, *key_value_rows),
        scratch(BF16, micro_count, capacity, 3 * capacity),
        scratch(BF16, *rows_all),
        scratch(F32, *rows_wide),
        scratch(BF16, *rows_wide),
        scratch(BF16, *rows_hidden),
        scratch(BF16, *rows_hidden),
        scratch(F32, *blocks),
        scratch(F32, *half_blocks),
        scratch(BF16, *half_blocks),
        scratch(BF16, *half_blocks),
        scratch(F32, *blocks),
        scratch(BF16, *blocks),
        scratch(BF16, *half_blocks),
        scratch(F32, *half_blocks),
        scratch(BF16, *rows_own),
        scratch(F32, *rows_own),
        scratch(BF16, *rows_wide),
        scratch(BF16, *rows_own),
        scratch(BF16, capacity, 3 * capacity),
        scratch(F32, micro_count, *key_value_rows),
        scratch(BF16, micro_count, 2, *key_value_rows),
        scratch(BF16, micro_count, 2, *key_value_rows),
        scratch(BF16, micro_count, capacity, 3 * head_dim),
        scratch(F32, head_count, 4 * micro_count, share),
        scratch(F32, 8, 4 * micro_count, share),
        scratch(F32, 2, 4, eighth, weight_width),
        scratch(BF16, 2, 4, eighth, weight_width),
        scratch(BF16, 4, eighth, weight_width),
        scratch(BF16, 3, eighth, weight_width),
        scratch(BF16, 7, eighth, 4 * head_dim),
    ]
    last = [
        scratch(BF16, eighth, weight_width),
        scratch(BF16, head_count, 2, 4, eighth, hidden),
        scratch(F32, full_width, full_width),
        scratch(BF16, 2, 2, full_width, full_width),
        scratch(BF16, 4, eighth, hidden),
    ]
    semaphores = [pltpu.SemaphoreType.DMA((count,)) for count in (96, 96, 16, 16)]
    operands = [patch_sizes, node_state, out_grad, index_rows, noise_embed, w_modulate, b_modulate]
    out_shape = [
        jax.ShapeDtypeStruct((micro_count, capacity, share), BF16),
        jax.ShapeDtypeStruct((micro_count, capacity, share), F32),
    ]
    summed_shape = jax.ShapeDtypeStruct((4 * micro_count, share), F32)
    if own_gather:
        operands += weights + moments
        out_shape += [
            jax.ShapeDtypeStruct((eighth, weight_width), F32),
            jax.ShapeDtypeStruct((4, eighth, hidden), BF16),
            summed_shape,
        ]
        scratches += last
    else:
        low_cat = jnp.concatenate(weights, axis=1).astype(BF16)
        low_cat = lax.all_gather(low_cat, "nodes", axis=0, tiled=True)
        low_cat = low_cat.reshape(8, eighth, weight_width)
        output_all = lax.all_gather(
            low_cat[:, :, 3 * head_dim : 4 * head_dim], "heads", axis=0, tiled=False
        )
        operands += [low_cat, output_all]
        out_shape += [jax.ShapeDtypeStruct((8, eighth, weight_width), F32), summed_shape]

    def layer_body(*refs):
        refs = list(refs)
        if own_gather:
            refs[7:15] = [refs[7:11], refs[11:15]]
        else:
            gathered = refs[7:9]
            refs[7:9] = [None, None]
            refs[12:12] = [None]
            refs[14:14] = [None] + gathered
            refs[-4:-4] = [None] * len(last)
        layer_kernel(patch_count, own_gather, *refs)

    updated = pl.pallas_call(
        layer_body,
        out_shape=out_shape,
        in_specs=[pl.BlockSpec(memory_space=pltpu.SMEM)] + [vmem] * (len(operands) - 1),
        out_specs=[vmem] * len(out_shape),
        scratch_shapes=scratches + semaphores,
        compiler_params=pltpu.CompilerParams(
            collective_id=0, has_side_effects=True, vmem_limit_bytes=60 << 20
        ),
        name="layer",
    )(*operands)
    if own_gather:
        layer_output, input_grad, moment_cat, ortho_all, mod_summed = updated
    else:
        layer_output, input_grad, grad_cat, mod_summed = updated
        mod_summed = lax.psum(mod_summed, "nodes")
        moment_cat = MOMENTUM_DECAY * jnp.concatenate(moments, axis=1) + lax.psum_scatter(
            grad_cat.reshape(full_width, weight_width), "nodes", scatter_dimension=0, tiled=True
        )
        whole = lax.all_gather(moment_cat.astype(BF16), ("nodes", "heads"), axis=0, tiled=False)
        whole = whole.reshape(patch_count, head_count, shard_rows, weight_width)
        whole = whole.transpose(0, 2, 1, 3).reshape(full_width, head_count, weight_width).astype(F32)
        pieces = []
        for number in range(4):
            columns = cuts[number + 1] - cuts[number]
            matrix = whole[:, :, cuts[number] : cuts[number + 1]].reshape(full_width, head_count * columns)
            ortho = lax.dynamic_slice(
                orthogonal(matrix),
                (patch_index * shard_rows, head_index * columns),
                (shard_rows, columns),
            )
            pieces.append(jnp.pad(ortho, ((0, 0), (0, hidden - columns))))
        ortho_all = jnp.stack(pieces)
    adam = [w_modulate, first_modulate, second_modulate, b_modulate, first_bias, second_bias]
    anywhere = pl.BlockSpec(memory_space=pl.ANY)

    def finish_body(*refs):
        finish_kernel(
            cuts, factors, *refs[:6], refs[6:10], refs[10:16], *refs[16:18], refs[18:22], refs[22:26], refs[26:32], refs[32]
        )

    shards = [jax.ShapeDtypeStruct(weight.shape, F32) for weight in weights]
    finished = pl.pallas_call(
        finish_body,
        out_shape=[
            jax.ShapeDtypeStruct(layer_output.shape, BF16),
            jax.ShapeDtypeStruct(input_grad.shape, F32),
            *shards,
            *shards,
            *[jax.ShapeDtypeStruct(array.shape, F32) for array in adam],
        ],
        in_specs=[anywhere] * 2 + [vmem] * 14,
        out_specs=[anywhere] * 2 + [vmem] * 14,
        scratch_shapes=[pltpu.SemaphoreType.DMA((2,))],
        compiler_params=pltpu.CompilerParams(vmem_limit_bytes=60 << 20),
        name="finish",
    )(layer_output, input_grad, moment_cat, ortho_all, mod_summed, noise_embed, *weights, *adam)

    def unpack(project, output, expand, contract):
        return (project, output.T, expand, contract.T)

    return (*finished[:2], *unpack(*finished[2:6]), *unpack(*finished[6:10]), *finished[10:])


def solution(mesh):
    in_specs = (
        P(None, "nodes", "heads"),
        P(),
        P(None, "nodes", "heads"),
        P(None, "nodes", None),
        P(None, "nodes"),
        P("nodes", "heads"),
        P("heads", "nodes"),
        P("nodes", "heads"),
        P("heads", "nodes"),
        P("nodes", "heads"),
        P("heads", "nodes"),
        P("nodes", "heads"),
        P("heads", "nodes"),
        P(None, None, "heads"),
        P(None, "heads"),
        P(None, None, "heads"),
        P(None, None, "heads"),
        P(None, "heads"),
        P(None, "heads"),
    )
    out_specs = (
        P(None, "nodes", "heads"),
        P(None, "nodes", "heads"),
        P("nodes", "heads"),
        P("heads", "nodes"),
        P("nodes", "heads"),
        P("heads", "nodes"),
        P("nodes", "heads"),
        P("heads", "nodes"),
        P("nodes", "heads"),
        P("heads", "nodes"),
        P(None, None, "heads"),
        P(None, None, "heads"),
        P(None, None, "heads"),
        P(None, "heads"),
        P(None, "heads"),
        P(None, "heads"),
    )
    return jax.shard_map(
        per_device, mesh=mesh, in_specs=in_specs, out_specs=out_specs, check_vma=False
    )
```

time: 632 us -> 177 us (0.28); the launches traced: 622 us -> 177 us
  matrix products: 208 us -> 0 us
  waiting for transfers between devices: 184 us -> 0 us
  Pallas kernels: 59 us -> 172 us
  local copies, waits for them, and re-layouts: 72.7 us -> 2.36 us
  other arithmetic: 39.2 us -> 0.87 us
  blocking collectives: 36.3 us -> 0 us
  between operations: 18.3 us -> 0.86 us
    dot_general x93 -> x0, matrix products: 208 us -> none  [the longest x20 39.2 us: orthogonal(): jnp.dot(gram, gram, precision=HIGH)]
    pallas_call x1 -> x2, Pallas kernels: 59 us -> 172 us  [the longest x1 144 us: per_device(): pl.pallas_call(layer_body, out_shape=out_shape, in_specs=[pl.BlockSpec(me...]
    unnamed x6 -> x0, waiting for transfers between devices: 65.4 us -> none
    reduce_scatter x2 -> x0, waiting for transfers between devices: 49.2 us -> none  [the longest x1 31.7 us: per_device(): lax.psum_scatter(mul(grad_projected, w_proj_low, NT), 'heads', scatter_di...]
    psum x1 -> x0, waiting for transfers between devices: 40.1 us -> none  [per_device(): grad_two = lax.psum(mul(grad_up, w_exp_low, NT), 'heads')]
    psum x2 -> x0, blocking collectives: 36.3 us -> none  [the longest x1 21.4 us: per_device(): lax.psum(jnp.stack([node_sum(grad_one), node_sum(grad_one * norm_one), no...]
    unnamed x132 -> x3, local copies, waits for them, and re-layouts: 31.5 us -> 1.3 us
    slice x11 -> x0, local copies, waits for them, and re-layouts: 22.8 us -> none  [the longest x7 18.2 us: per_device(): whole[:, :, cuts[number]:cuts[number + 1]]]
  transfers between devices with their start and end apart: 7 -> 0, of which waited for: 6 -> 0; matrix products, arithmetic and copies ran while one was open for 10% -> 0% of each run, Pallas kernels for 0% -> 0%
where the time goes in v3:
time: 177 us
  Pallas kernels  172 us (97%)
  local copies, waits for them, and re-layouts  2.36 us (1%)
    pallas_call x1, Pallas kernels, per_device(): pl.pallas_call(layer_body, out_shape=out_shape, in_specs=[pl.BlockSpec(me...  144 us
    pallas_call x1, Pallas kernels, per_device(): pl.pallas_call(finish_body, out_shape=[jax.ShapeDtypeStruct(layer_output....  28.2 us

profile of v3, /device:TPU:0, one launch (start us, length us, event | category | flops | bytes accessed | tf_op | source)
XLA Modules:
  0.0 176.5 jit_solution(10424182348492154527)
XLA Ops:
  0.7 0.0 copy-start
  0.7 0.6 copy-done
  1.3 0.6 copy.38.refs_0_
  2.0 0.9 add_select_fusion
  2.8 0.2 copy.37
  3.0 0.9 reshape.35.refs_3_
  3.9 144.2 %layer.1 = (bf16[2,512,128]{2,1,0:T(8,128)(2,1)}, f32[2,512,128]{2,1,0:T(8,128)}, f32[64,1536]{1,0:T(8,128)}, bf16[4,64,512]{2,1,0:T(8,128)(2,1)}, f32[8,128]{1,0:T(8,128)}) custom-call(s32[2,1]{1,0:T(2,128)} %copy.38.refs_0_, bf16[2,512,128]{2,1,0:T(8,128)(2,1)} %refs_1_.1, bf16[2,512,128]{2,1,0:T(8,128)(2,1)} %refs_2_.1, s32[2,32,256]{2,1,0:T(8,128)} %reshape.35.refs_3_, ...), custom_call_target="tpu_custom_call" | custom-call | tf_op jit(solution)/shard_map/layer/pallas_call | solution.py:1100
  148.1 28.2 %finish.1 = (bf16[2,512,128]{2,1,0:T(8,128)(2,1)}, f32[2,512,128]{2,1,0:T(8,128)}, f32[64,384]{1,0:T(8,128)}, f32[64,128]{1,0:T(8,128)}, f32[64,512]{1,0:T(8,128...) custom-call(bf16[2,512,128]{2,1,0:T(8,128)(2,1)} %get-tuple-element., ...), custom_call_target="tpu_custom_call" | custom-call | tf_op jit(solution)/shard_map/finish/pallas_call | solution.py:1142
Async XLA Ops:
  0.7 0.7 copy-start

commit v4 on v3

--- a/solution.py
+++ b/solution.py
@@ -146,7 +146,7 @@
     grad_low,
     grad_core,
     grad_line,
-    grad_near,
+    grad_wide,
     moment_low,
     matrix,
     gram,
@@ -205,7 +205,7 @@
 
     def live_rows(batch, start, count):
         slots = lax.broadcasted_iota(jnp.int32, (count, 1), 0) + start
-        return (slots < sizes_ref[batch, 0]).astype(F32)
+        return (slots < sizes_ref[0:1, batch : batch + 1]).astype(F32)
 
     def rows_at(step, count):
         start = step * count if isinstance(step, int) else pl.multiple_of(step * count, count)
@@ -219,10 +219,10 @@
         into = weight_all.at[node, :, columns]
         return [links.send(part, into, to) for to in peers], (part, into)
 
-    def pass_on(arriving, columns):
+    def pass_on(arriving, columns, which=(0, 1, 2)):
         passed = []
-        for k, copy in enumerate(arriving):
-            copy.wait_recv()
+        for k in which:
+            arriving[k].wait_recv()
             owner = lax.rem(node + patch_count - 2 * (k + 1), patch_count)
             part = weight_all.at[owner, :, columns]
             passed.append(links.send(part, part, to_partner))
@@ -240,9 +240,6 @@
         state_after.append(links.send(state_ref.at[b], halo.at[0, head, b], to_after))
         state_before.append(links.send(state_ref.at[b], halo.at[1, head, b], to_before))
         state_sibling.append(links.send(state_ref.at[b], state_all.at[head, b], to_sibling))
-    if own_gather:
-        other_peers, other_partner = spread(other_columns)
-    cot_across = [links.send(cot_ref.at[0], cot_all.at[head, 0], to_across)]
     if own_gather:
         weight_all[node] = weight_low[...]
     state_all[head] = state_ref[...]
@@ -284,11 +281,14 @@
         halo_across.append(to_chip)
         halo_sibling.append(to_core)
 
-    count(0)
+    if own_gather:
+        other_peers, other_partner = spread(other_columns)
+    for b in batches:
+        count(b)
     second_hops(0)
     if own_gather:
         first_passed = pass_on(first_peers, first_columns)
-    count(1)
+    cot_across = [links.send(cot_ref.at[0], cot_all.at[head, 0], to_across)]
     second_hops(1)
     if own_gather:
         other_partner = [links.send(*other_partner, to_partner)]
@@ -359,10 +359,13 @@
         output_part = weight_all.at[:, :, pl.ds(cuts[1], head_dim)]
         output_across = links.send(output_part, output_all.at[head], to_across)
         ready.append(links.send(output_part, output_all.at[head], to_sibling))
+        other_passed = pass_on(other_peers, other_columns, (0,))
     project_all(0)
+    if own_gather:
+        other_passed += pass_on(other_peers, other_columns, (1,))
     mixed_first = attend(0)
     if own_gather:
-        other_passed = pass_on(other_peers, other_columns)
+        other_passed += pass_on(other_peers, other_columns, (2,))
     project_all(1)
     mixed_first = pass_mixed(0, mixed_first)
     wait_all(cot_across)
@@ -444,32 +447,48 @@
     for k in range(4):
         mod_part[k] = jnp.zeros(mod_part.shape[1:], F32)
 
+    def store_grad(step, columns, value, add=False):
+        half = full_width // 8
+        for k in range(2):
+            part = value[k * half : (k + 1) * half]
+            if add:
+                part = grad_cat[k, step, :, columns] + part
+            grad_cat[k, step, :, columns] = part
+            grad_low[k, step, :, columns] = part.astype(BF16)
+
+    def both(ref, columns):
+        return ref[:, :, columns].reshape(micro_count * capacity, -1)
+
+    def one_pair(patch, columns):
+        pair = a_one[patch * micro_count : (patch + 1) * micro_count, :, columns]
+        return pair.reshape(micro_count * capacity, -1)
+
+    def live_cot(batch, columns):
+        return (cot_all[columns, batch].astype(F32) * live_rows(batch, 0, capacity)).astype(BF16)
+
+    def expand_grad(batch, step):
+        columns = pl.ds(pl.multiple_of(step * head_dim, head_dim), head_dim)
+        value = mul(a_two[batch, :, columns], grad_up[batch], TN)
+        store_grad(step, expand_columns, value, batch > 0)
+
+    def contract_grad(batch, step):
+        store_grad(step, contract_columns, mul(live_cot(batch, step), act[batch], TN), batch > 0)
+
     pl.loop(0, 2)(lambda step: feed_forward(0, step))
     core_first = to_core(0)
     mixed_second = pass_mixed(1, mixed_second)
     side_first = to_side(0, core_first)
+
+    @pl.loop(0, 4)
+    def _(step):
+        expand_grad(0, step)
+        contract_grad(0, step)
+
     wait_all(mixed_second)
     pl.loop(0, 2)(lambda step: feed_forward(1, step))
     core_second = to_core(1)
 
-    def store_grad(step, columns, value):
-        half = full_width // 8
-        for k in range(2):
-            part = value[k * half : (k + 1) * half]
-            grad_cat[k, step, :, columns] = part
-            grad_low[k, step, :, columns] = part.astype(BF16)
-
-    def both(ref, columns):
-        return ref[:, :, columns].reshape(micro_count * capacity, -1)
-
-    def one_pair(patch, columns):
-        pair = a_one[patch * micro_count : (patch + 1) * micro_count, :, columns]
-        return pair.reshape(micro_count * capacity, -1)
-
-    def live_cot(batch, columns):
-        return (cot_all[columns, batch].astype(F32) * live_rows(batch, 0, capacity)).astype(BF16)
-
-    late = slice(0, cuts[2])
+    late_one, late_two = slice(0, 2 * head_dim), slice(2 * head_dim, cuts[2])
 
     def grad_pair(columns):
         return links.send(
@@ -499,52 +518,51 @@
         summed = grad_cat[parity, plane, :, columns]
         for k in range(3):
             summed = summed + grad_line[k, :, columns].astype(F32)
-        store_moment(summed, columns)
-
-    def grad_direct(columns):
+        moment_new[:, columns] = summed
+
+    def grad_wide_planes(columns):
         sent = []
-        for k in range(1, patch_count):
-            target = lax.rem(node + k, patch_count)
+        for k in range(1, 4):
+            target = lax.rem(plane + k, 4)
             sent.append(
                 links.send(
-                    grad_low.at[lax.rem(target, 2), lax.div(target, 2), :, columns],
-                    grad_near.at[k - 1],
-                    (target, head),
+                    grad_low.at[:, target, :, columns],
+                    grad_wide.at[k - 1, :, :, columns],
+                    (2 * target + parity, head),
                 )
             )
         return sent
 
-    def grad_direct_finish(copies, columns):
-        summed = grad_cat[parity, plane, :, columns]
-        for k, copy in enumerate(copies):
-            copy.wait_recv()
-            summed = summed + grad_near[k].astype(F32)
-        store_moment(summed, columns)
-
-    def store_moment(summed, columns):
-        for number, ref in enumerate(moment_refs):
-            if columns.start <= cuts[number] < columns.stop:
-                own = slice(cuts[number], cuts[number + 1])
-                part = summed[:, cuts[number] - columns.start : cuts[number + 1] - columns.start]
-                moment = MOMENTUM_DECAY * ref[...] + part
-                moment_new[:, own] = moment
-                moment_low[:, own] = moment.astype(BF16)
-
-    @pl.loop(0, 4)
-    def _(step):
-        columns = pl.ds(pl.multiple_of(step * head_dim, head_dim), head_dim)
-        store_grad(step, expand_columns, mul(both(a_two, columns), grad_up[...].reshape(-1, hidden), TN))
-
+    def grad_wide_pair(copies, columns):
+        wait_all(copies)
+        for pair in range(2):
+            summed = grad_cat[pair, plane, :, columns]
+            for k in range(3):
+                summed = summed + grad_wide[k, pair, :, columns].astype(F32)
+            grad_cat[pair, plane, :, columns] = summed
+            grad_low[pair, plane, :, columns] = summed.astype(BF16)
+        return links.send(
+            grad_low.at[mirror, plane, :, columns], grad_core.at[plane, :, columns], to_partner
+        )
+
+    def grad_wide_finish(copy, columns):
+        copy.wait_recv()
+        summed = grad_cat[parity, plane, :, columns] + grad_core[plane, :, columns].astype(F32)
+        moment_new[:, columns] = summed
+
+    def store_moment(numbers):
+        for number in numbers:
+            own = slice(cuts[number], cuts[number + 1])
+            moment = MOMENTUM_DECAY * moment_refs[number][...] + moment_new[:, own]
+            moment_new[:, own] = moment
+            moment_low[:, own] = moment.astype(BF16)
+
+    pl.loop(0, 4)(lambda step: expand_grad(1, step))
     if own_gather:
         expand_pair = grad_pair(expand_columns)
-
-    @pl.loop(0, 4)
-    def _(step):
-        cot = jnp.concatenate([live_cot(b, step) for b in batches], axis=0)
-        store_grad(step, contract_columns, mul(cot, act[...].reshape(-1, hidden), TN))
-
-    if own_gather:
-        contract_pair = grad_pair(contract_columns)
+    pl.loop(0, 4)(lambda step: contract_grad(1, step))
+    if own_gather:
+        contract_wide = grad_wide_planes(contract_columns)
     side_second = to_side(1, core_second)
     all_first = to_all(0, side_first)
     out_copies = [links.send(out_low.at[b, 1 - core], out_core.at[b], to_sibling) for b in batches]
@@ -564,7 +582,7 @@
             grad_attn[batch, rows, :] = low
             grad_mixed[batch, rows, :] = mul(low, weight(slice(cuts[1], cuts[2]))).astype(BF16)
 
-    def attend_back(batch):
+    def attend_back(batch, between=lambda: None):
         attend_rows = 128
 
         @pl.loop(0, capacity // attend_rows)
@@ -579,6 +597,7 @@
             score_low[rows, :] = score
             grad_projected[batch, rows, :head_dim] = mul(score, keys).astype(BF16)
 
+        between()
         for patch in range(3):
             slots = slice(patch * capacity, (patch + 1) * capacity)
             grad_key = mul(score_low[:, slots], queries[batch], TN)
@@ -659,14 +678,13 @@
                 to_owner(number, plane).wait_send()
 
     all_first.wait_recv()
+    norm_two_back(0)
     if own_gather:
         expand_line = grad_planes(expand_pair, expand_columns)
-    norm_two_back(0)
-    attend_back(0)
+    all_second = []
+    attend_back(0, lambda: all_second.append(to_all(1, side_second)))
+    all_second = all_second[0]
     back_first = send_back(0)
-    all_second = to_all(1, side_second)
-    if own_gather:
-        contract_line = grad_planes(contract_pair, contract_columns)
     out_across_copies = []
     for batch in batches:
         out_copies[batch].wait_recv()
@@ -680,13 +698,18 @@
     all_second.wait_recv()
     norm_two_back(1)
     attend_back(1)
+    if own_gather:
+        contract_pair = grad_wide_pair(contract_wide, contract_columns)
 
     @pl.loop(0, 4)
     def _(step):
         columns = pl.ds(pl.multiple_of(step * head_dim, head_dim), head_dim)
-        queries_part = mul(one_pair(1, columns), both(grad_projected, slice(0, head_dim)), TN)
-        store_grad(step, slice(0, head_dim), queries_part)
-        rest = mul(one_pair(1, columns), grad_own[...].reshape(-1, 2 * head_dim).astype(BF16), TN)
+        own = jnp.concatenate(
+            [both(grad_projected, slice(0, head_dim)), grad_own[...].reshape(-1, 2 * head_dim).astype(BF16)], axis=1
+        )
+        own = mul(one_pair(1, columns), own, TN)
+        store_grad(step, slice(0, head_dim), own[:, :head_dim])
+        rest = own[:, head_dim:]
         for patch in (0, 2):
             away = grad_away[:, patch // 2].reshape(-1, 2 * head_dim)
             rest = rest + mul(one_pair(patch, columns), away, TN)
@@ -695,12 +718,16 @@
         store_grad(step, slice(cuts[1], cuts[2]), mul(both(grad_attn, columns), own_mixed, TN))
 
     if own_gather:
-        late_direct = grad_direct(late)
+        late_wide = grad_wide_planes(late_two)
+        late_pair = grad_pair(late_one)
     back_second = send_back(1)
     if own_gather:
         grad_finish(expand_line, expand_columns)
-        grad_finish(contract_line, contract_columns)
+        grad_wide_finish(contract_pair, contract_columns)
+        store_moment((2, 3))
         own_to_owner((2, 3))
+        late_line = grad_planes(late_pair, late_one)
+        late_pair = grad_wide_pair(late_wide, late_two)
     for batch in batches:
         out_across_copies[batch].wait_recv()
         own = hidden_one[batch, :, pl.ds(pl.multiple_of(head * head_dim, head_dim), head_dim)]
@@ -751,9 +778,11 @@
         links.close()
         return
 
-    grad_direct_finish(late_direct, late)
+    own_arrive((2, 3))
+    grad_wide_finish(late_pair, late_two)
+    grad_finish(late_line, late_one)
+    store_moment((0, 1))
     own_to_owner((0, 1))
-    own_arrive((2, 3))
     one_core.append(rows_back(1, back_second))
     own_arrive((0, 1))
     one_side = [to_side(b, one_core[b]) for b in batches]
@@ -898,14 +927,9 @@
     moment_outs,
     weight_outs,
     adam_outs,
-    sems,
 ):
-    copies = [
-        pltpu.make_async_copy(source, target, sems.at[k])
-        for k, (source, target) in enumerate(((layer_ref, layer_out), (input_ref, input_out)))
-    ]
-    for copy in copies:
-        copy.start()
+    layer_out[...] = layer_ref[...]
+    input_out[...] = input_ref[...]
     for number in range(4):
         columns = slice(cuts[number], cuts[number + 1])
         moment_outs[number][...] = moment_ref[:, columns]
@@ -927,8 +951,6 @@
         stepped = adam_step(bias[place, :], first_bias[place, :], second_bias[place, :], sum(rows))
         for ref, value in zip(adam_outs[3:], stepped):
             ref[place, :] = value
-    for copy in copies:
-        copy.wait()
 
 
 def adam_step(weight, first_old, second_old, gradient):
@@ -1051,7 +1073,7 @@
         scratch(BF16, 2, 4, eighth, weight_width),
         scratch(BF16, 4, eighth, weight_width),
         scratch(BF16, 3, eighth, weight_width),
-        scratch(BF16, 7, eighth, 4 * head_dim),
+        scratch(BF16, 3, 2, eighth, weight_width),
     ]
     last = [
         scratch(BF16, eighth, weight_width),
@@ -1061,7 +1083,7 @@
         scratch(BF16, 4, eighth, hidden),
     ]
     semaphores = [pltpu.SemaphoreType.DMA((count,)) for count in (96, 96, 16, 16)]
-    operands = [patch_sizes, node_state, out_grad, index_rows, noise_embed, w_modulate, b_modulate]
+    operands = [patch_sizes.T, node_state, out_grad, index_rows, noise_embed, w_modulate, b_modulate]
     out_shape = [
         jax.ShapeDtypeStruct((micro_count, capacity, share), BF16),
         jax.ShapeDtypeStruct((micro_count, capacity, share), F32),
@@ -1100,7 +1122,7 @@
     updated = pl.pallas_call(
         layer_body,
         out_shape=out_shape,
-        in_specs=[pl.BlockSpec(memory_space=pltpu.SMEM)] + [vmem] * (len(operands) - 1),
+        in_specs=[vmem] * len(operands),
         out_specs=[vmem] * len(out_shape),
         scratch_shapes=scratches + semaphores,
         compiler_params=pltpu.CompilerParams(
@@ -1131,11 +1153,10 @@
             pieces.append(jnp.pad(ortho, ((0, 0), (0, hidden - columns))))
         ortho_all = jnp.stack(pieces)
     adam = [w_modulate, first_modulate, second_modulate, b_modulate, first_bias, second_bias]
-    anywhere = pl.BlockSpec(memory_space=pl.ANY)
 
     def finish_body(*refs):
         finish_kernel(
-            cuts, factors, *refs[:6], refs[6:10], refs[10:16], *refs[16:18], refs[18:22], refs[22:26], refs[26:32], refs[32]
+            cuts, factors, *refs[:6], refs[6:10], refs[10:16], *refs[16:18], refs[18:22], refs[22:26], refs[26:32]
         )
 
     shards = [jax.ShapeDtypeStruct(weight.shape, F32) for weight in weights]
@@ -1148,9 +1169,8 @@
             *shards,
             *[jax.ShapeDtypeStruct(array.shape, F32) for array in adam],
         ],
-        in_specs=[anywhere] * 2 + [vmem] * 14,
-        out_specs=[anywhere] * 2 + [vmem] * 14,
-        scratch_shapes=[pltpu.SemaphoreType.DMA((2,))],
+        in_specs=[vmem] * 16,
+        out_specs=[vmem] * 16,
         compiler_params=pltpu.CompilerParams(vmem_limit_bytes=60 << 20),
         name="finish",
     )(layer_output, input_grad, moment_cat, ortho_all, mod_summed, noise_embed, *weights, *adam)

time: 177 us -> 148 us (0.84)
  Pallas kernels: 172 us -> 145 us
    pallas_call x1, Pallas kernels: 28.2 us -> 4.52 us  [per_device(): pl.pallas_call(finish_body, out_shape=[jax.ShapeDtypeStruct(layer_output....]
    pallas_call x1, Pallas kernels: 144 us -> 141 us  [per_device(): pl.pallas_call(layer_body, out_shape=out_shape, in_specs=[vmem] * len(ope...]
where the time goes in v4:
time: 148 us
  Pallas kernels  145 us (98%)
    pallas_call x1, Pallas kernels, per_device(): pl.pallas_call(layer_body, out_shape=out_shape, in_specs=[vmem] * len(ope...  141 us
    pallas_call x1, Pallas kernels, per_device(): pl.pallas_call(finish_body, out_shape=[jax.ShapeDtypeStruct(layer_output....  4.52 us

profile of v4, /device:TPU:0, one launch (start us, length us, event | category | flops | bytes accessed | tf_op | source)
XLA Modules:
  0.0 148.2 jit_solution(171991329556213682)
XLA Ops:
  0.7 0.9 add_select_fusion
  1.5 0.2 copy.36
  1.7 0.9 reshape.35.refs_3_
  2.6 140.9 %layer.1 = (bf16[2,512,128]{2,1,0:T(8,128)(2,1)}, f32[2,512,128]{2,1,0:T(8,128)}, f32[64,1536]{1,0:T(8,128)}, bf16[4,64,512]{2,1,0:T(8,128)(2,1)}, f32[8,128]{1,0:T(8,128)}) custom-call(s32[1,2]{1,0:T(1,128)} %bitcast.15, bf16[2,512,128]{2,1,0:T(8,128)(2,1)} %refs_1_.1, bf16[2,512,128]{2,1,0:T(8,128)(2,1)} %refs_2_.1, s32[2,32,256]{2,1,0:T(8,128)} %reshape.35.refs_3_, ...), custom_call_target="tpu_custom_call" | custom-call | tf_op jit(solution)/shard_map/layer/pallas_call | solution.py:1122
  143.5 4.5 %finish.1 = (bf16[2,512,128]{2,1,0:T(8,128)(2,1)}, f32[2,512,128]{2,1,0:T(8,128)}, f32[64,384]{1,0:T(8,128)}, f32[64,128]{1,0:T(8,128)}, f32[64,512]{1,0:T(8,128...) custom-call(bf16[2,512,128]{2,1,0:T(8,128)(2,1)} %get-tuple-element., ...), custom_call_target="tpu_custom_call" | custom-call | tf_op jit(solution)/shard_map/finish/pallas_call | solution.py:1163
